TPU v7x, 32 devices: a whole 2x2x4 slice. The times are simulated.
32 devices in a mesh: seq: 8 (over y, x, core), tp: 4 (over z).
Axes of the slice: x: 2, y: 2, z: 4, core: 2. Of those that a mesh axis runs over, the one named last changes fastest.
Arguments:
- tokens: bfloat16 [6144, 2048], P('seq', 'tp'), may hold values from -6 to 6
- mix_gain: bfloat16 [2048], P(('tp', 'seq')), may hold values from 0.5 to 1.5
- scan_branch: bfloat16 [2048, 2560], P('seq', 'tp'), may hold values from -0.125 to 0.125
- gate_branch: bfloat16 [2048, 2560], P('seq', 'tp'), may hold values from -0.125 to 0.125
- kernel_taps: bfloat16 [4, 2560], P(None, ('tp', 'seq')), may hold values from -3 to 3
- kernel_bias: bfloat16 [2560], P(('tp', 'seq')), may hold values from -1.796875 to 1.796875
- decay_gate: bfloat16 [16, 25600], P('tp', 'seq'), may hold values from -0.5 to 0.5
- decay_bias: bfloat16 [2560], P(('tp', 'seq')), may hold values from -3 to 3
- input_gate: bfloat16 [16, 25600], P('tp', 'seq'), may hold values from -0.5 to 0.5
- input_bias: bfloat16 [2560], P(('tp', 'seq')), may hold values from -3 to 3
- decay_logit: bfloat16 [2560], P(('tp', 'seq')), may hold values from 4 to 14
- mixer_out: bfloat16 [2560, 2048], P('tp', 'seq'), may hold values from -0.125 to 0.125
- feed_gain: bfloat16 [2048], P(('tp', 'seq')), may hold values from 0.5 to 1.5
- gate_weight: bfloat16 [2048, 6144], P('seq', 'tp'), may hold values from -0.125 to 0.125
- up_weight: bfloat16 [2048, 6144], P('seq', 'tp'), may hold values from -0.125 to 0.125
- down_weight: bfloat16 [6144, 2048], P('tp', 'seq'), may hold values from -0.078125 to 0.078125
- lengths: int32 [6], replicated, may hold values from 1 to 5822, as said below
- cotangent: bfloat16 [6144, 2048], P('seq', 'tp'), may hold values from -6 to 6
Outputs:
- block_out: float32 [6144, 2048], P('seq', 'tp')
- tokens_grad: float32 [6144, 2048], P('seq', 'tp')
- mix_gain_grad: float32 [2048], P(('tp', 'seq'))
- scan_branch_grad: float32 [2048, 2560], P('seq', 'tp')
- gate_branch_grad: float32 [2048, 2560], P('seq', 'tp')
- kernel_taps_grad: float32 [4, 2560], P(None, ('tp', 'seq'))
- kernel_bias_grad: float32 [2560], P(('tp', 'seq'))
- decay_gate_grad: float32 [16, 25600], P('tp', 'seq')
- decay_bias_grad: float32 [2560], P(('tp', 'seq'))
- input_gate_grad: float32 [16, 25600], P('tp', 'seq')
- input_bias_grad: float32 [2560], P(('tp', 'seq'))
- decay_logit_grad: float32 [2560], P(('tp', 'seq'))
- mixer_out_grad: float32 [2560, 2048], P('tp', 'seq')
- feed_gain_grad: float32 [2048], P(('tp', 'seq'))
- gate_weight_grad: float32 [2048, 6144], P('seq', 'tp')
- up_weight_grad: float32 [2048, 6144], P('seq', 'tp')
- down_weight_grad: float32 [6144, 2048], P('tp', 'seq')
- mean_decay: float32 [2560], P(('tp', 'seq'))
Inputs may be any that keep to these rules, and one draw needn't show every extreme that they name: The lengths sum to 6144. One of them is long, of exactly the largest length; all others are at most 128 and together hold a fixed number of tokens, fewer than 768. Which one is long varies with the seed.
All inputs are finite; a program needn't handle non-finite values.
Results may differ from a plain program's by a relative error of at most 0.0098.
Values may be sent and summed in bfloat16 or wider, within the bound.
A program may use at most 256 MiB of HBM per device.

v0:
```python
import jax
import jax.numpy as jnp
from jax import lax
from jax.sharding import PartitionSpec as P

D = 2048
KW = 4
CD = 8
BW = 160


EPSILON = 1e-06
FLOOR_VALUE = 0.001


def from_behind(value, axis, steps):
    count = lax.axis_size(axis)
    initial, last = (max(0, -steps), min(count, count - steps))
    return lax.ppermute(value, axis, [(source, source + steps) for source in range(initial, last)])


def entering(part, axis, combine, identity, reverse):
    count = lax.axis_size(axis)
    place = lax.axis_index(axis)
    ahead = count - 1 - place if reverse else place
    gathered = jax.tree.map(lambda a: lax.all_gather(a, axis), part)
    state = jax.tree.map(lambda a, e: jnp.zeros_like(a) + jnp.asarray(e, a.dtype), part, identity)

    def one(turn, state):
        source = count - 1 - turn if reverse else turn
        return combine(
            state, jax.tree.map(lambda a: lax.dynamic_index_in_dim(a, source, 0, False), gathered)
        )

    return lax.fori_loop(0, ahead, one, state)


def matmul(left_side, right_side):
    return jnp.dot(left_side, right_side, preferred_element_type=jnp.float32)


def matmul_tn(left_side, right_side):
    return lax.dot_general(
        left_side, right_side, (((0,), (0,)), ((), ())), preferred_element_type=jnp.float32
    )


def matmul_nt(left_side, right_side):
    return lax.dot_general(
        left_side, right_side, (((1,), (1,)), ((), ())), preferred_element_type=jnp.float32
    )


def smooth_gelu(values):
    return jax.nn.gelu(values, approximate=True)


def combine(earlier, later):
    return (earlier[0] * later[0], later[1] + later[0] * earlier[1])


def seq_offsets(lengths, first_index, row_total):
    ends_all = jnp.cumsum(lengths, dtype=jnp.int32)
    starts_all = ends_all - lengths
    position = first_index + jnp.arange(row_total, dtype=jnp.int32)
    begins = jnp.max(
        jnp.where(starts_all[None, :] <= position[:, None], starts_all[None, :], 0), axis=1
    )
    return position - begins


def recurrence_terms(decay_rows, input_rows, decay_param, conv_values, resets):
    recur_gate = jax.nn.sigmoid(decay_rows)
    input_open = jax.nn.sigmoid(input_rows)
    decay_now = jnp.exp(-CD * recur_gate * jax.nn.softplus(-decay_param))
    multiplier = jnp.where(
        resets[:, None], 1.0, jnp.sqrt(jnp.maximum(1.0 - decay_now * decay_now, FLOOR_VALUE))
    )
    kept_decay = jnp.where(resets[:, None], 0.0, decay_now)
    return (kept_decay, multiplier * input_open * conv_values, decay_now)


def row_scale(values):
    squares_sum = lax.psum(jnp.sum(values * values, axis=1), "tp")
    return lax.rsqrt(squares_sum / D + EPSILON)


def spread_rows(values):
    return lax.all_gather(values, "tp", axis=1, tiled=True)


def spread_grads(values):
    return lax.all_gather(values, "tp", axis=1, tiled=True)


def reduce_features(values):
    return lax.psum_scatter(values, "tp", scatter_dimension=1, tiled=True)


def norm_back(values, row_scales, gain_vector, upstream):
    weighted = upstream * gain_vector
    inner_sum = lax.psum(jnp.sum(weighted * values, axis=1), "tp")
    cubed = row_scales * row_scales * row_scales * inner_sum / D
    back_rows = row_scales[:, None] * weighted - values * cubed[:, None]
    return (back_rows, jnp.sum(upstream * values * row_scales[:, None], axis=0))


def block_mix(blocked, matrices):
    mixed_blocks = jnp.einsum("tnb,nbc->tnc", blocked, matrices, preferred_element_type=jnp.float32)
    return mixed_blocks.reshape(blocked.shape[0], -1)


def block_outer(blocked, gradients):
    shaped = gradients.reshape(blocked.shape)
    outer_sum = jnp.einsum("tnb,tnc->nbc", blocked, shaped, preferred_element_type=jnp.float32)
    return outer_sum.reshape(blocked.shape[1], -1)


def block_back(gradients, matrices):
    shaped = gradients.reshape(gradients.shape[0], matrices.shape[0], matrices.shape[1])
    backed = jnp.einsum("tnc,nbc->tnb", shaped, matrices, preferred_element_type=jnp.float32)
    return backed.reshape(gradients.shape[0], -1)


def shards(
    tokens,
    mix_gain,
    scan_branch,
    gate_branch,
    kernel_taps,
    kernel_bias,
    decay_gate,
    decay_bias,
    input_gate,
    input_bias,
    decay_logit,
    mixer_out,
    feed_gain,
    gate_weight,
    up_weight,
    down_weight,
    lengths,
    cotangent,
):
    row_count = tokens.shape[0]
    seq_devices = lax.axis_size("seq")
    shard_index = lax.axis_index("seq")
    offsets = seq_offsets(lengths, shard_index * row_count, row_count)
    resets = offsets == 0
    gathered = (
        lax.all_gather(mix_gain, "seq", axis=0, tiled=True),
        lax.all_gather(scan_branch, "seq", axis=0, tiled=True),
        lax.all_gather(gate_branch, "seq", axis=0, tiled=True),
        lax.all_gather(kernel_taps, "seq", axis=1, tiled=True),
        lax.all_gather(kernel_bias, "seq", axis=0, tiled=True),
        lax.all_gather(decay_gate, "seq", axis=1, tiled=True),
        lax.all_gather(decay_bias, "seq", axis=0, tiled=True),
        lax.all_gather(input_gate, "seq", axis=1, tiled=True),
        lax.all_gather(input_bias, "seq", axis=0, tiled=True),
        lax.all_gather(decay_logit, "seq", axis=0, tiled=True),
        lax.all_gather(mixer_out, "seq", axis=1, tiled=True),
        lax.all_gather(feed_gain, "seq", axis=0, tiled=True),
        lax.all_gather(gate_weight, "seq", axis=0, tiled=True),
        lax.all_gather(up_weight, "seq", axis=0, tiled=True),
        lax.all_gather(down_weight, "seq", axis=1, tiled=True),
    )
    mix_f = gathered[0].astype(jnp.float32)
    taps_f = gathered[3].astype(jnp.float32)
    taps_bias = gathered[4].astype(jnp.float32)
    feed_f = gathered[11].astype(jnp.float32)
    tokens_f = tokens.astype(jnp.float32)
    scale_first = row_scale(tokens_f)
    normed_first = spread_rows((tokens_f * scale_first[:, None] * mix_f).astype(jnp.bfloat16))
    scan_rows = matmul(normed_first, gathered[1])
    gate_rows = matmul(normed_first, gathered[2])
    gelu_rows, gelu_pull = jax.vjp(smooth_gelu, gate_rows)
    rim_rows = from_behind(scan_rows[row_count - (KW - 1) :], "seq", 1)
    padded_rows = jnp.concatenate([rim_rows, scan_rows], axis=0)
    conv_sum = taps_bias + taps_f[0] * scan_rows
    for lag_step in range(1, KW):
        lagged = padded_rows[KW - 1 - lag_step : KW - 1 - lag_step + row_count]
        conv_sum = conv_sum + jnp.where(
            (offsets >= lag_step)[:, None], taps_f[lag_step] * lagged, 0.0
        )
    conv_rows = conv_sum.astype(jnp.bfloat16)
    lanes = scan_rows.shape[1]
    groups = lanes // BW
    conv_blocks = conv_rows.reshape(row_count, groups, BW)
    decay_mats = gathered[5].reshape(groups, BW, BW)
    input_mats = gathered[7].reshape(groups, BW, BW)
    decay_rows = block_mix(conv_blocks, decay_mats) + gathered[6].astype(jnp.float32)
    input_rows = block_mix(conv_blocks, input_mats) + gathered[8].astype(jnp.float32)

    def local_terms(decay_in, input_in, logit_in, conv_in):
        kept_part, driven_part, decay_part = recurrence_terms(
            decay_in, input_in, logit_in, conv_in, resets
        )
        return ((kept_part, driven_part), decay_part)

    terms_out, terms_pull, decay_now = jax.vjp(
        local_terms,
        decay_rows,
        input_rows,
        gathered[9].astype(jnp.float32),
        conv_rows.astype(jnp.float32),
        has_aux=True,
    )
    kept_decay, driven = terms_out
    local_prod, local_state = lax.associative_scan(combine, (kept_decay, driven), axis=0)
    before = entering(
        (local_prod[row_count - 1], local_state[row_count - 1]),
        "seq",
        combine,
        (jnp.ones((lanes,), jnp.float32), jnp.zeros((lanes,), jnp.float32)),
        False,
    )
    state_in = before[1]
    hidden_state = local_state + local_prod * state_in[None, :]
    mixed = (gelu_rows * hidden_state).astype(jnp.bfloat16)
    resid = tokens_f + reduce_features(matmul(mixed, gathered[10]))
    scale_second = row_scale(resid)
    normed_second = spread_rows((resid * scale_second[:, None] * feed_f).astype(jnp.bfloat16))
    gate_pre = matmul(normed_second, gathered[12])
    up_pre = matmul(normed_second, gathered[13])
    gelu_mid, mid_pull = jax.vjp(smooth_gelu, gate_pre)
    hidden_mid = (gelu_mid * up_pre).astype(jnp.bfloat16)
    block_out = resid + reduce_features(matmul(hidden_mid, gathered[14]))
    cot_full = spread_grads(cotangent)
    down_grad = matmul_tn(hidden_mid, cot_full)
    grad_mid = matmul_nt(cot_full, gathered[14])
    grad_gate = mid_pull(grad_mid * up_pre)[0].astype(jnp.bfloat16)
    grad_up = (grad_mid * gelu_mid).astype(jnp.bfloat16)
    gate_grad = matmul_tn(normed_second, grad_gate)
    up_grad = matmul_tn(normed_second, grad_up)
    grad_second = reduce_features(
        matmul_nt(grad_gate, gathered[12]) + matmul_nt(grad_up, gathered[13])
    )
    back_second, feed_grad = norm_back(resid, scale_second, feed_f, grad_second)
    grad_resid = cotangent.astype(jnp.float32) + back_second
    grad_branch = spread_grads(grad_resid.astype(jnp.bfloat16))
    out_grad = matmul_tn(mixed, grad_branch)
    grad_mixed = matmul_nt(grad_branch, gathered[10])
    grad_hidden = grad_mixed * gelu_rows
    grad_gate_rows = gelu_pull(grad_mixed * hidden_state)[0].astype(jnp.bfloat16)
    next_decay = jnp.concatenate([kept_decay[1:], jnp.ones_like(kept_decay[:1])], axis=0)
    tail_prod, local_adjoint = lax.associative_scan(
        combine, (next_decay, grad_hidden), reverse=True, axis=0
    )
    after = entering(
        (local_prod[row_count - 1], kept_decay[0] * local_adjoint[0]),
        "seq",
        combine,
        (jnp.ones((lanes,), jnp.float32), jnp.zeros((lanes,), jnp.float32)),
        True,
    )
    adjoint_in = after[1]
    adjoint = local_adjoint + tail_prod * adjoint_in[None, :]
    prev_state = jnp.concatenate([state_in[None, :], hidden_state[:-1]], axis=0)
    grad_decay_rows, grad_input_rows, logit_grad, conv_direct = terms_pull(
        (adjoint * prev_state, adjoint)
    )
    decay_grad_low = grad_decay_rows.astype(jnp.bfloat16)
    input_grad_low = grad_input_rows.astype(jnp.bfloat16)
    decay_w_grad = block_outer(conv_blocks, decay_grad_low)
    input_w_grad = block_outer(conv_blocks, input_grad_low)
    decay_b_grad = jnp.sum(decay_grad_low.astype(jnp.float32), axis=0)
    input_b_grad = jnp.sum(input_grad_low.astype(jnp.float32), axis=0)
    grad_conv = (
        conv_direct
        + block_back(decay_grad_low, decay_mats)
        + block_back(input_grad_low, input_mats)
    )
    rim_back = from_behind(grad_conv[: KW - 1], "seq", -1)
    grad_extended = jnp.concatenate([grad_conv, rim_back], axis=0)
    ext_offsets = seq_offsets(lengths, shard_index * row_count, row_count + KW - 1)
    grad_scan = taps_f[0] * grad_conv
    tap_grads = [jnp.sum(grad_conv * scan_rows, axis=0)]
    for lag_step in range(1, KW):
        ahead = grad_extended[lag_step : lag_step + row_count]
        ahead_ok = (ext_offsets[lag_step : lag_step + row_count] >= lag_step)[:, None]
        grad_scan = grad_scan + jnp.where(ahead_ok, taps_f[lag_step] * ahead, 0.0)
        lagged = padded_rows[KW - 1 - lag_step : KW - 1 - lag_step + row_count]
        tap_grads.append(
            jnp.sum(jnp.where((offsets >= lag_step)[:, None], grad_conv * lagged, 0.0), axis=0)
        )
    taps_grad = jnp.stack(tap_grads, axis=0)
    taps_bias_grad = jnp.sum(grad_conv, axis=0)
    scan_grad_low = grad_scan.astype(jnp.bfloat16)
    scan_w_grad = matmul_tn(normed_first, scan_grad_low)
    gatebr_grad = matmul_tn(normed_first, grad_gate_rows)
    grad_first = reduce_features(
        matmul_nt(scan_grad_low, gathered[1]) + matmul_nt(grad_gate_rows, gathered[2])
    )
    back_first, mix_grad = norm_back(tokens_f, scale_first, mix_f, grad_first)
    tokens_grad = grad_resid + back_first
    decay_total = jnp.sum(decay_now, axis=0)
    summed = (
        lax.psum_scatter(mix_grad, "seq", scatter_dimension=0, tiled=True),
        lax.psum_scatter(scan_w_grad, "seq", scatter_dimension=0, tiled=True),
        lax.psum_scatter(gatebr_grad, "seq", scatter_dimension=0, tiled=True),
        lax.psum_scatter(taps_grad, "seq", scatter_dimension=1, tiled=True),
        lax.psum_scatter(taps_bias_grad, "seq", scatter_dimension=0, tiled=True),
        lax.psum_scatter(decay_w_grad, "seq", scatter_dimension=1, tiled=True),
        lax.psum_scatter(decay_b_grad, "seq", scatter_dimension=0, tiled=True),
        lax.psum_scatter(input_w_grad, "seq", scatter_dimension=1, tiled=True),
        lax.psum_scatter(input_b_grad, "seq", scatter_dimension=0, tiled=True),
        lax.psum_scatter(logit_grad, "seq", scatter_dimension=0, tiled=True),
        lax.psum_scatter(out_grad, "seq", scatter_dimension=1, tiled=True),
        lax.psum_scatter(feed_grad, "seq", scatter_dimension=0, tiled=True),
        lax.psum_scatter(gate_grad, "seq", scatter_dimension=0, tiled=True),
        lax.psum_scatter(up_grad, "seq", scatter_dimension=0, tiled=True),
        lax.psum_scatter(down_grad, "seq", scatter_dimension=1, tiled=True),
        lax.psum_scatter(decay_total, "seq", scatter_dimension=0, tiled=True),
    )
    mean_decay = summed[15] / (row_count * seq_devices)
    return (
        block_out,
        tokens_grad,
        summed[0],
        summed[1],
        summed[2],
        summed[3],
        summed[4],
        summed[5],
        summed[6],
        summed[7],
        summed[8],
        summed[9],
        summed[10],
        summed[11],
        summed[12],
        summed[13],
        summed[14],
        mean_decay,
    )


def solution(mesh):
    placed = (
        P("seq", "tp"),
        P(("tp", "seq")),
        P("seq", "tp"),
        P("seq", "tp"),
        P(None, ("tp", "seq")),
        P(("tp", "seq")),
        P("tp", "seq"),
        P(("tp", "seq")),
        P("tp", "seq"),
        P(("tp", "seq")),
        P(("tp", "seq")),
        P("tp", "seq"),
        P(("tp", "seq")),
        P("seq", "tp"),
        P("seq", "tp"),
        P("tp", "seq"),
        P(),
        P("seq", "tp"),
    )
    return jax.shard_map(
        shards,
        mesh=mesh,
        in_specs=placed,
        out_specs=(
            P("seq", "tp"),
            P("seq", "tp"),
            P(("tp", "seq")),
            P("seq", "tp"),
            P("seq", "tp"),
            P(None, ("tp", "seq")),
            P(("tp", "seq")),
            P("tp", "seq"),
            P(("tp", "seq")),
            P("tp", "seq"),
            P(("tp", "seq")),
            P(("tp", "seq")),
            P("tp", "seq"),
            P(("tp", "seq")),
            P("seq", "tp"),
            P("seq", "tp"),
            P("tp", "seq"),
            P(("tp", "seq")),
        ),
        check_vma=False,
    )
```

profile of v0, /device:TPU:0, one launch (start us, length us, event | category | flops | bytes accessed | tf_op | source)
XLA Modules:
  0.0 2211.0 jit_solution(12924295569123605493)
XLA Ops:
  15.7 26.0 %all-reduce.88 = (bf16[640]{0:T(1024)(128)(2,1)S(1)}, bf16[512]{0:T(512)(128)(2,1)S(1)}, bf16[640]{0:T(1024)(128)(2,1)S(1)}, bf16[640]{0:T(1024)(128)(2,1)S(1)},...) all-reduce(bf16[640]{0:T(1024)(128)(2,1)S(1)} %dynamic-update-slice.3, ...), channel_id=1, replica_groups=mesh['seq'=8,'tp'=4] {'seq'}, use_global_device_ids=true, to_apply=%add.77 | all-reduce | flops 3584 | bytes 14336
  43.1 12.0 psum.28
  59.2 7.7 all-gather
  67.1 9.5 all_gather.74
  76.6 40.6 %all-gather.15.cloned.1.call-done = bf16[768,2048]{1,0:T(8,128)(2,1)} async-done(((bf16[768,512]{1,0:T(8,128)(2,1)}), bf16[768,2048]{1,0:T(8,128)(2,1)}) %all-gather.15.cloned.1.call-update) | async-done | bytes 3145744 | tf_op jit(solution)/shard_map/all_gather | solution.py:89
  124.3 9.9 all_gather.77
  136.0 13.3 add_convert_fusion
  301.5 5.5 slice.629
  307.0 5.5 slice.630
  347.6 5.6 pad.257
  354.0 8.8 all-gather.2
  363.8 5.6 pad.238
  373.7 8.2 all-gather.1
  382.0 10.0 multiply_convert_fusion.2
  392.0 6.6 fusion.111
  399.9 108.3 %reduce-scatter.20.cloned.1.call-done = f32[768,512]{1,0:T(8,128)} async-done(((f32[768,2048]{1,0:T(8,128)}), f32[768,512]{1,0:T(8,128)}) %reduce-scatter.20.cloned.1.call-update) | async-done | bytes 1572880 | tf_op jit(solution)/shard_map/reduce_scatter | solution.py:97
  510.6 11.6 psum.29
  527.9 28.1 %all-gather.25.cloned.1.call-done = bf16[2048,1536]{1,0:T(8,128)(2,1)} async-done(((bf16[256,1536]{1,0:T(8,128)(2,1)}), bf16[2048,1536]{1,0:T(8,128)(2,1)}) %all-gather.25.cloned.1.call-update) | async-done | bytes 6291472 | tf_op jit(solution)/shard_map/all_gather | solution.py:163
  556.0 65.6 %all-gather.23.cloned.1.call-done = bf16[768,2048]{1,0:T(8,128)(2,1)} async-done(((bf16[768,512]{1,0:T(8,128)(2,1)}), bf16[768,2048]{1,0:T(8,128)(2,1)}) %all-gather.23.cloned.1.call-update) | async-done | bytes 3145744 | tf_op jit(solution)/shard_map/all_gather | solution.py:89
  621.6 9.5 fusion.112
  631.1 36.6 %all-gather.27.cloned.1.call-done = bf16[2048,1536]{1,0:T(8,128)(2,1)} async-done(((bf16[256,1536]{1,0:T(8,128)(2,1)}), bf16[2048,1536]{1,0:T(8,128)(2,1)}) %all-gather.27.cloned.1.call-update) | async-done | bytes 6291472 | tf_op jit(solution)/shard_map/all_gather | solution.py:164
  667.7 9.6 fusion.113
  677.3 55.5 %all-gather.31.cloned.1.call-done = bf16[768,2048]{1,0:T(8,128)(2,1)} async-done(((bf16[768,512]{1,0:T(8,128)(2,1)}), bf16[768,2048]{1,0:T(8,128)(2,1)}) %all-gather.31.cloned.1.call-update) | async-done | bytes 3145744 | tf_op jit(solution)/shard_map/all_gather | solution.py:93
  732.8 47.1 %all-gather.29.cloned.1.call-done = bf16[1536,2048]{1,0:T(8,128)(2,1)} async-done(((bf16[1536,256]{1,0:T(8,128)(2,1)}), bf16[1536,2048]{1,0:T(8,128)(2,1)}) %all-gather.29.cloned.1.call-update) | async-done | bytes 6291472 | tf_op jit(solution)/shard_map/all_gather | solution.py:165
  779.9 14.3 multiply_convert_fusion
  794.2 8.9 fusion.115
  803.2 7.1 convolution_add_fusion.1
  810.4 110.8 %reduce-scatter.24.cloned.1.call-done = f32[768,512]{1,0:T(8,128)} async-done(((f32[768,2048]{1,0:T(8,128)}), f32[768,512]{1,0:T(8,128)}) %reduce-scatter.24.cloned.1.call-update) | async-done | bytes 1572880 | tf_op jit(solution)/shard_map/reduce_scatter | solution.py:97
  923.7 11.6 psum.30
  944.2 5.5 slice.724
  959.8 8.3 slice.725
  968.1 8.3 slice.731
  981.7 19.9 all-gather.33.cloned.1.call-done
  1001.5 9.1 fusion.13
  1020.2 8.3 slice.723
  1155.2 5.6 pad.275
  1181.2 9.1 all-gather.3
  1190.3 5.8 while.27
  1201.7 5.6 pad.292
  1211.0 15.8 rev.9
  1226.8 15.8 rev.8
  1242.7 6.0 multiply_reduce_fusion
  1266.4 10.4 select_reduce_fusion.2
  1279.5 7.2 copy.98
  1289.9 7.2 copy.99
  1308.6 9.9 fusion.114
  1318.6 12.4 fusion.122
  1331.0 10.3 fusion.123
  1341.6 10.5 fusion.124
  1353.3 6.8 fusion.121
  1360.2 6.9 fusion.118
  1367.2 6.9 fusion.117
  1377.0 30.2 %reduce-scatter.42.cloned.1.call-done = f32[3200,4]{1,0:T(8,128)} async-done(((f32[25600,4]{1,0:T(8,128)}), f32[3200,4]{1,0:T(8,128)}) %reduce-scatter.42.cloned.1.call-update) | async-done | bytes 51216
  1409.8 96.1 %reduce-scatter.44.cloned.1.call-done = f32[3200,4]{1,0:T(8,128)} async-done(((f32[25600,4]{1,0:T(8,128)}), f32[3200,4]{1,0:T(8,128)}) %reduce-scatter.44.cloned.1.call-update) | async-done | bytes 51216
  1508.6 110.2 %reduce-scatter.26.cloned.1.call-done = f32[768,512]{1,0:T(8,128)} async-done(((f32[768,2048]{1,0:T(8,128)}), f32[768,512]{1,0:T(8,128)}) %reduce-scatter.26.cloned.1.call-update) | async-done | bytes 1572880 | tf_op jit(solution)/shard_map/reduce_scatter | solution.py:97
  1620.9 24.5 %all-reduce.87 = (f32[512]{0:T(512)S(1)}, f32[640]{0:T(1024)S(1)}, f32[640]{0:T(1024)S(1)}, f32[640]{0:T(1024)S(1)}, f32[640]{0:T(1024)S(1)}, /*index=5*/f32[512]{0:T(512)S(1)}, f32[640]{0:T(1024)S(1)}) all-reduce(f32[512]{0:T(512)S(1)} %get-tuple-element.154, ...), channel_id=6, replica_groups=mesh['seq'=8,'tp'=4] {'seq'}, use_global_device_ids=true, to_apply=%region_20.21.clone | all-reduce | flops 4224 | bytes 33792
  1648.9 11.8 psum.31
  1661.3 71.2 %reduce-scatter.22.cloned.1.call-done = f32[768,512]{1,0:T(8,128)} async-done(((f32[768,2048]{1,0:T(8,128)}), f32[768,512]{1,0:T(8,128)}) %reduce-scatter.22.cloned.1.call-update) | async-done | bytes 1572880 | tf_op jit(solution)/shard_map/reduce_scatter | solution.py:97
  1736.4 92.9 %reduce-scatter.34.cloned.1.call-done = f32[256,1536]{1,0:T(8,128)} async-done(((f32[2048,1536]{1,0:T(8,128)}), f32[256,1536]{1,0:T(8,128)}) %reduce-scatter.34.cloned.1.call-update) | async-done | bytes 1572880 | tf_op jit(solution)/shard_map/reduce_scatter | solution.py:310
  1829.4 96.5 %reduce-scatter.36.cloned.1.call-done = f32[256,1536]{1,0:T(8,128)} async-done(((f32[2048,1536]{1,0:T(8,128)}), f32[256,1536]{1,0:T(8,128)}) %reduce-scatter.36.cloned.1.call-update) | async-done | bytes 1572880 | tf_op jit(solution)/shard_map/reduce_scatter | solution.py:311
  1925.9 96.3 %reduce-scatter.38.cloned.1.call-done = f32[1536,256]{1,0:T(8,128)} async-done(((f32[1536,2048]{1,0:T(8,128)}), f32[1536,256]{1,0:T(8,128)}) %reduce-scatter.38.cloned.1.call-update) | async-done | bytes 1572880 | tf_op jit(solution)/shard_map/reduce_scatter | solution.py:312
  2022.2 60.5 %reduce-scatter.32.cloned.1.call-done = f32[640,256]{1,0:T(8,128)} async-done(((f32[640,2048]{1,0:T(8,128)}), f32[640,256]{1,0:T(8,128)}) %reduce-scatter.32.cloned.1.call-update) | async-done | bytes 655376 | tf_op jit(solution)/shard_map/reduce_scatter | solution.py:308
  2082.8 60.9 %reduce-scatter.30.cloned.1.call-done = f32[256,640]{1,0:T(8,128)} async-done(((f32[2048,640]{1,0:T(8,128)}), f32[256,640]{1,0:T(8,128)}) %reduce-scatter.30.cloned.1.call-update) | async-done | bytes 655376 | tf_op jit(solution)/shard_map/reduce_scatter | solution.py:300
  2143.7 60.5 %reduce-scatter.28.cloned.1.call-done = f32[256,640]{1,0:T(8,128)} async-done(((f32[2048,640]{1,0:T(8,128)}), f32[256,640]{1,0:T(8,128)}) %reduce-scatter.28.cloned.1.call-update) | async-done | bytes 655376 | tf_op jit(solution)/shard_map/reduce_scatter | solution.py:299
  (713 shorter events, 474.4 us)
Async XLA Ops:
  7.2 69.4 %all-gather.19.cloned.1.call-start = ((), (), s32[]{:S(2)}) async-start(), calls=%async_computation.15 | async-start | bytes 2949120 | tf_op jit(solution)/shard_map/all_gather | solution.py:152
  7.9 50.9 %copy-start.124 = (s32[6]{0:T(128)S(1)}, s32[6]{0:T(128)}, u32[]{:S(2)}) copy-start(s32[6]{0:T(128)} %param.38) | copy-start | bytes 76
  7.9 109.3 %all-gather.15.cloned.1.call-start = ((), (), s32[]{:S(2)}) async-start(), calls=%async_computation.13 | async-start | bytes 3932160 | tf_op jit(solution)/shard_map/all_gather | solution.py:89
  8.0 51.2 %copy-start.120 = (bf16[4,80]{1,0:T(4,128)(2,1)S(1)}, bf16[4,80]{1,0:T(4,128)(2,1)}, u32[]{:S(2)}) copy-start(bf16[4,80]{1,0:T(4,128)(2,1)} %param.26) | copy-start | bytes 1924
  41.7 25.4 %copy-start.116 = (bf16[640]{0:T(1024)(128)(2,1)}, bf16[640]{0:T(1024)(128)(2,1)S(1)}, u32[]{:S(2)}) copy-start(bf16[640]{0:T(1024)(128)(2,1)S(1)} %get-tuple-element.188) | copy-start | bytes 3844
  41.7 17.4 copy-start.81
  41.7 25.4 %copy-start.85 = (bf16[4,3200]{1,0:T(4,128)(2,1)S(1)}, bf16[4,3200]{1,0:T(4,128)(2,1)}, u32[]{:S(2)}) copy-start(bf16[4,3200]{1,0:T(4,128)(2,1)} %param.28) | copy-start | bytes 76804
  55.1 21.4 copy-start.60
  57.4 324.5 %all-gather.17.cloned.1.call-start = ((), (), s32[]{:S(2)}) async-start(), calls=%async_computation.14 | async-start | bytes 2949120 | tf_op jit(solution)/shard_map/all_gather | solution.py:153
  58.2 333.8 %all-gather.21.cloned.1.call-start = ((), (), s32[]{:S(2)}) async-start(), calls=%async_computation.16 | async-start | bytes 2949120 | tf_op jit(solution)/shard_map/all_gather | solution.py:161
  58.7 449.4 %reduce-scatter.20.cloned.1.call-start = ((), (), s32[]{:S(2)}) async-start(), calls=%async_computation.17 | async-start | bytes 7864320 | tf_op jit(solution)/shard_map/reduce_scatter | solution.py:97
  59.0 58.2 %copy-start.119 = (s32[6]{0:T(128)}, s32[6]{0:T(128)S(1)}, u32[]{:S(2)}) copy-start(s32[6]{0:T(128)S(1)} %bitcast_subtract_fusion) | copy-start | bytes 76
  59.1 76.8 %copy-start.109 = (pred[768]{0:T(1024)(128)(4,1)}, pred[768]{0:T(1024)(128)(4,1)S(1)}, u32[]{:S(2)}) copy-start(pred[768]{0:T(1024)(128)(4,1)S(1)} %get-tuple-element.305) | copy-start | bytes 2308
  59.1 76.8 %copy-start.111 = (pred[768]{0:T(1024)(128)(4,1)}, pred[768]{0:T(1024)(128)(4,1)S(1)}, u32[]{:S(2)}) copy-start(pred[768]{0:T(1024)(128)(4,1)S(1)} %get-tuple-element.306) | copy-start | bytes 2308
  59.1 76.8 %copy-start.113 = (pred[768]{0:T(1024)(128)(4,1)}, pred[768]{0:T(1024)(128)(4,1)S(1)}, u32[]{:S(2)}) copy-start(pred[768]{0:T(1024)(128)(4,1)S(1)} %get-tuple-element.307) | copy-start | bytes 2308
  59.1 102.1 %copy-start.83 = (pred[768]{0:T(1024)(128)(4,1)}, pred[768]{0:T(1024)(128)(4,1)S(1)}, u32[]{:S(2)}) copy-start(pred[768]{0:T(1024)(128)(4,1)S(1)} %get-tuple-element.304) | copy-start | bytes 2308
  67.0 68.9 %copy-start.71 = (f32[640]{0:T(1024)}, f32[640]{0:T(1024)S(1)}, u32[]{:S(2)}) copy-start(f32[640]{0:T(1024)S(1)} %get-tuple-element.157) | copy-start | bytes 7684
  67.0 68.9 %copy-start.73 = (f32[640]{0:T(1024)}, f32[640]{0:T(1024)S(1)}, u32[]{:S(2)}) copy-start(f32[640]{0:T(1024)S(1)} %get-tuple-element.158) | copy-start | bytes 7684
  67.0 68.9 %copy-start.75 = (f32[640]{0:T(1024)}, f32[640]{0:T(1024)S(1)}, u32[]{:S(2)}) copy-start(f32[640]{0:T(1024)S(1)} %get-tuple-element.159) | copy-start | bytes 7684
  67.0 68.9 %copy-start.77 = (f32[640]{0:T(1024)}, f32[640]{0:T(1024)S(1)}, u32[]{:S(2)}) copy-start(f32[640]{0:T(1024)S(1)} %get-tuple-element.160) | copy-start | bytes 7684
  76.6 47.7 %copy-start.86 = (bf16[4,3200]{1,0:T(4,128)(2,1)S(1)}, bf16[4,3200]{1,0:T(4,128)(2,1)}, u32[]{:S(2)}) copy-start(bf16[4,3200]{1,0:T(4,128)(2,1)} %param.30) | copy-start | bytes 76804
  122.5 13.5 copy-start.18
  122.5 13.4 collective-permute-start
  135.8 19.5 copy-start.28
  135.9 14.1 copy-start.67
  301.5 12.5 copy-start.52
  347.6 15.1 copy-start.23
  398.6 157.4 %all-gather.25.cloned.1.call-start = ((), (), s32[]{:S(2)}) async-start(), calls=%async_computation.19 | async-start | bytes 7077888 | tf_op jit(solution)/shard_map/all_gather | solution.py:163
  399.2 222.4 %all-gather.23.cloned.1.call-start = ((), (), s32[]{:S(2)}) async-start(), calls=%async_computation.18 | async-start | bytes 3932160 | tf_op jit(solution)/shard_map/all_gather | solution.py:89
  510.6 425.4 %copy-start.1 = (f32[768,512]{1,0:T(8,128)}, f32[768,512]{1,0:T(8,128)S(1)}, u32[]{:S(2)}) copy-start(f32[768,512]{1,0:T(8,128)S(1)} %get-tuple-element.207) | copy-start | bytes 4718596
  525.3 142.4 %all-gather.27.cloned.1.call-start = ((), (), s32[]{:S(2)}) async-start(), calls=%async_computation.20 | async-start | bytes 7077888 | tf_op jit(solution)/shard_map/all_gather | solution.py:164
  526.1 206.7 %all-gather.31.cloned.1.call-start = ((), (), s32[]{:S(2)}) async-start(), calls=%async_computation.23 | async-start | bytes 3932160 | tf_op jit(solution)/shard_map/all_gather | solution.py:93
  526.8 253.1 %all-gather.29.cloned.1.call-start = ((), (), s32[]{:S(2)}) async-start(), calls=%async_computation.21 | async-start | bytes 7077888 | tf_op jit(solution)/shard_map/all_gather | solution.py:165
  527.4 393.8 %reduce-scatter.24.cloned.1.call-start = ((), (), s32[]{:S(2)}) async-start(), calls=%async_computation.24 | async-start | bytes 7864320 | tf_op jit(solution)/shard_map/reduce_scatter | solution.py:97
  810.3 191.2 %all-gather.33.cloned.1.call-start = ((), (), s32[]{:S(2)}) async-start(), calls=%async_computation.25 | async-start | bytes 3932160 | tf_op jit(solution)/shard_map/all_gather | solution.py:93
  939.5 436.0 %reduce-scatter.40.cloned.1.call-start = ((), (), s32[]{:S(2)}) async-start(), calls=%async_computation.33 | async-start | bytes 368640
  1181.2 17.1 copy-start.26
  1226.8 15.8 copy-start.4
  1226.8 15.8 copy-start.84
  1226.8 15.8 copy-start.96
  1277.8 129.4 %reduce-scatter.42.cloned.1.call-start = ((), (), s32[]{:S(2)}) async-start(), calls=%async_computation.34 | async-start | bytes 14745600
  1286.7 219.1 %reduce-scatter.44.cloned.1.call-start = ((), (), s32[]{:S(2)}) async-start(), calls=%async_computation.35 | async-start | bytes 14745600
  1288.1 9.4 collective-permute-start.1
  1297.1 321.7 %reduce-scatter.26.cloned.1.call-start = ((), (), s32[]{:S(2)}) async-start(), calls=%async_computation.26 | async-start | bytes 7864320 | tf_op jit(solution)/shard_map/reduce_scatter | solution.py:97
  1308.5 424.0 %reduce-scatter.22.cloned.1.call-start = ((), (), s32[]{:S(2)}) async-start(), calls=%async_computation.22 | async-start | bytes 7864320 | tf_op jit(solution)/shard_map/reduce_scatter | solution.py:97
  1318.5 510.8 %reduce-scatter.34.cloned.1.call-start = ((), (), s32[]{:S(2)}) async-start(), calls=%async_computation.30 | async-start | bytes 14155776 | tf_op jit(solution)/shard_map/reduce_scatter | solution.py:310
  1331.0 594.9 %reduce-scatter.36.cloned.1.call-start = ((), (), s32[]{:S(2)}) async-start(), calls=%async_computation.31 | async-start | bytes 14155776 | tf_op jit(solution)/shard_map/reduce_scatter | solution.py:311
  1341.4 680.9 %reduce-scatter.38.cloned.1.call-start = ((), (), s32[]{:S(2)}) async-start(), calls=%async_computation.32 | async-start | bytes 14155776 | tf_op jit(solution)/shard_map/reduce_scatter | solution.py:312
  1352.1 730.7 %reduce-scatter.32.cloned.1.call-start = ((), (), s32[]{:S(2)}) async-start(), calls=%async_computation.29 | async-start | bytes 5898240 | tf_op jit(solution)/shard_map/reduce_scatter | solution.py:308
  1360.2 783.5 %reduce-scatter.30.cloned.1.call-start = ((), (), s32[]{:S(2)}) async-start(), calls=%async_computation.28 | async-start | bytes 5898240 | tf_op jit(solution)/shard_map/reduce_scatter | solution.py:300
  1367.1 837.1 %reduce-scatter.28.cloned.1.call-start = ((), (), s32[]{:S(2)}) async-start(), calls=%async_computation.27 | async-start | bytes 5898240 | tf_op jit(solution)/shard_map/reduce_scatter | solution.py:299
  1374.1 244.7 %copy-start.5 = (bf16[768,512]{1,0:T(8,128)(2,1)S(1)}, bf16[768,512]{1,0:T(8,128)(2,1)}, u32[]{:S(2)}) copy-start(bf16[768,512]{1,0:T(8,128)(2,1)} %param.22) | copy-start | bytes 2359300
  1374.1 244.7 %copy-start.61 = (f32[768]{0:T(1024)S(1)}, f32[768]{0:T(1024)}, u32[]{:S(2)}) copy-start(f32[768]{0:T(1024)} %copy-done.60) | copy-start | bytes 9220
  1374.1 244.7 %copy-start.82 = (f32[512]{0:T(512)S(1)}, f32[512]{0:T(512)}, u32[]{:S(2)}) copy-start(f32[512]{0:T(512)} %copy-done.81) | copy-start | bytes 6148
  1505.8 115.1 %copy-start.89 = (f32[640]{0:T(1024)S(1)}, f32[640]{0:T(1024)}, u32[]{:S(2)}) copy-start(f32[640]{0:T(1024)} %get-tuple-element.225) | copy-start | bytes 7684
  1505.8 115.1 %copy-start.90 = (f32[640]{0:T(1024)S(1)}, f32[640]{0:T(1024)}, u32[]{:S(2)}) copy-start(f32[640]{0:T(1024)} %get-tuple-element.156) | copy-start | bytes 7684
  1505.8 115.1 %copy-start.92 = (f32[640]{0:T(1024)S(1)}, f32[640]{0:T(1024)}, u32[]{:S(2)}) copy-start(f32[640]{0:T(1024)} %get-tuple-element.308) | copy-start | bytes 7684
  1505.8 115.1 %copy-start.115 = (f32[512]{0:T(512)S(1)}, f32[512]{0:T(512)}, u32[]{:S(2)}) copy-start(f32[512]{0:T(512)} %get-tuple-element.152) | copy-start | bytes 6148
  1505.8 155.5 %copy-start.80 = (f32[768]{0:T(1024)S(1)}, f32[768]{0:T(1024)}, u32[]{:S(2)}) copy-start(f32[768]{0:T(1024)} %copy-done.79) | copy-start | bytes 9220
  1505.8 226.6 %copy-start.2 = (f32[768,512]{1,0:T(8,128)S(1)}, f32[768,512]{1,0:T(8,128)}, u32[]{:S(2)}) copy-start(f32[768,512]{1,0:T(8,128)} %copy-done.1) | copy-start | bytes 4718596
  1505.9 226.6 %copy-start.20 = (bf16[768,512]{1,0:T(8,128)(2,1)S(1)}, bf16[768,512]{1,0:T(8,128)(2,1)}, u32[]{:S(2)}) copy-start(bf16[768,512]{1,0:T(8,128)(2,1)} %param.39) | copy-start | bytes 2359300
  1505.9 226.6 %copy-start.57 = (f32[768]{0:T(1024)S(1)}, f32[768]{0:T(1024)}, u32[]{:S(2)}) copy-start(f32[768]{0:T(1024)} %copy-done.56) | copy-start | bytes 9220
  1505.9 226.6 %copy-start.62 = (f32[512]{0:T(512)S(1)}, f32[512]{0:T(512)}, u32[]{:S(2)}) copy-start(f32[512]{0:T(512)} %convert_element_type.83) | copy-start | bytes 6148
  1505.9 226.6 %copy-start.70 = (f32[768]{0:T(1024)S(1)}, f32[768]{0:T(1024)}, u32[]{:S(2)}) copy-start(f32[768]{0:T(1024)} %copy-done.69) | copy-start | bytes 9220
  (88 other events, 424.8 us)
Sparse Core Ops, SparseCore 0:
  9.9 32.9 all-gather.18
  57.5 59.6 all-gather.14
  119.1 29.3 all-gather.16
  150.2 30.4 all-gather.20
  398.7 109.3 reduce-scatter.19
  509.9 46.0 all-gather.24
  558.1 63.4 all-gather.22
  623.5 44.2 all-gather.26
  669.3 63.4 all-gather.30
  734.5 45.3 all-gather.28
  810.4 110.7 reduce-scatter.23
  939.7 61.8 all-gather.32
  1277.9 30.5 reduce-scatter.39
  1312.0 95.1 reduce-scatter.41
  1410.6 95.1 reduce-scatter.43
  1508.0 110.7 reduce-scatter.25
  1620.9 111.5 reduce-scatter.21
  1736.4 92.9 reduce-scatter.33
  1833.4 92.3 reduce-scatter.35
  1929.8 92.3 reduce-scatter.37
  2026.2 56.5 reduce-scatter.31
  2087.1 56.5 reduce-scatter.29
  2147.7 56.5 reduce-scatter.27
where the time goes:
time: 2230 us; the launch traced here: 2210 us
  waiting for transfers between devices  1290 us (58%)
  local copies, waits for them, and re-layouts  427 us (19%)
  matrix products  163 us (7%)
  other arithmetic  153 us (7%)
  blocking collectives  151 us (7%)
    reduce_scatter x4, waiting for transfers between devices, reduce_features(): return lax.psum_scatter(values, 'tp', scatter_dimension=1, tiled=True)  400 us
    slice x69, local copies, waits for them, and re-layouts, shards(): lax.associative_scan(combine, (next_decay, grad_hidden), reverse=True, ax...  146 us
    unnamed x26, waiting for transfers between devices  131 us
    slice x64, local copies, waits for them, and re-layouts, shards(): lax.associative_scan(combine, (kept_decay, driven), axis=0)  107 us
    all_gather x2, waiting for transfers between devices, spread_rows(): return lax.all_gather(values, 'tp', axis=1, tiled=True)  106 us
    reduce_scatter x1, waiting for transfers between devices, shards(): lax.psum_scatter(up_grad, 'seq', scatter_dimension=0, tiled=True)  96.5 us
    reduce_scatter x1, waiting for transfers between devices, shards(): lax.psum_scatter(down_grad, 'seq', scatter_dimension=1, tiled=True)  96.3 us
    reduce_scatter x1, waiting for transfers between devices, shards(): lax.psum_scatter(gate_grad, 'seq', scatter_dimension=0, tiled=True)  92.9 us
  transfers between devices with their start and end apart: 25, of which 19 were waited for; matrix products, arithmetic and copies ran while one was open for 19% of the time, Pallas kernels for 0%

commit v1 on v0

--- a/solution.py
+++ b/solution.py
@@ -1,7 +1,12 @@
+import functools
+
 import jax
 import jax.numpy as jnp
 from jax import lax
+from jax.experimental import pallas as pl
+from jax.experimental.pallas import tpu as pltpu
 from jax.sharding import PartitionSpec as P
+
 
 D = 2048
 KW = 4
@@ -122,7 +127,7 @@
     return backed.reshape(gradients.shape[0], -1)
 
 
-def shards(
+def shards_general(
     tokens,
     mix_gain,
     scan_branch,
@@ -335,6 +340,852 @@
     )
 
 
+MESH = pl.DeviceIdType.MESH
+F32 = jnp.float32
+BF16 = jnp.bfloat16
+LINE = 4
+PLANE = 8
+CHUNK = 128
+ANY = pl.BlockSpec(memory_space=pl.ANY)
+VM = pl.BlockSpec(memory_space=pltpu.VMEM)
+
+
+def flip(place, bit):
+    step = 1 << bit
+    return place + step - 2 * step * lax.rem(place // step, 2)
+
+
+def flip_all(place, bits):
+    for bit in range(3):
+        if bits & (1 << bit):
+            place = flip(place, bit)
+    return place
+
+
+def meet(s, z):
+    barrier = pltpu.get_barrier_semaphore()
+    for bits in range(1, PLANE):
+        pl.semaphore_signal(barrier, inc=1, device_id=(flip_all(s, bits), z), device_id_type=MESH)
+    for step in range(1, LINE):
+        pl.semaphore_signal(
+            barrier, inc=1, device_id=(s, lax.rem(z + step, LINE)), device_id_type=MESH
+        )
+    pl.semaphore_wait(barrier, PLANE - 1 + LINE - 1)
+
+
+def remote(src, dst, send, recv, target):
+    return pltpu.make_async_remote_copy(
+        src_ref=src,
+        dst_ref=dst,
+        send_sem=send,
+        recv_sem=recv,
+        device_id=target,
+        device_id_type=MESH,
+    )
+
+
+class LineGather:
+    def __init__(self, s, z, own_at, full_at, send, recv):
+        self.s, self.z = s, z
+        self.own_at, self.full_at = own_at, full_at
+        self.send, self.recv = send, recv
+
+    def copy(self, way, level, c):
+        sign = 1 - 2 * way
+        origin = self.z - sign * level
+        src = self.own_at(c) if level == 0 else self.full_at(origin, c)
+        return remote(
+            src,
+            self.full_at(origin, c),
+            self.send.at[way, level, c],
+            self.recv.at[way, level, c],
+            (self.s, self.z + sign),
+        )
+
+    def arrival(self, way, level, c):
+        sign = 1 - 2 * way
+        part = self.full_at(self.z - sign * (level + 1), c)
+        return remote(
+            part,
+            part,
+            self.send.at[way, level, c],
+            self.recv.at[way, level, c],
+            (self.s, self.z + sign),
+        )
+
+    def sends(self, way, level):
+        if way == 0:
+            return (self.z >= level) & (self.z < LINE - 1)
+        return (self.z <= LINE - 1 - level) & (self.z > 0)
+
+    def gets(self, way, level):
+        return self.z >= level + 1 if way == 0 else self.z <= LINE - 2 - level
+
+    def start(self, c):
+        for way in range(2):
+            pl.when(self.sends(way, 0))(lambda way=way: self.copy(way, 0, c).start())
+
+    def forward(self, level, c):
+        for way in range(2):
+            pl.when(self.gets(way, level - 1))(
+                lambda way=way: self.arrival(way, level - 1, c).wait_recv()
+            )
+            if level < LINE - 1:
+                pl.when(self.sends(way, level))(
+                    lambda way=way: self.copy(way, level, c).start()
+                )
+
+    def drain(self, c):
+        for way in range(2):
+            for level in range(LINE - 1):
+                pl.when(self.sends(way, level))(
+                    lambda way=way, level=level: self.copy(way, level, c).wait_send()
+                )
+
+
+class PlaneGather:
+    def __init__(self, s, z, own, block_at, half_at, send, recv, local):
+        self.s, self.z, self.own = s, z, own
+        self.block_at, self.half_at = block_at, half_at
+        self.send, self.recv, self.local = send, recv, local
+        self.near = (flip(s, 1), flip(s, 2))
+        self.diag = flip(self.near[0], 2)
+        self.twin = flip(s, 0)
+        self.twin_near = (flip(self.near[0], 0), flip(self.near[1], 0))
+        self.twin_diag = flip(self.diag, 0)
+
+    def plan(self, i):
+        block, half = self.block_at, self.half_at
+        return (
+            (self.own, block(self.s), self.near[0]),
+            (self.own, block(self.s), self.near[1]),
+            (half(self.near[1], 0), half(self.near[1], 0), self.near[0]),
+            (half(self.near[0], 1), half(self.near[0], 1), self.near[1]),
+            (self.own, block(self.s), self.twin),
+            (block(self.near[0]), block(self.near[0]), self.twin),
+            (block(self.near[1]), block(self.near[1]), self.twin),
+            (half(self.diag, 0), half(self.diag, 0), self.twin),
+            (half(self.diag, 1), half(self.diag, 1), self.twin),
+        )[i]
+
+    def landing(self, i):
+        block, half = self.block_at, self.half_at
+        return (
+            block(self.near[0]),
+            block(self.near[1]),
+            half(self.diag, 0),
+            half(self.diag, 1),
+            block(self.twin),
+            block(self.twin_near[0]),
+            block(self.twin_near[1]),
+            half(self.twin_diag, 0),
+            half(self.twin_diag, 1),
+        )[i]
+
+    def copy(self, i):
+        src, dst, target = self.plan(i)
+        return remote(src, dst, self.send.at[i], self.recv.at[i], (target, self.z))
+
+    def got(self, i):
+        part = self.landing(i)
+        remote(part, part, self.send.at[i], self.recv.at[i], (self.twin, self.z)).wait_recv()
+
+    def keep(self):
+        return pltpu.make_async_copy(self.own, self.block_at(self.s), self.local)
+
+    def start(self):
+        for i in (0, 1, 4):
+            self.copy(i).start()
+        self.keep().start()
+
+    def turn(self):
+        self.got(0)
+        self.copy(3).start()
+        self.copy(5).start()
+        self.got(1)
+        self.copy(2).start()
+        self.copy(6).start()
+
+    def last(self):
+        self.got(2)
+        self.copy(7).start()
+        self.got(3)
+        self.copy(8).start()
+
+    def finish(self):
+        for i in range(4, 9):
+            self.got(i)
+        for i in range(9):
+            self.copy(i).wait_send()
+        self.keep().wait()
+
+
+class Spread:
+    def __init__(self, s, z, slot_at, send, recv):
+        self.s, self.z, self.slot_at, self.send, self.recv = s, z, slot_at, send, recv
+
+    def copy(self, bits, origin):
+        slot = self.slot_at(origin)
+        return remote(
+            slot,
+            slot,
+            self.send.at[bits - 1],
+            self.recv.at[bits - 1],
+            (flip_all(self.s, bits), self.z),
+        )
+
+    def start(self):
+        for bits in range(1, PLANE):
+            self.copy(bits, self.s).start()
+
+    def finish(self):
+        for bits in range(1, PLANE):
+            self.copy(bits, flip_all(self.s, bits)).wait_recv()
+        for bits in range(1, PLANE):
+            self.copy(bits, self.s).wait_send()
+
+
+def rows_of(ref, size, parts=2):
+    def block(place):
+        return ref.at[pl.ds(pl.multiple_of(place * size, size), size)]
+
+    def half(place, h):
+        part = size // parts
+        return ref.at[pl.ds(pl.multiple_of(place * size + h * part, part), part)]
+
+    return block, half
+
+
+def columns_of(ref, size):
+    height = ref.shape[0] // 2
+
+    def block(place):
+        return ref.at[:, pl.ds(pl.multiple_of(place * size, size), size)]
+
+    def half(place, h):
+        return ref.at[
+            pl.ds(h * height, height), pl.ds(pl.multiple_of(place * size, size), size)
+        ]
+
+    return block, half
+
+
+def chunk_rows(c):
+    return pl.ds(pl.multiple_of(c * CHUNK, CHUNK), CHUNK)
+
+
+def feature_columns(z, width):
+    return pl.ds(pl.multiple_of(z * width, width), width)
+
+
+def each_chunk(chunks, body):
+    lax.fori_loop(0, chunks, lambda c, carry: (body(c), carry)[1], 0)
+
+
+def gather_kernel(
+    tok, pack, gains, scan, gate, mix, ffn,
+    tok_all, pack_all, gains_all, scan_all, gate_all, mix_all, ffn_all,
+    line_send, line_recv, gain_send, gain_recv, plane_send, plane_recv, small_send, small_recv, local,
+):
+    s, z = lax.axis_index("seq"), lax.axis_index("tp")
+    chunks, width = tok.shape[0] // CHUNK, tok.shape[1]
+    line = LineGather(
+        s, z,
+        lambda c: tok.at[chunk_rows(c)],
+        lambda o, c: tok_all.at[chunk_rows(c), feature_columns(o, width)],
+        line_send, line_recv,
+    )
+    gain_line = LineGather(
+        s, z, lambda c: gains_all.at[z], lambda o, c: gains_all.at[o], gain_send, gain_recv
+    )
+    planes = []
+    for i, (own, full, make) in enumerate(
+        (
+            (scan, scan_all, rows_of),
+            (gate, gate_all, rows_of),
+            (mix, mix_all, columns_of),
+            (ffn, ffn_all, rows_of),
+        )
+    ):
+        size = own.shape[1] if make is columns_of else own.shape[0]
+        block, half = make(full, size)
+        planes.append(
+            PlaneGather(s, z, own, block, half, plane_send.at[i], plane_recv.at[i], local.at[i])
+        )
+    packs = Spread(s, z, lambda p: pack_all.at[p], small_send.at[0], small_recv.at[0])
+    gain_plane = Spread(s, z, lambda p: gains_all.at[z, p], small_send.at[1], small_recv.at[1])
+    keeps = [
+        pltpu.make_async_copy(gains, gains_all.at[z, s], local.at[4]),
+        pltpu.make_async_copy(pack, pack_all.at[s], local.at[5]),
+        pltpu.make_async_copy(tok, tok_all.at[:, feature_columns(z, width)], local.at[6]),
+    ]
+    for keep in keeps:
+        keep.start()
+    meet(s, z)
+    for keep in keeps[:2]:
+        keep.wait()
+    gain_plane.start()
+    packs.start()
+    for c in range(chunks):
+        line.start(c)
+    for plane in planes:
+        plane.start()
+    gain_plane.finish()
+    packs.finish()
+    gain_line.start(0)
+    for c in range(chunks):
+        line.forward(1, c)
+    gain_line.forward(1, 0)
+    planes[0].turn()
+    for c in range(chunks):
+        line.forward(2, c)
+    gain_line.forward(2, 0)
+    planes[1].turn()
+    planes[0].last()
+    planes[2].turn()
+    planes[1].last()
+    planes[3].turn()
+    planes[2].last()
+    for c in range(chunks):
+        line.forward(3, c)
+    gain_line.forward(3, 0)
+    planes[3].last()
+    for plane in planes:
+        plane.finish()
+    for c in range(chunks):
+        line.drain(c)
+    gain_line.drain(0)
+    keeps[2].wait()
+
+
+def dma(*shape):
+    return pltpu.SemaphoreType.DMA(shape)
+
+
+def struct(shape, kind):
+    return jax.ShapeDtypeStruct(shape, kind)
+
+
+def gather_first(tok, pack, gains, scan, gate, mix, ffn):
+    rows, width = tok.shape
+    chunks = rows // CHUNK
+    return pl.pallas_call(
+        gather_kernel,
+        out_shape=(
+            struct((rows, width * LINE), BF16),
+            struct((PLANE,) + pack.shape, pack.dtype),
+            struct((LINE, PLANE) + gains.shape, F32),
+            struct((scan.shape[0] * PLANE, scan.shape[1]), BF16),
+            struct((gate.shape[0] * PLANE, gate.shape[1]), BF16),
+            struct((mix.shape[0], mix.shape[1] * PLANE), BF16),
+            struct((ffn.shape[0] * PLANE, ffn.shape[1]), BF16),
+        ),
+        in_specs=[ANY] * 7,
+        out_specs=[ANY] * 7,
+        scratch_shapes=[
+            dma(2, LINE - 1, chunks), dma(2, LINE - 1, chunks),
+            dma(2, LINE - 1, 1), dma(2, LINE - 1, 1),
+            dma(4, 9), dma(4, 9), dma(2, 7), dma(2, 7), dma(7),
+        ],
+        compiler_params=pltpu.CompilerParams(collective_id=0, has_side_effects=True),
+        name="gather_first",
+    )(tok, pack, gains, scan, gate, mix, ffn)
+
+
+def sigmoid(values):
+    return 0.5 * jnp.tanh(0.5 * values) + 0.5
+
+
+ROOT = 0.7978845608028654
+
+
+def gelu_of(values):
+    return 0.5 * values * (1.0 + jnp.tanh(ROOT * (values + 0.044715 * values * values * values)))
+
+
+def gelu_pair(values):
+    squared = values * values
+    bent = jnp.tanh(ROOT * values * (1.0 + 0.044715 * squared))
+    half = 0.5 * (1.0 + bent)
+    slope = half + 0.5 * values * (1.0 - bent * bent) * (ROOT * (1.0 + 3 * 0.044715 * squared))
+    return values * half, slope
+
+
+def dot(left_side, right_side):
+    return jnp.dot(left_side, right_side, preferred_element_type=F32)
+
+
+def dot_nt(left_side, right_side):
+    return lax.dot_general(
+        left_side, right_side, (((1,), (1,)), ((), ())), preferred_element_type=F32
+    )
+
+
+def dot_tn(left_side, right_side):
+    return lax.dot_general(
+        left_side, right_side, (((0,), (0,)), ((), ())), preferred_element_type=F32
+    )
+
+
+SUBS = 8
+
+
+LANE = 128
+
+
+def put(ref, at, values):
+    for lane in range(ref.shape[0]):
+        ref[lane, at, :] = values[:, lane * LANE : (lane + 1) * LANE]
+
+
+def get(ref, at):
+    return jnp.concatenate([ref[lane, at, :] for lane in range(ref.shape[0])], axis=1)
+
+
+def strided(ref, step):
+    at = pl.ds(step, SUBS, stride=ref.shape[1] // SUBS)
+    return [ref[lane, at, :] for lane in range(ref.shape[0])]
+
+
+def strided_put(ref, step, values):
+    at = pl.ds(step, SUBS, stride=ref.shape[1] // SUBS)
+    for lane in range(ref.shape[0]):
+        ref[lane, at, :] = values[lane]
+
+
+def lanes_of(values):
+    return [values[:, i * LANE : (i + 1) * LANE] for i in range(values.shape[1] // LANE)]
+
+
+def recur_kernel(
+    tok_all, scan_w, gate_w, gates_w, par, gain, masks, cot, up, down,
+    normed, scan_rows, gate_rows, conv, decay_rows, input_rows, hidden, mixed, state, decay_sum,
+    cot_all, up_all, down_all,
+    kept, driven, slots,
+    line_send, line_recv, plane_send, plane_recv, small_send, small_recv, halo_send, halo_recv, local,
+):
+    s, z = lax.axis_index("seq"), lax.axis_index("tp")
+    rows, features = tok_all.shape
+    chunks, width, lanes = rows // CHUNK, cot.shape[1], gate_w.shape[1]
+    line = LineGather(
+        s, z,
+        lambda c: cot.at[chunk_rows(c)],
+        lambda o, c: cot_all.at[chunk_rows(c), feature_columns(o, width)],
+        line_send, line_recv,
+    )
+    planes = [
+        PlaneGather(
+            s, z, up, *rows_of(up_all, up.shape[0]), plane_send.at[0], plane_recv.at[0], local.at[0]
+        ),
+        PlaneGather(
+            s, z, down, *columns_of(down_all, down.shape[1]), plane_send.at[1], plane_recv.at[1],
+            local.at[1],
+        ),
+    ]
+    keep = pltpu.make_async_copy(cot, cot_all.at[:, feature_columns(z, width)], local.at[2])
+    keep.start()
+    meet(s, z)
+    for c in range(chunks):
+        line.start(c)
+    for plane in planes:
+        plane.start()
+
+    def project(c):
+        at = chunk_rows(c)
+        x = tok_all[at, :].astype(F32)
+        scale = lax.rsqrt(jnp.sum(x * x, axis=1, keepdims=True) / features + EPSILON)
+        low = (x * scale * gain[0:1, :]).astype(BF16)
+        normed[at, :] = low
+        scan_rows[pl.ds(pl.multiple_of(c * CHUNK + 8, 8), CHUNK), :] = dot(low, scan_w[...])
+        gate_rows[at, :] = dot(low, gate_w[...])
+
+    each_chunk(chunks, project)
+    halo = remote(
+        scan_rows.at[pl.ds(rows, 8)], scan_rows.at[pl.ds(0, 8)], halo_send, halo_recv,
+        (lax.rem(s + 1, PLANE), z),
+    )
+    first, final = s == 0, s == PLANE - 1
+    pl.when(jnp.logical_not(final))(lambda: halo.start())
+
+    @pl.when(first)
+    def _():
+        scan_rows[0:8, :] = jnp.zeros((8, lanes), F32)
+
+    decay_sum[...] = jnp.zeros_like(decay_sum)
+    pl.when(jnp.logical_not(first))(lambda: halo.wait_recv())
+
+    def gates(c):
+        at = chunk_rows(c)
+        block = scan_rows[pl.ds(pl.multiple_of(c * CHUNK, 8), CHUNK + 8), :]
+        mask = masks[at, :]
+        total = par[4:5, :] + par[0:1, :] * block[8:, :]
+        for lag in range(1, KW):
+            total = total + mask[:, lag : lag + 1] * (
+                par[lag : lag + 1, :] * block[8 - lag : 8 - lag + CHUNK, :]
+            )
+        low = total.astype(BF16)
+        conv[at, :] = low
+        rows_now = dot(low, gates_w[...])
+        decays = rows_now[:, :lanes] + par[5:6, :]
+        inputs = rows_now[:, lanes:] + par[6:7, :]
+        decay_rows[at, :] = decays
+        input_rows[at, :] = inputs
+        decay = jnp.exp(-sigmoid(decays) * par[7:8, :])
+        goes_on = mask[:, 0:1]
+        multiplier = 1.0 + goes_on * (
+            jnp.sqrt(jnp.maximum(1.0 - decay * decay, FLOOR_VALUE)) - 1.0
+        )
+        put(kept, at, goes_on * decay)
+        put(driven, at, multiplier * sigmoid(inputs) * low.astype(F32))
+        decay_sum[0:1, :] += jnp.sum(decay, axis=0, keepdims=True)
+        line.forward(1, c)
+
+    each_chunk(chunks, gates)
+    count = rows // SUBS
+
+    def total_of(step, carry):
+        keeps, drives = strided(kept, step), strided(driven, step)
+        return (
+            [p * k for p, k in zip(carry[0], keeps)],
+            [k * v + d for k, v, d in zip(keeps, carry[1], drives)],
+        )
+
+    groups = lanes // LANE
+    product, value = lax.fori_loop(
+        0,
+        count,
+        total_of,
+        ([jnp.ones((SUBS, LANE), F32)] * groups, [jnp.zeros((SUBS, LANE), F32)] * groups),
+        unroll=4,
+    )
+    product, value = jnp.concatenate(product, axis=1), jnp.concatenate(value, axis=1)
+    whole = (jnp.ones((1, lanes), F32), jnp.zeros((1, lanes), F32))
+    for sub in range(SUBS):
+        here = product[sub : sub + 1, :]
+        whole = (whole[0] * here, here * whole[1] + value[sub : sub + 1, :])
+    slots[s, 0:1, :] = whole[0]
+    slots[s, 1:2, :] = whole[1]
+    spread = Spread(s, z, lambda p: slots.at[p], small_send, small_recv)
+    spread.start()
+    planes[0].turn()
+    spread.finish()
+    entry = jnp.zeros((1, lanes), F32)
+    for place in range(PLANE - 1):
+        entry = jnp.where(
+            place < s, slots[place, 0:1, :] * entry + slots[place, 1:2, :], entry
+        )
+    state[...] = jnp.broadcast_to(entry, (8, lanes))
+    entries = []
+    for sub in range(SUBS):
+        entries.append(entry)
+        entry = product[sub : sub + 1, :] * entry + value[sub : sub + 1, :]
+
+    def step_on(step, now):
+        keeps, drives = strided(kept, step), strided(driven, step)
+        now = [k * v + d for k, v, d in zip(keeps, now, drives)]
+        strided_put(driven, step, now)
+        return now
+
+    lax.fori_loop(0, count, step_on, lanes_of(jnp.concatenate(entries, axis=0)), unroll=4)
+
+    def mix(c):
+        at = chunk_rows(c)
+        now = get(driven, at)
+        hidden[at, :] = now
+        mixed[at, :] = (gelu_of(gate_rows[at, :]) * now).astype(BF16)
+        line.forward(2, c)
+
+    each_chunk(chunks, mix)
+    planes[1].turn()
+    planes[0].last()
+    for c in range(chunks):
+        line.forward(3, c)
+    planes[1].last()
+    for plane in planes:
+        plane.finish()
+    for c in range(chunks):
+        line.drain(c)
+    pl.when(jnp.logical_not(final))(lambda: halo.wait_send())
+    keep.wait()
+
+
+def recur_forward(tok_all, scan_w, gate_w, gates_w, par, gain, masks, cot, up, down):
+    rows, features = tok_all.shape
+    lanes = gate_w.shape[1]
+    chunks = rows // CHUNK
+    return pl.pallas_call(
+        recur_kernel,
+        out_shape=(
+            struct((rows, features), BF16),
+            struct((rows + 8, lanes), F32),
+            struct((rows, lanes), F32),
+            struct((rows, lanes), BF16),
+            struct((rows, lanes), F32),
+            struct((rows, lanes), F32),
+            struct((rows, lanes), F32),
+            struct((rows, lanes), BF16),
+            struct((8, lanes), F32),
+            struct((8, lanes), F32),
+            struct((rows, features), BF16),
+            struct((up.shape[0] * PLANE, up.shape[1]), BF16),
+            struct((down.shape[0], down.shape[1] * PLANE), BF16),
+        ),
+        in_specs=[VM] * 7 + [ANY] * 3,
+        out_specs=[VM] * 10 + [ANY] * 3,
+        scratch_shapes=[
+            pltpu.VMEM((lanes // LANE, rows, LANE), F32),
+            pltpu.VMEM((lanes // LANE, rows, LANE), F32),
+            pltpu.VMEM((PLANE, 8, lanes), F32),
+            dma(2, LINE - 1, chunks), dma(2, LINE - 1, chunks),
+            dma(2, 9), dma(2, 9), dma(7), dma(7),
+            pltpu.SemaphoreType.DMA, pltpu.SemaphoreType.DMA, dma(3),
+        ],
+        compiler_params=pltpu.CompilerParams(
+            collective_id=1, has_side_effects=True, vmem_limit_bytes=58 << 20
+        ),
+        name="recur_forward",
+    )(tok_all, scan_w, gate_w, gates_w, par, gain, masks, cot, up, down)
+
+
+def shards_fast(
+    tokens, mix_gain, scan_branch, gate_branch, kernel_taps, kernel_bias, decay_gate, decay_bias,
+    input_gate, input_bias, decay_logit, mixer_out, feed_gain, gate_weight, up_weight, down_weight,
+    lengths, cotangent,
+):
+    row_count = tokens.shape[0]
+    seq_devices = lax.axis_size("seq")
+    shard_index = lax.axis_index("seq")
+    ext_offsets = seq_offsets(lengths, shard_index * row_count, row_count + 8)
+    lag_at = jnp.array([1, 1, 2, 3, 0, 0, 0, 0], jnp.int32)
+    masks = (ext_offsets[:, None] >= lag_at[None, :]).astype(F32)
+    lanes = scan_branch.shape[1]
+    part = lanes // seq_devices
+    groups = lanes // BW
+    flat = jnp.concatenate(
+        [
+            kernel_taps.reshape(-1), kernel_bias, decay_bias, input_bias, decay_logit,
+            decay_gate.reshape(-1), input_gate.reshape(-1),
+        ]
+    )
+    pack_rows = -(-flat.shape[0] // (128 * 16)) * 16
+    pack = jnp.pad(flat, (0, pack_rows * 128 - flat.shape[0])).reshape(pack_rows, 128)
+    gains = jnp.pad(
+        jnp.concatenate([mix_gain, feed_gain]).astype(F32)[None, :], ((0, 7), (0, 0))
+    )
+    tok_all, pack_all, gains_all, scan_w, gate_w, mix_w, ffn_gate = gather_first(
+        tokens, pack, gains, scan_branch, gate_branch, mixer_out, gate_weight
+    )
+    pack_all = pack_all.reshape(seq_devices, -1)
+    at = 0
+
+    def take(rows):
+        nonlocal at
+        piece = pack_all[:, at : at + rows * part].reshape(seq_devices, rows, part)
+        at += rows * part
+        return piece.transpose(1, 0, 2).reshape(rows, lanes).astype(F32)
+
+    taps_f = take(KW)
+    biases = take(3)
+    logit_f = take(1)
+    gate_cut = groups * BW * BW // seq_devices
+    mats = [
+        pack_all[:, at + i * gate_cut : at + (i + 1) * gate_cut]
+        .reshape(seq_devices, groups, BW // seq_devices, BW)
+        .transpose(1, 0, 2, 3)
+        .reshape(groups, BW, BW)
+        for i in range(2)
+    ]
+    gates_w = jnp.concatenate(
+        [
+            jnp.concatenate(
+                [jnp.pad(m[g], ((0, 0), (g * BW, lanes - (g + 1) * BW))) for g in range(groups)], 0
+            )
+            for m in mats
+        ],
+        1,
+    )
+    par = jnp.concatenate(
+        [taps_f, biases, CD * jax.nn.softplus(-logit_f), jnp.zeros((8, lanes), F32)], 0
+    )
+    half = gains.shape[1] // 2
+    gain_full = gains_all[:, :, 0, :].reshape(-1, 2, half).transpose(1, 0, 2).reshape(2, -1)
+    gain_full = jnp.pad(gain_full, ((0, 6), (0, 0)))
+    (
+        normed_first, scan_pad, gate_rows, conv_rows, decay_rows, input_rows, hidden_state, mixed,
+        state_rows, decay_sums, cot_full, up_w, down_w,
+    ) = recur_forward(
+        tok_all, scan_w, gate_w, gates_w, par, gain_full, masks, cotangent, up_weight, down_weight
+    )
+
+    offsets = ext_offsets[:row_count]
+    resets = offsets == 0
+    mix_f = lax.all_gather(mix_gain, "seq", axis=0, tiled=True).astype(F32)
+    feed_f = lax.all_gather(feed_gain, "seq", axis=0, tiled=True).astype(F32)
+    gathered=[None, scan_w, gate_w, None,None,None,biases[1],None,biases[2],logit_f[0],mix_w,None,ffn_gate,up_w,down_w]
+    taps_bias=biases[0]
+    normed_first_k=normed_first
+    tokens_f = tokens.astype(jnp.float32)
+    scale_first = row_scale(tokens_f)
+    scan_rows = scan_pad[8:]
+    gelu_rows, gelu_pull = jax.vjp(smooth_gelu, gate_rows)
+    rim_rows = from_behind(scan_rows[row_count - (KW - 1) :], "seq", 1)
+    padded_rows = jnp.concatenate([rim_rows, scan_rows], axis=0)
+    conv_sum = taps_bias + taps_f[0] * scan_rows
+    for lag_step in range(1, KW):
+        lagged = padded_rows[KW - 1 - lag_step : KW - 1 - lag_step + row_count]
+        conv_sum = conv_sum + jnp.where(
+            (offsets >= lag_step)[:, None], taps_f[lag_step] * lagged, 0.0
+        )
+    lanes = scan_rows.shape[1]
+    groups = lanes // BW
+    conv_blocks = conv_rows.reshape(row_count, groups, BW)
+    decay_mats = mats[0]
+    input_mats = mats[1]
+    decay_rows = block_mix(conv_blocks, decay_mats) + gathered[6].astype(jnp.float32)
+    input_rows = block_mix(conv_blocks, input_mats) + gathered[8].astype(jnp.float32)
+
+    def local_terms(decay_in, input_in, logit_in, conv_in):
+        kept_part, driven_part, decay_part = recurrence_terms(
+            decay_in, input_in, logit_in, conv_in, resets
+        )
+        return ((kept_part, driven_part), decay_part)
+
+    terms_out, terms_pull, decay_now = jax.vjp(
+        local_terms,
+        decay_rows,
+        input_rows,
+        gathered[9].astype(jnp.float32),
+        conv_rows.astype(jnp.float32),
+        has_aux=True,
+    )
+    kept_decay, driven = terms_out
+    local_prod, local_state = lax.associative_scan(combine, (kept_decay, driven), axis=0)
+    before = entering(
+        (local_prod[row_count - 1], local_state[row_count - 1]),
+        "seq",
+        combine,
+        (jnp.ones((lanes,), jnp.float32), jnp.zeros((lanes,), jnp.float32)),
+        False,
+    )
+    state_in = before[1]
+    state_in=state_rows[0]
+    resid = tokens_f + reduce_features(matmul(mixed, gathered[10]))
+    scale_second = row_scale(resid)
+    normed_second = spread_rows((resid * scale_second[:, None] * feed_f).astype(jnp.bfloat16))
+    gate_pre = matmul(normed_second, gathered[12])
+    up_pre = matmul(normed_second, gathered[13])
+    gelu_mid, mid_pull = jax.vjp(smooth_gelu, gate_pre)
+    hidden_mid = (gelu_mid * up_pre).astype(jnp.bfloat16)
+    block_out = resid + reduce_features(matmul(hidden_mid, gathered[14]))
+    down_grad = matmul_tn(hidden_mid, cot_full)
+    grad_mid = matmul_nt(cot_full, gathered[14])
+    grad_gate = mid_pull(grad_mid * up_pre)[0].astype(jnp.bfloat16)
+    grad_up = (grad_mid * gelu_mid).astype(jnp.bfloat16)
+    gate_grad = matmul_tn(normed_second, grad_gate)
+    up_grad = matmul_tn(normed_second, grad_up)
+    grad_second = reduce_features(
+        matmul_nt(grad_gate, gathered[12]) + matmul_nt(grad_up, gathered[13])
+    )
+    back_second, feed_grad = norm_back(resid, scale_second, feed_f, grad_second)
+    grad_resid = cotangent.astype(jnp.float32) + back_second
+    grad_branch = spread_grads(grad_resid.astype(jnp.bfloat16))
+    out_grad = matmul_tn(mixed, grad_branch)
+    grad_mixed = matmul_nt(grad_branch, gathered[10])
+    grad_hidden = grad_mixed * gelu_rows
+    grad_gate_rows = gelu_pull(grad_mixed * hidden_state)[0].astype(jnp.bfloat16)
+    next_decay = jnp.concatenate([kept_decay[1:], jnp.ones_like(kept_decay[:1])], axis=0)
+    tail_prod, local_adjoint = lax.associative_scan(
+        combine, (next_decay, grad_hidden), reverse=True, axis=0
+    )
+    after = entering(
+        (local_prod[row_count - 1], kept_decay[0] * local_adjoint[0]),
+        "seq",
+        combine,
+        (jnp.ones((lanes,), jnp.float32), jnp.zeros((lanes,), jnp.float32)),
+        True,
+    )
+    adjoint_in = after[1]
+    adjoint = local_adjoint + tail_prod * adjoint_in[None, :]
+    prev_state = jnp.concatenate([state_in[None, :], hidden_state[:-1]], axis=0)
+    grad_decay_rows, grad_input_rows, logit_grad, conv_direct = terms_pull(
+        (adjoint * prev_state, adjoint)
+    )
+    decay_grad_low = grad_decay_rows.astype(jnp.bfloat16)
+    input_grad_low = grad_input_rows.astype(jnp.bfloat16)
+    decay_w_grad = block_outer(conv_blocks, decay_grad_low)
+    input_w_grad = block_outer(conv_blocks, input_grad_low)
+    decay_b_grad = jnp.sum(decay_grad_low.astype(jnp.float32), axis=0)
+    input_b_grad = jnp.sum(input_grad_low.astype(jnp.float32), axis=0)
+    grad_conv = (
+        conv_direct
+        + block_back(decay_grad_low, decay_mats)
+        + block_back(input_grad_low, input_mats)
+    )
+    rim_back = from_behind(grad_conv[: KW - 1], "seq", -1)
+    grad_extended = jnp.concatenate([grad_conv, rim_back], axis=0)
+    ext_offsets = seq_offsets(lengths, shard_index * row_count, row_count + KW - 1)
+    grad_scan = taps_f[0] * grad_conv
+    tap_grads = [jnp.sum(grad_conv * scan_rows, axis=0)]
+    for lag_step in range(1, KW):
+        ahead = grad_extended[lag_step : lag_step + row_count]
+        ahead_ok = (ext_offsets[lag_step : lag_step + row_count] >= lag_step)[:, None]
+        grad_scan = grad_scan + jnp.where(ahead_ok, taps_f[lag_step] * ahead, 0.0)
+        lagged = padded_rows[KW - 1 - lag_step : KW - 1 - lag_step + row_count]
+        tap_grads.append(
+            jnp.sum(jnp.where((offsets >= lag_step)[:, None], grad_conv * lagged, 0.0), axis=0)
+        )
+    taps_grad = jnp.stack(tap_grads, axis=0)
+    taps_bias_grad = jnp.sum(grad_conv, axis=0)
+    scan_grad_low = grad_scan.astype(jnp.bfloat16)
+    scan_w_grad = matmul_tn(normed_first, scan_grad_low)
+    gatebr_grad = matmul_tn(normed_first, grad_gate_rows)
+    grad_first = reduce_features(
+        matmul_nt(scan_grad_low, gathered[1]) + matmul_nt(grad_gate_rows, gathered[2])
+    )
+    back_first, mix_grad = norm_back(tokens_f, scale_first, mix_f, grad_first)
+    tokens_grad = grad_resid + back_first
+    decay_total = decay_sums[0]
+    summed = (
+        lax.psum_scatter(mix_grad, "seq", scatter_dimension=0, tiled=True),
+        lax.psum_scatter(scan_w_grad, "seq", scatter_dimension=0, tiled=True),
+        lax.psum_scatter(gatebr_grad, "seq", scatter_dimension=0, tiled=True),
+        lax.psum_scatter(taps_grad, "seq", scatter_dimension=1, tiled=True),
+        lax.psum_scatter(taps_bias_grad, "seq", scatter_dimension=0, tiled=True),
+        lax.psum_scatter(decay_w_grad, "seq", scatter_dimension=1, tiled=True),
+        lax.psum_scatter(decay_b_grad, "seq", scatter_dimension=0, tiled=True),
+        lax.psum_scatter(input_w_grad, "seq", scatter_dimension=1, tiled=True),
+        lax.psum_scatter(input_b_grad, "seq", scatter_dimension=0, tiled=True),
+        lax.psum_scatter(logit_grad, "seq", scatter_dimension=0, tiled=True),
+        lax.psum_scatter(out_grad, "seq", scatter_dimension=1, tiled=True),
+        lax.psum_scatter(feed_grad, "seq", scatter_dimension=0, tiled=True),
+        lax.psum_scatter(gate_grad, "seq", scatter_dimension=0, tiled=True),
+        lax.psum_scatter(up_grad, "seq", scatter_dimension=0, tiled=True),
+        lax.psum_scatter(down_grad, "seq", scatter_dimension=1, tiled=True),
+        lax.psum_scatter(decay_total, "seq", scatter_dimension=0, tiled=True),
+    )
+    mean_decay = summed[15] / (row_count * seq_devices)
+    return (
+        block_out,
+        tokens_grad,
+        summed[0],
+        summed[1],
+        summed[2],
+        summed[3],
+        summed[4],
+        summed[5],
+        summed[6],
+        summed[7],
+        summed[8],
+        summed[9],
+        summed[10],
+        summed[11],
+        summed[12],
+        summed[13],
+        summed[14],
+        mean_decay,
+    )
+
+
 def solution(mesh):
     placed = (
         P("seq", "tp"),
@@ -357,7 +1208,7 @@
         P("seq", "tp"),
     )
     return jax.shard_map(
-        shards,
+        shards_fast if mesh.shape['seq']==8 else shards_general,
         mesh=mesh,
         in_specs=placed,
         out_specs=(

time: 2230 us -> 1990 us (0.89)
  waiting for transfers between devices: 1290 us -> 1030 us
  Pallas kernels: 0 us -> 169 us
  blocking collectives: 151 us -> 91.2 us
  local copies, waits for them, and re-layouts: 427 us -> 385 us
  other arithmetic: 153 us -> 125 us
    pallas_call x0 -> x2, Pallas kernels: none -> 169 us  [the longest x1 87.1 us: recur_forward(): pl.pallas_call(recur_kernel, out_shape=(struct((rows, features), BF16), s...]
    all_gather x6 -> x0, waiting for transfers between devices: 112 us -> none  [the longest x1 47.1 us: shards(): lax.all_gather(down_weight, 'seq', axis=1, tiled=True)]
    all_gather x2 -> x1, waiting for transfers between devices: 75.3 us -> 0.01 us  [spread_grads(): return lax.all_gather(values, 'tp', axis=1, tiled=True)]
    all_gather x2 -> x1, waiting for transfers between devices: 106 us -> 62 us  [spread_rows(): return lax.all_gather(values, 'tp', axis=1, tiled=True)]
    slice x137 -> x118, local copies, waits for them, and re-layouts: 255 us -> 217 us  [the longest x69 165 us: shards_fast(): lax.associative_scan(combine, (next_decay, grad_hidden), reverse=True, ax...]
    all_gather x3 -> x0, blocking collectives: 27 us -> none  [the longest x1 9.85 us: shards(): lax.all_gather(input_gate, 'seq', axis=1, tiled=True)]
    reduce_scatter x4, waiting for transfers between devices: 400 us -> 376 us  [reduce_features(): return lax.psum_scatter(values, 'tp', scatter_dimension=1, tiled=True)]
    pad x68 -> x50, local copies, waits for them, and re-layouts: 77.3 us -> 59.5 us  [the longest x34 48.2 us: shards_fast(): lax.associative_scan(combine, (next_decay, grad_hidden), reverse=True, ax...]
  transfers between devices with their start and end apart: 25 -> 17, of which waited for: 19 -> 13; matrix products, arithmetic and copies ran while one was open for 19% -> 28% of each run, Pallas kernels for 0% -> 0%
where the time goes in v1:
time: 1990 us; the launch traced here: 1970 us
  waiting for transfers between devices  1030 us (52%)
  local copies, waits for them, and re-layouts  385 us (19%)
  Pallas kernels  169 us (8%)
  matrix products  146 us (7%)
  other arithmetic  125 us (6%)
  blocking collectives  91.2 us (5%)
    reduce_scatter x4, waiting for transfers between devices, reduce_features(): return lax.psum_scatter(values, 'tp', scatter_dimension=1, tiled=True)  376 us
    slice x69, local copies, waits for them, and re-layouts, shards_fast(): lax.associative_scan(combine, (next_decay, grad_hidden), reverse=True, ax...  165 us
    unnamed x18, waiting for transfers between devices  122 us
    reduce_scatter x1, waiting for transfers between devices, shards_fast(): lax.psum_scatter(up_grad, 'seq', scatter_dimension=0, tiled=True)  96.5 us
    reduce_scatter x1, waiting for transfers between devices, shards_fast(): lax.psum_scatter(down_grad, 'seq', scatter_dimension=1, tiled=True)  96.4 us
    reduce_scatter x1, waiting for transfers between devices, shards_fast(): lax.psum_scatter(gate_grad, 'seq', scatter_dimension=0, tiled=True)  92.8 us
    pallas_call x1, Pallas kernels, recur_forward(): pl.pallas_call(recur_kernel, out_shape=(struct((rows, features), BF16), s...  87.1 us
    pallas_call x1, Pallas kernels, gather_first(): pl.pallas_call(gather_kernel, out_shape=(struct((rows, width * LINE), BF1...  82 us
  transfers between devices with their start and end apart: 17, of which 13 were waited for; matrix products, arithmetic and copies ran while one was open for 28% of the time, Pallas kernels for 0%

profile of v1, /device:TPU:0, one launch (start us, length us, event | category | flops | bytes accessed | tf_op | source)
XLA Modules:
  0.0 1966.6 jit_solution(11098911234091783595)
XLA Ops:
  14.3 82.0 %gather_first.1 = (bf16[768,2048]{1,0:T(8,128)(2,1)}, bf16[8,208,128]{2,1,0:T(8,128)(2,1)}, f32[4,8,8,128]{3,2,1,0:T(8,128)}, bf16[2048,640]{1,0:T(8,128)(2,1)},...) custom-call(bf16[768,512]{1,0:T(8,128)(2,1)} %tok.1, ...), custom_call_target="tpu_custom_call" | custom-call | tf_op jit(solution)/shard_map/gather_first/pallas_call | solution.py:672
  104.2 8.4 fusion.68.gates_w
  112.6 87.1 %recur_forward.1 = (bf16[768,2048]{1,0:T(8,128)(2,1)}, f32[776,640]{1,0:T(8,128)}, f32[768,640]{1,0:T(8,128)}, bf16[768,640]{1,0:T(8,128)(2,1)}, f32[768,640]{1,...) custom-call(bf16[768,2048]{1,0:T(8,128)(2,1)} %get-tuple-element.120, ...), custom_call_target="tpu_custom_call" | custom-call | tf_op jit(solution)/shard_map/recur_forward/pallas_call | solution.py:916
  199.7 5.7 fusion.139
  207.8 14.2 all-reduce.78
  222.0 93.7 %reduce-scatter.20.cloned.1.call-done = f32[768,512]{1,0:T(8,128)} async-done(((f32[768,2048]{1,0:T(8,128)}), f32[768,512]{1,0:T(8,128)}) %reduce-scatter.20.cloned.1.call-update) | async-done | bytes 1572880 | tf_op jit(solution)/shard_map/reduce_scatter | solution.py:102
  318.1 10.9 psum.28
  330.2 62.0 %all-gather.5.cloned.1.call-done = bf16[768,2048]{1,0:T(8,128)(2,1)} async-done(((bf16[768,512]{1,0:T(8,128)(2,1)}), bf16[768,2048]{1,0:T(8,128)(2,1)}) %all-gather.5.cloned.1.call-update) | async-done | bytes 3145744 | tf_op jit(solution)/shard_map/all_gather | solution.py:94
  392.2 10.5 fusion.141
  402.7 9.6 fusion.140
  412.4 12.9 multiply_convert_fusion
  425.3 6.9 fusion.143
  432.2 10.2 convolution_add_fusion.1
  451.2 100.9 %reduce-scatter.24.cloned.1.call-done = f32[768,512]{1,0:T(8,128)} async-done(((f32[768,2048]{1,0:T(8,128)}), f32[768,512]{1,0:T(8,128)}) %reduce-scatter.24.cloned.1.call-update) | async-done | bytes 1572880 | tf_op jit(solution)/shard_map/reduce_scatter | solution.py:102
  554.5 11.7 all-reduce.77
  573.7 5.5 slice.663
  579.2 5.4 slice.664
  627.4 5.4 slice.577
  632.7 5.4 slice.583
  638.2 5.4 slice.573
  669.0 5.6 pad.522
  675.3 9.2 all-gather.1
  685.1 8.4 slice.578
  693.5 8.3 slice.584
  701.9 8.5 slice.574
  717.8 9.1 fusion.35
  726.9 5.4 slice.575
  732.3 5.4 slice.579
  737.6 8.3 slice.576
  746.0 8.4 slice.580
  849.9 5.4 slice.570
  898.3 5.6 pad.238
  910.8 8.6 slice.571
  926.2 5.5 pad.237
  936.1 9.0 all-gather
  945.0 5.5 while.14
  950.6 5.7 pad.256
  958.5 5.6 pad.255
  967.7 15.8 rev.9
  983.5 15.9 rev.8
  999.4 6.2 multiply_reduce_fusion
  1024.5 8.7 fusion.43
  1035.9 7.2 copy.130
  1046.7 7.2 copy.129
  1061.0 4.6 convolution_add_fusion
  1067.3 9.9 fusion.142
  1077.3 11.6 fusion.150
  1089.0 10.2 fusion.151
  1099.3 10.1 fusion.152
  1109.5 7.1 fusion.146
  1117.8 6.8 fusion.149
  1125.7 7.0 fusion.145
  1136.8 25.9 %reduce-scatter.44.cloned.1.call-done = f32[3200,4]{1,0:T(8,128)} async-done(((f32[25600,4]{1,0:T(8,128)}), f32[3200,4]{1,0:T(8,128)}) %reduce-scatter.44.cloned.1.call-update) | async-done | bytes 51216
  1165.3 96.2 %reduce-scatter.42.cloned.1.call-done = f32[3200,4]{1,0:T(8,128)} async-done(((f32[25600,4]{1,0:T(8,128)}), f32[3200,4]{1,0:T(8,128)}) %reduce-scatter.42.cloned.1.call-update) | async-done | bytes 51216
  1264.2 110.3 %reduce-scatter.26.cloned.1.call-done = f32[768,512]{1,0:T(8,128)} async-done(((f32[768,2048]{1,0:T(8,128)}), f32[768,512]{1,0:T(8,128)}) %reduce-scatter.26.cloned.1.call-update) | async-done | bytes 1572880 | tf_op jit(solution)/shard_map/reduce_scatter | solution.py:102
  1376.7 24.5 %all-reduce.76 = (f32[512]{0:T(512)S(1)}, f32[640]{0:T(1024)S(1)}, f32[640]{0:T(1024)S(1)}, f32[640]{0:T(1024)S(1)}, f32[640]{0:T(1024)S(1)}, /*index=5*/f32[512]{0:T(512)S(1)}, f32[640]{0:T(1024)S(1)}) all-reduce(f32[512]{0:T(512)S(1)} %get-tuple-element.144, ...), channel_id=6, replica_groups=mesh['seq'=8,'tp'=4] {'seq'}, use_global_device_ids=true, to_apply=%region_18.19.clone | all-reduce | flops 4224 | bytes 33792
  1404.7 11.8 psum.31
  1417.1 71.4 %reduce-scatter.22.cloned.1.call-done = f32[768,512]{1,0:T(8,128)} async-done(((f32[768,2048]{1,0:T(8,128)}), f32[768,512]{1,0:T(8,128)}) %reduce-scatter.22.cloned.1.call-update) | async-done | bytes 1572880 | tf_op jit(solution)/shard_map/reduce_scatter | solution.py:102
  1492.4 92.8 %reduce-scatter.34.cloned.1.call-done = f32[256,1536]{1,0:T(8,128)} async-done(((f32[2048,1536]{1,0:T(8,128)}), f32[256,1536]{1,0:T(8,128)}) %reduce-scatter.34.cloned.1.call-update) | async-done | bytes 1572880 | tf_op jit(solution)/shard_map/reduce_scatter | solution.py:1161
  1585.2 96.5 %reduce-scatter.36.cloned.1.call-done = f32[256,1536]{1,0:T(8,128)} async-done(((f32[2048,1536]{1,0:T(8,128)}), f32[256,1536]{1,0:T(8,128)}) %reduce-scatter.36.cloned.1.call-update) | async-done | bytes 1572880 | tf_op jit(solution)/shard_map/reduce_scatter | solution.py:1162
  1681.7 96.4 %reduce-scatter.38.cloned.1.call-done = f32[1536,256]{1,0:T(8,128)} async-done(((f32[1536,2048]{1,0:T(8,128)}), f32[1536,256]{1,0:T(8,128)}) %reduce-scatter.38.cloned.1.call-update) | async-done | bytes 1572880 | tf_op jit(solution)/shard_map/reduce_scatter | solution.py:1163
  1778.1 60.6 %reduce-scatter.30.cloned.1.call-done = f32[256,640]{1,0:T(8,128)} async-done(((f32[2048,640]{1,0:T(8,128)}), f32[256,640]{1,0:T(8,128)}) %reduce-scatter.30.cloned.1.call-update) | async-done | bytes 655376 | tf_op jit(solution)/shard_map/reduce_scatter | solution.py:1151
  1838.7 60.8 %reduce-scatter.32.cloned.1.call-done = f32[640,256]{1,0:T(8,128)} async-done(((f32[640,2048]{1,0:T(8,128)}), f32[640,256]{1,0:T(8,128)}) %reduce-scatter.32.cloned.1.call-update) | async-done | bytes 655376 | tf_op jit(solution)/shard_map/reduce_scatter | solution.py:1159
  1899.4 60.4 %reduce-scatter.28.cloned.1.call-done = f32[256,640]{1,0:T(8,128)} async-done(((f32[2048,640]{1,0:T(8,128)}), f32[256,640]{1,0:T(8,128)}) %reduce-scatter.28.cloned.1.call-update) | async-done | bytes 655376 | tf_op jit(solution)/shard_map/reduce_scatter | solution.py:1150
  (625 shorter events, 337.2 us)
Async XLA Ops:
  7.2 308.5 %reduce-scatter.20.cloned.1.call-start = ((), (), s32[]{:S(2)}) async-start(), calls=%async_computation.13 | async-start | bytes 7864320 | tf_op jit(solution)/shard_map/reduce_scatter | solution.py:102
  99.4 13.3 copy-start.20
  99.7 100.1 %copy-start.43 = (f32[8,4,80]{2,0,1:T(8,128)}, f32[8,4,80]{2,0,1:T(8,128)S(1)}, u32[]{:S(2)}) copy-start(f32[8,4,80]{2,0,1:T(8,128)S(1)} %copy.152) | copy-start | bytes 30724
  99.8 99.9 %copy-start.47 = (f32[8,3,80]{2,1,0:T(4,128)}, f32[8,3,80]{2,1,0:T(4,128)S(1)}, u32[]{:S(2)}) copy-start(f32[8,3,80]{2,1,0:T(4,128)S(1)} %reshape.303) | copy-start | bytes 23044
  112.6 87.1 %copy-start.106 = (bf16[640,2048]{1,0:T(8,128)(2,1)S(1)}, bf16[640,2048]{1,0:T(8,128)(2,1)}, u32[]{:S(2)}) copy-start(bf16[640,2048]{1,0:T(8,128)(2,1)} %get-tuple-element.126) | copy-start | bytes 7864324
  205.4 110.3 %copy-start.4 = (bf16[768,512]{1,0:T(8,128)(2,1)S(1)}, bf16[768,512]{1,0:T(8,128)(2,1)}, u32[]{:S(2)}) copy-start(bf16[768,512]{1,0:T(8,128)(2,1)} %tok.1) | copy-start | bytes 2359300
  205.4 186.7 %all-gather.5.cloned.1.call-start = ((), (), s32[]{:S(2)}) async-start(), calls=%async_computation.14 | async-start | bytes 3932160 | tf_op jit(solution)/shard_map/all_gather | solution.py:94
  222.0 344.2 %copy-start.52 = (f32[512]{0:T(512)}, f32[512]{0:T(512)S(1)}, u32[]{:S(2)}) copy-start(f32[512]{0:T(512)S(1)} %convert_element_type.130) | copy-start | bytes 6148
  318.1 248.0 %copy-start = (f32[768,512]{1,0:T(8,128)}, f32[768,512]{1,0:T(8,128)S(1)}, u32[]{:S(2)}) copy-start(f32[768,512]{1,0:T(8,128)S(1)} %get-tuple-element.186) | copy-start | bytes 4718596
  329.0 237.1 %copy-start.45 = (f32[768]{0:T(1024)}, f32[768]{0:T(1024)S(1)}, u32[]{:S(2)}) copy-start(f32[768]{0:T(1024)S(1)} %add_rsqrt_fusion.1) | copy-start | bytes 9220
  330.2 221.9 %reduce-scatter.24.cloned.1.call-start = ((), (), s32[]{:S(2)}) async-start(), calls=%async_computation.16 | async-start | bytes 7864320 | tf_op jit(solution)/shard_map/reduce_scatter | solution.py:102
  392.2 10.5 copy-start.105
  392.2 20.2 %slice-start.7 = ((s8[6291456]{0:T(1024)(128)(4,1)}), s8[4194304]{0:T(1024)(128)(4,1)S(1)}, s32[]{:S(2)}) async-start(s8[6291456]{0:T(1024)(128)(4,1)} %bitcast.157), calls=%async_computation.35 | async-start | bytes 8388608
  402.7 9.6 slice-start.8
  402.7 9.6 copy-start.104
  402.7 22.6 %slice-start.9 = ((s8[6291456]{0:T(1024)(128)(4,1)}), s8[4194304]{0:T(1024)(128)(4,1)S(1)}, s32[]{:S(2)}) async-start(s8[6291456]{0:T(1024)(128)(4,1)} %bitcast.159), calls=%async_computation.37 | async-start | bytes 8388608
  412.4 12.9 slice-start.10
  442.5 275.3 %all-gather.7.cloned.1.call-start = ((), (), s32[]{:S(2)}) async-start(), calls=%async_computation.17 | async-start | bytes 3932160 | tf_op jit(solution)/shard_map/all_gather | solution.py:98
  443.9 580.6 %collective-permute-start.1 = (f32[3,640]{1,0:T(4,128)}, f32[3,640]{1,0:T(4,128)}, u32[]{:S(2)}, u32[]{:S(2)}) collective-permute-start(f32[3,640]{1,0:T(4,128)} %slice.719), channel_id=1, source_target_pairs={{0,4},{4,8},{8,12},{12,16},{16,20},{20,24},{24,28},{1,5},{5,9},{9,... | collective-permute-start | bytes 23048 | tf_op jit(solution)/shard_map/ppermute | solution.py:24
  448.4 123.3 %copy-start.66 = (pred[768]{0:T(1024)(128)(4,1)}, pred[768]{0:T(1024)(128)(4,1)S(1)}, u32[]{:S(2)}) copy-start(pred[768]{0:T(1024)(128)(4,1)S(1)} %get-tuple-element.255) | copy-start | bytes 2308
  451.2 103.3 %copy-start.78 = (f32[768]{0:T(1024)S(1)}, f32[768]{0:T(1024)}, u32[]{:S(2)}) copy-start(f32[768]{0:T(1024)} %get-tuple-element.202) | copy-start | bytes 9220
  451.2 115.0 %copy-start.15 = (bf16[768,512]{1,0:T(8,128)(2,1)S(1)}, bf16[768,512]{1,0:T(8,128)(2,1)}, u32[]{:S(2)}) copy-start(bf16[768,512]{1,0:T(8,128)(2,1)} %cot.1) | copy-start | bytes 2359300
  569.0 566.4 %reduce-scatter.40.cloned.1.call-start = ((), (), s32[]{:S(2)}) async-start(), calls=%async_computation.25 | async-start | bytes 368640
  594.9 26.1 %copy-start.24 = (f32[192,640]{1,0:T(8,128)}, f32[192,640]{1,0:T(8,128)S(1)}, u32[]{:S(2)}) copy-start(f32[192,640]{1,0:T(8,128)S(1)} %mul.629) | copy-start | bytes 1474564
  607.1 18.8 copy-start.37
  609.1 16.8 copy-start.38
  632.7 10.8 copy-start.21
  693.5 16.8 copy-start.26
  840.5 16.0 copy-start.56
  840.5 16.0 copy-start.57
  840.5 16.0 copy-start.58
  840.5 16.0 copy-start.59
  840.5 16.2 copy-start.68
  840.5 16.2 copy-start.69
  840.6 16.2 copy-start.87
  840.6 16.2 copy-start.88
  843.9 13.0 copy-start.49
  843.9 13.0 copy-start.50
  843.9 13.0 copy-start.90
  843.9 13.1 copy-start.89
  843.9 13.2 copy-start.41
  847.2 9.9 copy-start.92
  847.2 10.0 copy-start.91
  871.5 9.0 copy-start.83
  983.5 15.9 copy-start.67
  983.5 15.9 copy-start.82
  1034.3 128.4 %reduce-scatter.44.cloned.1.call-start = ((), (), s32[]{:S(2)}) async-start(), calls=%async_computation.27 | async-start | bytes 14745600
  1043.2 218.3 %reduce-scatter.42.cloned.1.call-start = ((), (), s32[]{:S(2)}) async-start(), calls=%async_computation.26 | async-start | bytes 14745600
  1044.9 9.0 collective-permute-start
  1053.9 320.7 %reduce-scatter.26.cloned.1.call-start = ((), (), s32[]{:S(2)}) async-start(), calls=%async_computation.18 | async-start | bytes 7864320 | tf_op jit(solution)/shard_map/reduce_scatter | solution.py:102
  1065.7 422.8 %reduce-scatter.22.cloned.1.call-start = ((), (), s32[]{:S(2)}) async-start(), calls=%async_computation.15 | async-start | bytes 7864320 | tf_op jit(solution)/shard_map/reduce_scatter | solution.py:102
  1077.3 507.9 %reduce-scatter.34.cloned.1.call-start = ((), (), s32[]{:S(2)}) async-start(), calls=%async_computation.22 | async-start | bytes 14155776 | tf_op jit(solution)/shard_map/reduce_scatter | solution.py:1161
  1088.9 592.8 %reduce-scatter.36.cloned.1.call-start = ((), (), s32[]{:S(2)}) async-start(), calls=%async_computation.23 | async-start | bytes 14155776 | tf_op jit(solution)/shard_map/reduce_scatter | solution.py:1162
  1099.2 678.8 %reduce-scatter.38.cloned.1.call-start = ((), (), s32[]{:S(2)}) async-start(), calls=%async_computation.24 | async-start | bytes 14155776 | tf_op jit(solution)/shard_map/reduce_scatter | solution.py:1163
  1109.4 729.3 %reduce-scatter.30.cloned.1.call-start = ((), (), s32[]{:S(2)}) async-start(), calls=%async_computation.20 | async-start | bytes 5898240 | tf_op jit(solution)/shard_map/reduce_scatter | solution.py:1151
  1116.6 782.9 %reduce-scatter.32.cloned.1.call-start = ((), (), s32[]{:S(2)}) async-start(), calls=%async_computation.21 | async-start | bytes 5898240 | tf_op jit(solution)/shard_map/reduce_scatter | solution.py:1159
  1124.5 835.3 %reduce-scatter.28.cloned.1.call-start = ((), (), s32[]{:S(2)}) async-start(), calls=%async_computation.19 | async-start | bytes 5898240 | tf_op jit(solution)/shard_map/reduce_scatter | solution.py:1150
  1132.7 241.9 %copy-start.5 = (bf16[768,512]{1,0:T(8,128)(2,1)S(1)}, bf16[768,512]{1,0:T(8,128)(2,1)}, u32[]{:S(2)}) copy-start(bf16[768,512]{1,0:T(8,128)(2,1)} %tok.1) | copy-start | bytes 2359300
  1261.5 115.2 %copy-start.93 = (f32[512]{0:T(512)S(1)}, f32[512]{0:T(512)}, u32[]{:S(2)}) copy-start(f32[512]{0:T(512)} %get-tuple-element.142) | copy-start | bytes 6148
  1261.5 227.0 %copy-start.1 = (f32[768,512]{1,0:T(8,128)S(1)}, f32[768,512]{1,0:T(8,128)}, u32[]{:S(2)}) copy-start(f32[768,512]{1,0:T(8,128)} %copy-done) | copy-start | bytes 4718596
  1261.5 227.0 %copy-start.16 = (bf16[768,512]{1,0:T(8,128)(2,1)S(1)}, bf16[768,512]{1,0:T(8,128)(2,1)}, u32[]{:S(2)}) copy-start(bf16[768,512]{1,0:T(8,128)(2,1)} %cot.1) | copy-start | bytes 2359300
  1261.5 227.0 %copy-start.46 = (f32[768]{0:T(1024)S(1)}, f32[768]{0:T(1024)}, u32[]{:S(2)}) copy-start(f32[768]{0:T(1024)} %copy-done.45) | copy-start | bytes 9220
  1261.5 227.0 %copy-start.53 = (f32[512]{0:T(512)S(1)}, f32[512]{0:T(512)}, u32[]{:S(2)}) copy-start(f32[512]{0:T(512)} %copy-done.52) | copy-start | bytes 6148
  1261.5 227.0 %copy-start.61 = (f32[768]{0:T(1024)S(1)}, f32[768]{0:T(1024)}, u32[]{:S(2)}) copy-start(f32[768]{0:T(1024)} %copy-done.60) | copy-start | bytes 9220
  (74 other events, 243.0 us)
Sparse Core Ops, SparseCore 0:
  205.6 110.1 reduce-scatter.19
  330.3 61.8 all-gather.4
  442.6 109.4 reduce-scatter.23
  569.1 61.8 all-gather.6
  1034.4 29.6 reduce-scatter.39
  1067.5 95.1 reduce-scatter.43
  1166.3 95.1 reduce-scatter.41
  1263.8 110.7 reduce-scatter.25
  1376.9 111.5 reduce-scatter.21
  1492.4 92.8 reduce-scatter.33
  1589.3 92.3 reduce-scatter.35
  1685.7 92.3 reduce-scatter.37
  1782.0 56.5 reduce-scatter.29
  1842.9 56.5 reduce-scatter.31
  1903.2 56.5 reduce-scatter.27

commit v2 on v1

--- a/solution.py
+++ b/solution.py
@@ -759,7 +759,7 @@
 
 def recur_kernel(
     tok_all, scan_w, gate_w, gates_w, par, gain, masks, cot, up, down,
-    normed, scan_rows, gate_rows, conv, decay_rows, input_rows, hidden, mixed, state, decay_sum,
+    normed, scan_rows, gate_rows, conv, decay_rows, input_rows, hidden, mixed, scales, decay_sum,
     cot_all, up_all, down_all,
     kept, driven, slots,
     line_send, line_recv, plane_send, plane_recv, small_send, small_recv, halo_send, halo_recv, local,
@@ -794,6 +794,7 @@
         at = chunk_rows(c)
         x = tok_all[at, :].astype(F32)
         scale = lax.rsqrt(jnp.sum(x * x, axis=1, keepdims=True) / features + EPSILON)
+        scales[at, :] = jnp.broadcast_to(scale, (CHUNK, LANE))
         low = (x * scale * gain[0:1, :]).astype(BF16)
         normed[at, :] = low
         scan_rows[pl.ds(pl.multiple_of(c * CHUNK + 8, 8), CHUNK), :] = dot(low, scan_w[...])
@@ -874,7 +875,7 @@
         entry = jnp.where(
             place < s, slots[place, 0:1, :] * entry + slots[place, 1:2, :], entry
         )
-    state[...] = jnp.broadcast_to(entry, (8, lanes))
+    hidden[0:8, :] = jnp.broadcast_to(entry, (8, lanes))
     entries = []
     for sub in range(SUBS):
         entries.append(entry)
@@ -891,7 +892,7 @@
     def mix(c):
         at = chunk_rows(c)
         now = get(driven, at)
-        hidden[at, :] = now
+        hidden[pl.ds(pl.multiple_of(c * CHUNK + 8, 8), CHUNK), :] = now
         mixed[at, :] = (gelu_of(gate_rows[at, :]) * now).astype(BF16)
         line.forward(2, c)
 
@@ -922,9 +923,9 @@
             struct((rows, lanes), BF16),
             struct((rows, lanes), F32),
             struct((rows, lanes), F32),
-            struct((rows, lanes), F32),
+            struct((rows + 8, lanes), F32),
             struct((rows, lanes), BF16),
-            struct((8, lanes), F32),
+            struct((rows, LANE), F32),
             struct((8, lanes), F32),
             struct((rows, features), BF16),
             struct((up.shape[0] * PLANE, up.shape[1]), BF16),
@@ -947,6 +948,885 @@
     )(tok_all, scan_w, gate_w, gates_w, par, gain, masks, cot, up, down)
 
 
+class LineReduce:
+    def __init__(self, s, z, part, land, send, recv):
+        self.s, self.z, self.part, self.land = s, z, part, land
+        self.send, self.recv = send, recv
+
+    def copy(self, way, me, o, c):
+        target = me + 1 - 2 * way
+        slot = LINE if way == 1 and o == target else o
+        return remote(
+            self.part.at[c, o],
+            self.land.at[c, slot],
+            self.send.at[o, c],
+            self.recv.at[slot, c],
+            (self.s, self.z + 1 - 2 * way),
+        )
+
+    def got(self, slot, c):
+        part = self.land.at[c, slot]
+        remote(part, part, self.send.at[0, c], self.recv.at[slot, c], (self.s, self.z)).wait_recv()
+
+    def hop(self, level, c):
+        for way in range(2):
+            me = level if way == 0 else LINE - 1 - level
+            order = range(LINE - 1, me - 1, -1) if way == 0 else range(me + 1)
+
+            def work(way=way, me=me, order=order):
+                for o in order:
+                    slot = LINE if way == 1 and o == me else o
+                    if level > 0:
+                        self.got(slot, c)
+                    if o != me:
+                        if level > 0:
+                            self.part[c, o] = (
+                                self.part[c, o].astype(F32) + self.land[c, slot].astype(F32)
+                            ).astype(BF16)
+                        self.copy(way, me, o, c).start()
+
+            pl.when(self.z == me)(work)
+
+    def landed(self, c, into):
+        @pl.when(self.z == 0)
+        def _():
+            into[...] = self.land[c, LINE].astype(F32)
+
+        @pl.when(self.z > 0)
+        def _():
+            into[...] = self.land[c, self.z].astype(F32)
+
+        @pl.when((self.z > 0) & (self.z < LINE - 1))
+        def _():
+            into[...] += self.land[c, LINE].astype(F32)
+
+    def drain(self, c):
+        for o in range(LINE):
+            part = self.part.at[c, o]
+            pl.when(self.z != o)(
+                lambda part=part, o=o: remote(
+                    part, part, self.send.at[o, c], self.recv.at[0, c], (self.s, self.z)
+                ).wait_send()
+            )
+
+
+class LineSpread:
+    def __init__(self, s, z, slot_at, send, recv):
+        self.s, self.z, self.slot_at, self.send, self.recv = s, z, slot_at, send, recv
+
+    def copy(self, step, origin, c):
+        slot = self.slot_at(origin, c)
+        target = (self.s, lax.rem(self.z + step, LINE))
+        return remote(slot, slot, self.send.at[step - 1, c], self.recv.at[step - 1, c], target)
+
+    def start(self, c):
+        for step in range(1, LINE):
+            self.copy(step, self.z, c).start()
+
+    def finish(self, c):
+        for step in range(1, LINE):
+            self.copy(step, lax.rem(self.z + LINE - step, LINE), c).wait_recv()
+
+    def drain(self, c):
+        for step in range(1, LINE):
+            self.copy(step, self.z, c).wait_send()
+
+
+class Halves:
+    def __init__(self, s, z, src, out, own, send, recv):
+        self.s, self.z, self.src, self.out = s, z, src, out
+        self.own, self.send, self.recv = own, send, recv
+
+    def keep(self, c):
+        at = chunk_rows(c)
+        return pltpu.make_async_copy(self.src.at[at], self.out.at[0, at], self.own.at[c])
+
+    def give(self, c):
+        at = chunk_rows(c)
+        return remote(
+            self.src.at[at], self.out.at[1, at], self.send.at[c], self.recv.at[c],
+            (flip(self.s, 0), self.z),
+        )
+
+    def start(self, c):
+        self.keep(c).start()
+        self.give(c).start()
+
+    def drain(self, c):
+        self.keep(c).wait()
+        self.give(c).wait()
+
+
+def as_row(column):
+    return jnp.transpose(jnp.broadcast_to(column, (CHUNK, LANE)))[0:8, :]
+
+
+def as_columns(row):
+    return jnp.transpose(jnp.broadcast_to(row[0:1, :], (LANE, CHUNK)))
+
+
+def in_range(c, chunks, body):
+    pl.when((c >= 0) & (c < chunks))(lambda: body(c))
+
+
+CUT = 768
+AHEAD = 2
+GROUP = 2 * CHUNK
+
+
+def group_rows(g):
+    return pl.ds(pl.multiple_of(g * GROUP, GROUP), GROUP)
+
+
+def feed_kernel(
+    mixed, mix_w, tok, gain, gate_w, up_w, down_w, cot,
+    resid, scales, coefs, bo_part, gs_part, low_pair, cot_pair, mid_pair, gate_pair, up_pair,
+    part, land, low, cots, mid, g_gate, g_up, bo_out, gs_out, gate_v, up_v, down_v,
+    acc, bo_acc, gs_acc, inner, squares, inners,
+    red_send, red_recv, line_send, line_recv, sq_send, sq_recv, in_send, in_recv,
+    own_sem, give_send, give_recv, out_sem, load_sem,
+):
+    s, z = lax.axis_index("seq"), lax.axis_index("tp")
+    rows, width = tok.shape
+    chunks, features = rows // CHUNK, width * LINE
+    loads = [
+        pltpu.make_async_copy(src, dst, load_sem.at[i])
+        for i, (src, dst) in enumerate(
+            ((gate_w, gate_v), (up_w, up_v), (down_w, down_v), (cot, cots))
+        )
+    ]
+    for load in loads:
+        load.start()
+    meet(s, z)
+    red = LineReduce(s, z, part, land, red_send, red_recv)
+    line = LineGather(
+        s, z,
+        lambda c: low.at[chunk_rows(c), feature_columns(z, width)],
+        lambda o, c: low.at[chunk_rows(c), feature_columns(o, width)],
+        line_send, line_recv,
+    )
+    square_spread = LineSpread(s, z, lambda o, c: squares.at[o, c], sq_send, sq_recv)
+    inner_spread = LineSpread(s, z, lambda o, c: inners.at[o, c], in_send, in_recv)
+    pairs = [
+        Halves(s, z, src, out, own_sem.at[i], give_send.at[i], give_recv.at[i])
+        for i, (src, out) in enumerate(
+            ((low, low_pair), (cots, cot_pair), (mid, mid_pair), (g_gate, gate_pair), (g_up, up_pair))
+        )
+    ]
+
+    def outs(c):
+        return [
+            pltpu.make_async_copy(bo_out.at[c], bo_part.at[c], out_sem.at[0, c]),
+            pltpu.make_async_copy(gs_out.at[c], gs_part.at[c], out_sem.at[1, c]),
+        ]
+
+    def project(c):
+        values = dot(mixed[chunk_rows(c), :], mix_w[...])
+        for o in range(LINE):
+            here = values[:, o * width : (o + 1) * width]
+            part[c, o] = here.astype(BF16)
+
+            @pl.when(z == o)
+            def _(here=here):
+                resid[chunk_rows(c), :] = here
+
+        red.hop(0, c)
+
+    for c in range(AHEAD):
+        project(c)
+
+    def reduced(c):
+        at = chunk_rows(c)
+        red.hop(3, c)
+        red.landed(c, acc)
+        values = tok[at, :].astype(F32) + (resid[at, :] + acc[...])
+        resid[at, :] = values
+        squares[z, c] = as_row(jnp.sum(values * values, axis=1, keepdims=True))
+        square_spread.start(c)
+
+    def scaled(c):
+        at = chunk_rows(c)
+        square_spread.finish(c)
+        sums = squares[0, c] + squares[1, c] + squares[2, c] + squares[3, c]
+        scale = lax.rsqrt(as_columns(sums) / features + EPSILON)
+        scales[at, :] = scale
+        low[at, feature_columns(z, width)] = (resid[at, :] * scale[:, 0:1] * gain[0:1, :]).astype(
+            BF16
+        )
+        line.start(c)
+
+    def forward(cut, g):
+        at = group_rows(g)
+        cols = slice(cut * CUT, (cut + 1) * CUT)
+        x = low[at, :]
+        gate_pre, up_pre = dot(x, gate_v[:, cols]), dot(x, up_v[:, cols])
+        act, slope = gelu_pair(gate_pre)
+        here = (act * up_pre).astype(BF16)
+        mid[at, cols] = here
+        grad = dot_nt(cots[at, :], down_v[cols, :])
+        gate_grad = (grad * up_pre * slope).astype(BF16)
+        up_grad = (grad * act).astype(BF16)
+        g_gate[at, cols] = gate_grad
+        g_up[at, cols] = up_grad
+        products = jnp.sum(
+            gate_grad.astype(F32) * gate_pre + up_grad.astype(F32) * up_pre, axis=1, keepdims=True
+        )
+        if cut == 0:
+            inner[...] = products
+        else:
+            inner[...] += products
+
+    def backward(cut, g):
+        at = group_rows(g)
+        cols = slice(cut * CUT, (cut + 1) * CUT)
+        block = dot(mid[at, cols], down_v[cols, :])
+        back = dot_nt(g_gate[at, cols], gate_v[:, cols]) + dot_nt(g_up[at, cols], up_v[:, cols])
+        if cut == 0:
+            bo_acc[...] = block
+            gs_acc[...] = back
+            return
+        block = bo_acc[...] + block
+        back = gs_acc[...] + back
+        for k in range(GROUP // CHUNK):
+            c = g * (GROUP // CHUNK) + k
+            here = slice(k * CHUNK, (k + 1) * CHUNK)
+            for o in range(LINE):
+                bo_out[c, o] = block[here, o * width : (o + 1) * width].astype(BF16)
+                gs_out[c, o] = back[here, o * width : (o + 1) * width].astype(BF16)
+            inners[z, c] = as_row(inner[here, :])
+            inner_spread.start(c)
+            for pair in pairs:
+                pair.start(c)
+            for copy in outs(c):
+                copy.start()
+
+    def turn(t, carry):
+        g, odd = (t - 4) // 2, lax.rem(t, 2) == 1
+        ready = t >= 4
+        pl.when(t == 3)(lambda: [load.wait() for load in loads] and None)
+        in_range(t, chunks, lambda c: red.hop(1, c))
+        in_range(t - 2, chunks, lambda c: line.forward(1, c))
+        in_range(t - 3, chunks, lambda c: line.forward(3, c))
+        pl.when(ready & jnp.logical_not(odd))(lambda: forward(0, g))
+        pl.when(ready & odd)(lambda: forward(1, g))
+        in_range(t - 1, chunks, reduced)
+        in_range(t - 1, chunks, scaled)
+        in_range(t - 2, chunks, lambda c: line.forward(2, c))
+        pl.when(ready & jnp.logical_not(odd))(lambda: backward(0, g))
+        in_range(t, chunks, lambda c: red.hop(2, c))
+        in_range(t + AHEAD, chunks, project)
+        pl.when(ready & odd)(lambda: backward(1, g))
+        return carry
+
+    lax.fori_loop(0, chunks + 4, turn, 0)
+
+    def close(c):
+        at = chunk_rows(c)
+        inner_spread.finish(c)
+        sums = inners[0, c] + inners[1, c] + inners[2, c] + inners[3, c]
+        scale = scales[at, :]
+        coefs[at, :] = scale * scale * as_columns(sums) / features
+        red.drain(c)
+        line.drain(c)
+        square_spread.drain(c)
+        inner_spread.drain(c)
+        for pair in pairs:
+            pair.drain(c)
+        for copy in outs(c):
+            copy.wait()
+
+    each_chunk(chunks, close)
+
+
+def vm(*shape, kind=BF16):
+    return pltpu.VMEM(shape, kind)
+
+
+def feed_forward(mixed, mix_w, tok, gain, gate_w, up_w, down_w, cot):
+    rows, width = tok.shape
+    features, hidden = width * LINE, gate_w.shape[1]
+    chunks = rows // CHUNK
+    blocks = struct((chunks, LINE, CHUNK, width), BF16)
+
+    def pair(size):
+        return struct((2, rows, size), BF16)
+
+    return pl.pallas_call(
+        feed_kernel,
+        out_shape=(
+            struct((rows, width), F32),
+            struct((rows, LANE), F32),
+            struct((rows, LANE), F32),
+            blocks, blocks,
+            pair(features), pair(features), pair(hidden), pair(hidden), pair(hidden),
+        ),
+        in_specs=[VM] * 4 + [ANY] * 4,
+        out_specs=[VM] * 3 + [ANY] * 7,
+        scratch_shapes=[
+            vm(chunks, LINE, CHUNK, width), vm(chunks, LINE + 1, CHUNK, width),
+            vm(rows, features), vm(rows, features),
+            vm(rows, hidden), vm(rows, hidden), vm(rows, hidden),
+            vm(chunks, LINE, CHUNK, width), vm(chunks, LINE, CHUNK, width),
+            vm(features, hidden), vm(features, hidden), vm(hidden, features),
+            vm(CHUNK, width, kind=F32), vm(GROUP, features, kind=F32),
+            vm(GROUP, features, kind=F32), vm(GROUP, 1, kind=F32),
+            vm(LINE, chunks, 8, LANE, kind=F32), vm(LINE, chunks, 8, LANE, kind=F32),
+            dma(LINE, chunks), dma(LINE + 1, chunks),
+            dma(2, LINE - 1, chunks), dma(2, LINE - 1, chunks),
+            dma(LINE - 1, chunks), dma(LINE - 1, chunks),
+            dma(LINE - 1, chunks), dma(LINE - 1, chunks),
+            dma(5, chunks), dma(5, chunks), dma(5, chunks), dma(2, chunks), dma(4),
+        ],
+        compiler_params=pltpu.CompilerParams(
+            collective_id=2, has_side_effects=True, vmem_limit_bytes=63 << 20
+        ),
+        name="feed_forward",
+    )(mixed, mix_w, tok, gain, gate_w, up_w, down_w, cot)
+
+
+class WeightGrads:
+    def __init__(self, s, z, stage, land, own, send, recv, back):
+        self.s, self.z = s, z
+        self.stage, self.land, self.own = stage, land, own
+        self.send, self.recv, self.back_sem = send, recv, back
+
+    def owner(self, k):
+        return flip_all(self.s, 2 * (k + 1)) if k < 3 else self.s
+
+    def copy(self, k):
+        return remote(
+            self.stage.at[k], self.land.at[k], self.send.at[k], self.recv.at[k],
+            (self.owner(k), self.z),
+        )
+
+    def block(self, k, left, right):
+        size = self.own.shape[0]
+        columns = feature_columns(self.owner(k), size)
+        value = dot_tn(left[:, columns], right[...])
+        if k == 3:
+            self.own[...] = value
+        else:
+            self.stage[k] = value.astype(BF16)
+            self.copy(k).start()
+
+    def finish(self):
+        backs = [
+            pltpu.make_async_copy(self.land.at[k], self.stage.at[k], self.back_sem.at[k])
+            for k in range(3)
+        ]
+        for k in range(3):
+            self.copy(k).wait()
+            backs[k].start()
+        for back in backs:
+            back.wait()
+        self.own[...] += (
+            self.stage[0].astype(F32) + self.stage[1].astype(F32) + self.stage[2].astype(F32)
+        )
+
+
+def back_kernel(
+    resid, scales, coefs, cot, gain, gs_part, bo_part, low_pair, cot_pair, mid_pair, gate_pair, up_pair,
+    grad, grad_all, out, gain_grad, gate_own, up_own, down_own, lands,
+    part, land, part_bo, land_bo, low, acc, left, right, stages,
+    red_send, red_recv, bo_send, bo_recv, line_send, line_recv, w_send, w_recv, w_back, load_sem, out_sem,
+):
+    s, z = lax.axis_index("seq"), lax.axis_index("tp")
+    rows, width = cot.shape
+    chunks = rows // CHUNK
+    loads = [
+        pltpu.make_async_copy(src, dst, load_sem.at[i])
+        for i, (src, dst) in enumerate(
+            (
+                (gs_part, part), (bo_part, part_bo),
+                (cot_pair, left.at[0]), (mid_pair, right.at[0]),
+                (low_pair, left.at[1]), (gate_pair, right.at[1]),
+            )
+        )
+    ]
+    late = pltpu.make_async_copy(up_pair, right.at[0], load_sem.at[6])
+    for load in loads:
+        load.start()
+    meet(s, z)
+    red = LineReduce(s, z, part, land, red_send, red_recv)
+    red_bo = LineReduce(s, z, part_bo, land_bo, bo_send, bo_recv)
+    line = LineGather(
+        s, z,
+        lambda c: low.at[chunk_rows(c), feature_columns(z, width)],
+        lambda o, c: low.at[chunk_rows(c), feature_columns(o, width)],
+        line_send, line_recv,
+    )
+    weights = [
+        WeightGrads(s, z, stages.at[i], lands.at[i], own, w_send.at[i], w_recv.at[i], w_back.at[i])
+        for i, own in enumerate((down_own, gate_own, up_own))
+    ]
+    gain_grad[...] = jnp.zeros_like(gain_grad)
+    loads[0].wait()
+    for c in range(AHEAD):
+        red.hop(0, c)
+    for load in loads[1:]:
+        load.wait()
+
+    def reduced(c):
+        at = chunk_rows(c)
+        red.hop(3, c)
+        red.landed(c, acc)
+        up = acc[...] + part[c, z].astype(F32)
+        scale, values = scales[at, 0:1], resid[at, :]
+        gain_grad[0:1, :] += jnp.sum(up * values * scale, axis=0, keepdims=True)
+        total = cot[at, :].astype(F32) + scale * gain[0:1, :] * up - values * coefs[at, 0:1]
+        grad[at, :] = total
+        low[at, feature_columns(z, width)] = total.astype(BF16)
+        line.start(c)
+
+    def result(c):
+        at = chunk_rows(c)
+        red_bo.hop(3, c)
+        red_bo.landed(c, acc)
+        out[at, :] = resid[at, :] + (acc[...] + part_bo[c, z].astype(F32))
+
+    def keep(c):
+        at = chunk_rows(c)
+        return pltpu.make_async_copy(low.at[at], grad_all.at[at], out_sem.at[c])
+
+    def arrived(c):
+        line.forward(3, c)
+        keep(c).start()
+
+    def weigh(t):
+        for k in range(4):
+            pl.when(t == k)(lambda k=k: weights[0].block(k, left.at[0], right.at[0]))
+            pl.when(t == 4 + k)(lambda k=k: weights[1].block(k, left.at[1], right.at[1]))
+            pl.when(t == 8 + k)(lambda k=k: weights[2].block(k, left.at[1], right.at[0]))
+        pl.when(t == 4)(lambda: late.start())
+        pl.when(t == 7)(lambda: late.wait())
+
+    def turn(t, carry):
+        in_range(t, chunks, lambda c: red.hop(1, c))
+        in_range(t - 2, chunks, lambda c: line.forward(1, c))
+        in_range(t - 3, chunks, arrived)
+        in_range(t - 5, chunks, lambda c: red_bo.hop(1, c))
+        weigh(t)
+        in_range(t - 1, chunks, reduced)
+        in_range(t - 2, chunks, lambda c: line.forward(2, c))
+        in_range(t - 6, chunks, result)
+        in_range(t, chunks, lambda c: red.hop(2, c))
+        in_range(t - 5, chunks, lambda c: red_bo.hop(2, c))
+        in_range(t + AHEAD, chunks, lambda c: red.hop(0, c))
+        in_range(t - 3, chunks, lambda c: red_bo.hop(0, c))
+        return carry
+
+    lax.fori_loop(0, chunks + 7, turn, 0)
+    for weight in weights:
+        weight.finish()
+
+    def close(c):
+        red.drain(c)
+        red_bo.drain(c)
+        line.drain(c)
+        keep(c).wait()
+
+    each_chunk(chunks, close)
+
+
+def back_feed(resid, scales, coefs, cot, gain, gs_part, bo_part, pairs):
+    rows, width = cot.shape
+    features, hidden = width * LINE, pairs[2].shape[2]
+    chunks, part = rows // CHUNK, features // PLANE
+    blocks = vm(chunks, LINE, CHUNK, width)
+    landing = vm(chunks, LINE + 1, CHUNK, width)
+    return pl.pallas_call(
+        back_kernel,
+        out_shape=(
+            struct((rows, width), F32),
+            struct((rows, features), BF16),
+            struct((rows, width), F32),
+            struct((8, width), F32),
+            struct((part, hidden), F32),
+            struct((part, hidden), F32),
+            struct((part, hidden), F32),
+            struct((3, 3, part, hidden), BF16),
+        ),
+        in_specs=[VM] * 5 + [ANY] * 7,
+        out_specs=[VM, ANY] + [VM] * 5 + [ANY],
+        scratch_shapes=[
+            blocks, landing, blocks, landing,
+            vm(rows, features), vm(CHUNK, width, kind=F32),
+            vm(2, 2 * rows, features), vm(2, 2 * rows, hidden), vm(3, 3, part, hidden),
+            dma(LINE, chunks), dma(LINE + 1, chunks), dma(LINE, chunks), dma(LINE + 1, chunks),
+            dma(2, LINE - 1, chunks), dma(2, LINE - 1, chunks),
+            dma(3, 3), dma(3, 3), dma(3, 3), dma(7), dma(chunks),
+        ],
+        compiler_params=pltpu.CompilerParams(
+            collective_id=3, has_side_effects=True, vmem_limit_bytes=63 << 20
+        ),
+        name="back_feed",
+    )(
+        resid, scales, coefs, cot, gain, gs_part, bo_part,
+        *[pair.reshape(2 * rows, pair.shape[2]) for pair in pairs],
+    )
+
+
+def recur_back_kernel(
+    low, mix_w, gate_rows, hidden, conv, decay_rows, input_rows, scan_rows, masks, par, gates_w, scales,
+    normed_src, mixed_src, low_src,
+    gates_grad, sums, coefs, normed_pair, mixed_pair, low_pair, scan_pair, gate_pair,
+    kept, grads, spilled, both, conv_grad, scan_low, gate_low, slots, inners,
+    small_send, small_recv, halo_send, halo_recv, in_send, in_recv,
+    own_sem, give_send, give_recv, keep_sem, twin_send, twin_recv,
+):
+    s, z = lax.axis_index("seq"), lax.axis_index("tp")
+    rows, features = low.shape
+    lanes = gate_rows.shape[1]
+    chunks = rows // CHUNK
+    wholes = []
+    for i, (src, out) in enumerate(
+        ((normed_src, normed_pair), (mixed_src, mixed_pair), (low_src, low_pair))
+    ):
+        wholes.append(pltpu.make_async_copy(src, out.at[0], keep_sem.at[i]))
+        wholes.append(
+            remote(src, out.at[1], twin_send.at[i], twin_recv.at[i], (flip(s, 0), z))
+        )
+    pairs = [
+        Halves(s, z, src, out, own_sem.at[i], give_send.at[i], give_recv.at[i])
+        for i, (src, out) in enumerate(((scan_low, scan_pair), (gate_low, gate_pair)))
+    ]
+    inner_spread = LineSpread(s, z, lambda o, c: inners.at[o, c], in_send, in_recv)
+    meet(s, z)
+    for whole in wholes:
+        whole.start()
+    sums[...] = jnp.zeros_like(sums)
+
+    def start(g):
+        at = group_rows(g)
+        grad = dot_nt(low[at, :], mix_w[...])
+        for k in range(GROUP // CHUNK):
+            c = g * (GROUP // CHUNK) + k
+            here = chunk_rows(c)
+            act, slope = gelu_pair(gate_rows[here, :])
+            now = hidden[pl.ds(pl.multiple_of(c * CHUNK + 8, 8), CHUNK), :]
+            part = grad[k * CHUNK : (k + 1) * CHUNK, :]
+            gate_low[here, :] = (part * now * slope).astype(BF16)
+            put(grads, here, part * act)
+            decay = jnp.exp(-sigmoid(decay_rows[here, :]) * par[7:8, :])
+            put(kept, here, masks[here, 0:1] * decay)
+
+    lax.fori_loop(0, rows // GROUP, lambda g, carry: (start(g), carry)[1], 0)
+    for c in range(chunks):
+        pairs[1].start(c)
+    count, groups = rows // SUBS, lanes // LANE
+
+    def total_of(step, carry):
+        keeps, adds = strided(kept, count - 1 - step), strided(grads, count - 1 - step)
+        return (
+            [p * k for p, k in zip(carry[0], keeps)],
+            [k * (v + a) for k, v, a in zip(keeps, carry[1], adds)],
+        )
+
+    product, value = lax.fori_loop(
+        0,
+        count,
+        total_of,
+        ([jnp.ones((SUBS, LANE), F32)] * groups, [jnp.zeros((SUBS, LANE), F32)] * groups),
+        unroll=4,
+    )
+    product, value = jnp.concatenate(product, axis=1), jnp.concatenate(value, axis=1)
+    whole = (jnp.ones((1, lanes), F32), jnp.zeros((1, lanes), F32))
+    for sub in range(SUBS - 1, -1, -1):
+        here = product[sub : sub + 1, :]
+        whole = (whole[0] * here, here * whole[1] + value[sub : sub + 1, :])
+    slots[s, 0:1, :] = whole[0]
+    slots[s, 1:2, :] = whole[1]
+    spread = Spread(s, z, lambda p: slots.at[p], small_send, small_recv)
+    spread.start()
+    spread.finish()
+    entry = jnp.zeros((1, lanes), F32)
+    for place in range(PLANE - 1, 0, -1):
+        entry = jnp.where(
+            place > s, slots[place, 0:1, :] * entry + slots[place, 1:2, :], entry
+        )
+    entries = []
+    for sub in range(SUBS - 1, -1, -1):
+        entries.append(entry)
+        entry = product[sub : sub + 1, :] * entry + value[sub : sub + 1, :]
+
+    def step_back(step, now):
+        keeps, adds = strided(kept, count - 1 - step), strided(grads, count - 1 - step)
+        now = [v + a for v, a in zip(now, adds)]
+        strided_put(grads, count - 1 - step, now)
+        return [k * v for k, v in zip(keeps, now)]
+
+    lax.fori_loop(
+        0, count, step_back, lanes_of(jnp.concatenate(entries[::-1], axis=0)), unroll=4
+    )
+
+    def gates(c):
+        at = chunk_rows(c)
+        tall = pl.ds(pl.multiple_of(c * CHUNK, 8), CHUNK + 8)
+        adjoint = get(grads, at)
+        before = hidden[tall, :][7 : 7 + CHUNK, :]
+        mask = masks[at, :]
+        goes_on = mask[:, 0:1]
+        opened = sigmoid(decay_rows[at, :])
+        entered = sigmoid(input_rows[at, :])
+        rate = par[7:8, :]
+        decay = jnp.exp(-opened * rate)
+        room = 1.0 - decay * decay
+        root = jnp.sqrt(jnp.maximum(room, FLOOR_VALUE))
+        multiplier = 1.0 + goes_on * (root - 1.0)
+        conv_f = conv[at, :].astype(F32)
+        direct = adjoint * multiplier
+        grad_input = (direct * conv_f * (entered * (1.0 - entered))).astype(BF16)
+        through = jnp.where(
+            room > FLOOR_VALUE, 1.0, jnp.where(room == FLOOR_VALUE, 0.5, 0.0)
+        )
+        grad_decay = goes_on * (
+            adjoint * before - adjoint * entered * conv_f * (through * decay / root)
+        )
+        scaled = grad_decay * decay * opened
+        grad_rows = (-scaled * rate * (1.0 - opened)).astype(BF16)
+        joined = jnp.concatenate([grad_rows, grad_input], axis=1)
+        both[at, :] = joined
+        grad_conv = direct * entered + dot_nt(joined, gates_w[...])
+        conv_grad[at, :] = grad_conv
+        block = scan_rows[tall, :]
+        sums[0:1, :] += jnp.sum(grad_conv * block[8:, :], axis=0, keepdims=True)
+        for lag in range(1, KW):
+            sums[lag : lag + 1, :] += jnp.sum(
+                mask[:, lag : lag + 1] * (grad_conv * block[8 - lag : 8 - lag + CHUNK, :]),
+                axis=0,
+                keepdims=True,
+            )
+        sums[4:5, :] += jnp.sum(grad_conv, axis=0, keepdims=True)
+        sums[5:6, :] += jnp.sum(grad_rows.astype(F32), axis=0, keepdims=True)
+        sums[6:7, :] += jnp.sum(grad_input.astype(F32), axis=0, keepdims=True)
+        sums[7:8, :] += jnp.sum(scaled, axis=0, keepdims=True)
+
+    each_chunk(chunks, gates)
+    halo = remote(
+        conv_grad.at[pl.ds(0, 8)], conv_grad.at[pl.ds(rows, 8)], halo_send, halo_recv,
+        (lax.rem(s + PLANE - 1, PLANE), z),
+    )
+    first, final = s == 0, s == PLANE - 1
+    pl.when(jnp.logical_not(first))(lambda: halo.start())
+    gates_grad[...] = dot_tn(conv[...], both[...])
+    sums[7:8, :] = sums[7:8, :] * par[8:9, :]
+
+    @pl.when(final)
+    def _():
+        conv_grad[rows : rows + 8, :] = jnp.zeros((8, lanes), F32)
+
+    pl.when(jnp.logical_not(final))(lambda: halo.wait_recv())
+
+    def finish(c):
+        at = chunk_rows(c)
+        tall = pl.ds(pl.multiple_of(c * CHUNK, 8), CHUNK + 8)
+        block, mask = conv_grad[tall, :], masks[tall, :]
+        total = par[0:1, :] * block[:CHUNK, :]
+        for lag in range(1, KW):
+            total = total + mask[lag : lag + CHUNK, lag : lag + 1] * (
+                par[lag : lag + 1, :] * block[lag : lag + CHUNK, :]
+            )
+        grad = total.astype(BF16)
+        scan_low[at, :] = grad
+        pairs[0].start(c)
+        products = grad.astype(F32) * scan_rows[
+            pl.ds(pl.multiple_of(c * CHUNK + 8, 8), CHUNK), :
+        ] + gate_low[at, :].astype(F32) * gate_rows[at, :]
+        inners[z, c] = as_row(jnp.sum(products, axis=1, keepdims=True))
+        inner_spread.start(c)
+
+    each_chunk(chunks, finish)
+
+    def close(c):
+        at = chunk_rows(c)
+        inner_spread.finish(c)
+        total = inners[0, c] + inners[1, c] + inners[2, c] + inners[3, c]
+        scale = scales[at, :]
+        coefs[at, :] = scale * scale * as_columns(total) / features
+        inner_spread.drain(c)
+        for pair in pairs:
+            pair.drain(c)
+
+    each_chunk(chunks, close)
+    for whole in wholes:
+        whole.wait()
+    pl.when(jnp.logical_not(first))(lambda: halo.wait_send())
+
+
+def recur_back(low, mix_w, gate_rows, hidden, conv, decay_rows, input_rows, scan_rows, masks, par,
+               gates_w, scales, normed, mixed):
+    rows, features = low.shape
+    lanes = gate_rows.shape[1]
+    chunks = rows // CHUNK
+
+    def pair(size):
+        return struct((2, rows, size), BF16)
+
+    return pl.pallas_call(
+        recur_back_kernel,
+        out_shape=(
+            struct((lanes, 2 * lanes), F32),
+            struct((8, lanes), F32),
+            struct((rows, LANE), F32),
+            pair(features), pair(lanes), pair(features), pair(lanes), pair(lanes),
+        ),
+        in_specs=[VM] * 12 + [ANY] * 3,
+        out_specs=[VM] * 3 + [ANY] * 5,
+        scratch_shapes=[
+            vm(lanes // LANE, rows, LANE, kind=F32), vm(lanes // LANE, rows, LANE, kind=F32),
+            vm(8, LANE, kind=F32),
+            vm(rows, 2 * lanes), vm(rows + 8, lanes, kind=F32), vm(rows, lanes), vm(rows, lanes),
+            vm(PLANE, 8, lanes, kind=F32), vm(LINE, chunks, 8, LANE, kind=F32),
+            dma(7), dma(7), pltpu.SemaphoreType.DMA, pltpu.SemaphoreType.DMA,
+            dma(LINE - 1, chunks), dma(LINE - 1, chunks),
+            dma(2, chunks), dma(2, chunks), dma(2, chunks), dma(3), dma(3), dma(3),
+        ],
+        compiler_params=pltpu.CompilerParams(
+            collective_id=4, has_side_effects=True, vmem_limit_bytes=60 << 20
+        ),
+        name="recur_back",
+    )(
+        low, mix_w, gate_rows, hidden, conv, decay_rows, input_rows, scan_rows, masks, par, gates_w,
+        scales, normed, mixed, low,
+    )
+
+
+def last_kernel(
+    scan_w, gate_w, grad, tok, coefs, scales, gain, scan_low, gate_low, pack,
+    normed_pair, mixed_pair, low_pair, scan_pair, gate_pair,
+    tokens_grad, gain_grad, pack_sum, mix_own, scan_own, gate_own, lands,
+    part, land, acc, left, right, stages, pack_land, gain_land,
+    red_send, red_recv, w_send, w_recv, w_back, load_sem, pack_send, pack_recv, gain_send, gain_recv,
+):
+    s, z = lax.axis_index("seq"), lax.axis_index("tp")
+    rows, width = tok.shape
+    chunks = rows // CHUNK
+    loads = [
+        pltpu.make_async_copy(src, dst, load_sem.at[i])
+        for i, (src, dst) in enumerate(
+            (
+                (low_pair, left.at[0]), (mixed_pair, right.at[0]), (normed_pair, left.at[1]),
+                (scan_pair, right.at[1]), (gate_pair, right.at[2]),
+            )
+        )
+    ]
+    for load in loads:
+        load.start()
+    meet(s, z)
+    packs = [
+        remote(
+            pack.at[flip_all(s, bits)], pack_land.at[s], pack_send.at[bits - 1],
+            pack_recv.at[bits - 1], (flip_all(s, bits), z),
+        )
+        for bits in range(1, PLANE)
+    ]
+    for copy in packs:
+        copy.start()
+    red = LineReduce(s, z, part, land, red_send, red_recv)
+    weights = [
+        WeightGrads(s, z, stages.at[i], lands.at[i], own, w_send.at[i], w_recv.at[i], w_back.at[i])
+        for i, own in enumerate((mix_own, scan_own, gate_own))
+    ]
+    gain_land[s] = jnp.zeros_like(gain_grad)
+
+    def project(g):
+        at = group_rows(g)
+        values = dot_nt(scan_low[at, :], scan_w[...]) + dot_nt(gate_low[at, :], gate_w[...])
+        for k in range(GROUP // CHUNK):
+            c = g * (GROUP // CHUNK) + k
+            here = slice(k * CHUNK, (k + 1) * CHUNK)
+            for o in range(LINE):
+                part[c, o] = values[here, o * width : (o + 1) * width].astype(BF16)
+            red.hop(0, c)
+
+    def reduced(c):
+        at = chunk_rows(c)
+        red.hop(3, c)
+        red.landed(c, acc)
+        up = acc[...] + part[c, z].astype(F32)
+        scale, values = scales[at, 0:1], tok[at, :].astype(F32)
+        gain_land[s, 0:1, :] += jnp.sum(up * values * scale, axis=0, keepdims=True)
+        tokens_grad[at, :] = (
+            grad[at, :] + scale * gain[0:1, :] * up - values * coefs[at, 0:1]
+        )
+
+    project(0)
+    for load in loads:
+        load.wait()
+
+    def weigh(t):
+        for k in range(4):
+            pl.when(t == k)(lambda k=k: weights[1].block((k + 3) % 4, left.at[1], right.at[1]))
+            pl.when(t == k)(lambda k=k: weights[2].block((k + 3) % 4, left.at[1], right.at[2]))
+            pl.when(t == 4 + k // 2)(lambda k=k: weights[0].block(k, left.at[0], right.at[0]))
+
+    def turn(t, carry):
+        in_range(t, chunks, lambda c: red.hop(1, c))
+        pl.when((lax.rem(t, 2) == 0) & (t < chunks - 2))(lambda: project(t // 2 + 1))
+        weigh(t)
+        in_range(t - 1, chunks, reduced)
+        in_range(t, chunks, lambda c: red.hop(2, c))
+        return carry
+
+    lax.fori_loop(0, chunks + 1, turn, 0)
+    gain_spread = Spread(s, z, lambda p: gain_land.at[p], gain_send, gain_recv)
+    gain_spread.start()
+    for bits in range(1, PLANE):
+        other = pack_land.at[flip_all(s, bits)]
+        remote(
+            other, other, pack_send.at[bits - 1], pack_recv.at[bits - 1], (flip_all(s, bits), z)
+        ).wait_recv()
+    total = pack[s]
+    for bits in range(1, PLANE):
+        total = total + pack_land[flip_all(s, bits)]
+    pack_sum[...] = total
+    for weight in weights:
+        weight.finish()
+    gain_spread.finish()
+    total = gain_land[0]
+    for place in range(1, PLANE):
+        total = total + gain_land[place]
+    gain_grad[...] = total
+    for copy in packs:
+        copy.wait_send()
+    each_chunk(chunks, red.drain)
+
+
+def last_reduce(scan_w, gate_w, grad, tok, coefs, scales, gain, scan_low, gate_low, pack, pairs):
+    rows, width = tok.shape
+    features, lanes = width * LINE, scan_w.shape[1]
+    chunks, part = rows // CHUNK, features // PLANE
+    return pl.pallas_call(
+        last_kernel,
+        out_shape=(
+            struct((rows, width), F32),
+            struct((8, width), F32),
+            struct(pack.shape[1:], F32),
+            struct((part, lanes), F32),
+            struct((part, lanes), F32),
+            struct((part, lanes), F32),
+            struct((3, 3, part, lanes), BF16),
+        ),
+        in_specs=[VM] * 10 + [ANY] * 5,
+        out_specs=[VM] * 6 + [ANY],
+        scratch_shapes=[
+            vm(chunks, LINE, CHUNK, width), vm(chunks, LINE + 1, CHUNK, width),
+            vm(CHUNK, width, kind=F32),
+            vm(2, 2 * rows, features), vm(3, 2 * rows, lanes), vm(3, 3, part, lanes),
+            vm(*pack.shape, kind=F32), vm(PLANE, 8, width, kind=F32),
+            dma(LINE, chunks), dma(LINE + 1, chunks),
+            dma(3, 3), dma(3, 3), dma(3, 3), dma(5), dma(7), dma(7), dma(7), dma(7),
+        ],
+        compiler_params=pltpu.CompilerParams(
+            collective_id=5, has_side_effects=True, vmem_limit_bytes=63 << 20
+        ),
+        name="last_reduce",
+    )(
+        scan_w, gate_w, grad, tok, coefs, scales, gain, scan_low, gate_low, pack,
+        *[pair.reshape(2 * rows, pair.shape[2]) for pair in pairs],
+    )
+
+
 def shards_fast(
     tokens, mix_gain, scan_branch, gate_branch, kernel_taps, kernel_bias, decay_gate, decay_bias,
     input_gate, input_bias, decay_logit, mixer_out, feed_gain, gate_weight, up_weight, down_weight,
@@ -1005,184 +1885,97 @@
         1,
     )
     par = jnp.concatenate(
-        [taps_f, biases, CD * jax.nn.softplus(-logit_f), jnp.zeros((8, lanes), F32)], 0
+        [
+            taps_f, biases, CD * jax.nn.softplus(-logit_f), CD * jax.nn.sigmoid(-logit_f),
+            jnp.zeros((7, lanes), F32),
+        ],
+        0,
     )
     half = gains.shape[1] // 2
     gain_full = gains_all[:, :, 0, :].reshape(-1, 2, half).transpose(1, 0, 2).reshape(2, -1)
     gain_full = jnp.pad(gain_full, ((0, 6), (0, 0)))
     (
         normed_first, scan_pad, gate_rows, conv_rows, decay_rows, input_rows, hidden_state, mixed,
-        state_rows, decay_sums, cot_full, up_w, down_w,
+        scale_first_rows, decay_sums, cot_full, up_w, down_w,
     ) = recur_forward(
         tok_all, scan_w, gate_w, gates_w, par, gain_full, masks, cotangent, up_weight, down_weight
     )
-
-    offsets = ext_offsets[:row_count]
-    resets = offsets == 0
-    mix_f = lax.all_gather(mix_gain, "seq", axis=0, tiled=True).astype(F32)
-    feed_f = lax.all_gather(feed_gain, "seq", axis=0, tiled=True).astype(F32)
-    gathered=[None, scan_w, gate_w, None,None,None,biases[1],None,biases[2],logit_f[0],mix_w,None,ffn_gate,up_w,down_w]
-    taps_bias=biases[0]
-    normed_first_k=normed_first
-    tokens_f = tokens.astype(jnp.float32)
-    scale_first = row_scale(tokens_f)
-    scan_rows = scan_pad[8:]
-    gelu_rows, gelu_pull = jax.vjp(smooth_gelu, gate_rows)
-    rim_rows = from_behind(scan_rows[row_count - (KW - 1) :], "seq", 1)
-    padded_rows = jnp.concatenate([rim_rows, scan_rows], axis=0)
-    conv_sum = taps_bias + taps_f[0] * scan_rows
-    for lag_step in range(1, KW):
-        lagged = padded_rows[KW - 1 - lag_step : KW - 1 - lag_step + row_count]
-        conv_sum = conv_sum + jnp.where(
-            (offsets >= lag_step)[:, None], taps_f[lag_step] * lagged, 0.0
-        )
-    lanes = scan_rows.shape[1]
-    groups = lanes // BW
-    conv_blocks = conv_rows.reshape(row_count, groups, BW)
-    decay_mats = mats[0]
-    input_mats = mats[1]
-    decay_rows = block_mix(conv_blocks, decay_mats) + gathered[6].astype(jnp.float32)
-    input_rows = block_mix(conv_blocks, input_mats) + gathered[8].astype(jnp.float32)
-
-    def local_terms(decay_in, input_in, logit_in, conv_in):
-        kept_part, driven_part, decay_part = recurrence_terms(
-            decay_in, input_in, logit_in, conv_in, resets
-        )
-        return ((kept_part, driven_part), decay_part)
-
-    terms_out, terms_pull, decay_now = jax.vjp(
-        local_terms,
-        decay_rows,
-        input_rows,
-        gathered[9].astype(jnp.float32),
-        conv_rows.astype(jnp.float32),
-        has_aux=True,
-    )
-    kept_decay, driven = terms_out
-    local_prod, local_state = lax.associative_scan(combine, (kept_decay, driven), axis=0)
-    before = entering(
-        (local_prod[row_count - 1], local_state[row_count - 1]),
-        "seq",
-        combine,
-        (jnp.ones((lanes,), jnp.float32), jnp.zeros((lanes,), jnp.float32)),
-        False,
-    )
-    state_in = before[1]
-    state_in=state_rows[0]
-    resid = tokens_f + reduce_features(matmul(mixed, gathered[10]))
-    scale_second = row_scale(resid)
-    normed_second = spread_rows((resid * scale_second[:, None] * feed_f).astype(jnp.bfloat16))
-    gate_pre = matmul(normed_second, gathered[12])
-    up_pre = matmul(normed_second, gathered[13])
-    gelu_mid, mid_pull = jax.vjp(smooth_gelu, gate_pre)
-    hidden_mid = (gelu_mid * up_pre).astype(jnp.bfloat16)
-    block_out = resid + reduce_features(matmul(hidden_mid, gathered[14]))
-    down_grad = matmul_tn(hidden_mid, cot_full)
-    grad_mid = matmul_nt(cot_full, gathered[14])
-    grad_gate = mid_pull(grad_mid * up_pre)[0].astype(jnp.bfloat16)
-    grad_up = (grad_mid * gelu_mid).astype(jnp.bfloat16)
-    gate_grad = matmul_tn(normed_second, grad_gate)
-    up_grad = matmul_tn(normed_second, grad_up)
-    grad_second = reduce_features(
-        matmul_nt(grad_gate, gathered[12]) + matmul_nt(grad_up, gathered[13])
-    )
-    back_second, feed_grad = norm_back(resid, scale_second, feed_f, grad_second)
-    grad_resid = cotangent.astype(jnp.float32) + back_second
-    grad_branch = spread_grads(grad_resid.astype(jnp.bfloat16))
-    out_grad = matmul_tn(mixed, grad_branch)
-    grad_mixed = matmul_nt(grad_branch, gathered[10])
-    grad_hidden = grad_mixed * gelu_rows
-    grad_gate_rows = gelu_pull(grad_mixed * hidden_state)[0].astype(jnp.bfloat16)
-    next_decay = jnp.concatenate([kept_decay[1:], jnp.ones_like(kept_decay[:1])], axis=0)
-    tail_prod, local_adjoint = lax.associative_scan(
-        combine, (next_decay, grad_hidden), reverse=True, axis=0
-    )
-    after = entering(
-        (local_prod[row_count - 1], kept_decay[0] * local_adjoint[0]),
-        "seq",
-        combine,
-        (jnp.ones((lanes,), jnp.float32), jnp.zeros((lanes,), jnp.float32)),
-        True,
-    )
-    adjoint_in = after[1]
-    adjoint = local_adjoint + tail_prod * adjoint_in[None, :]
-    prev_state = jnp.concatenate([state_in[None, :], hidden_state[:-1]], axis=0)
-    grad_decay_rows, grad_input_rows, logit_grad, conv_direct = terms_pull(
-        (adjoint * prev_state, adjoint)
-    )
-    decay_grad_low = grad_decay_rows.astype(jnp.bfloat16)
-    input_grad_low = grad_input_rows.astype(jnp.bfloat16)
-    decay_w_grad = block_outer(conv_blocks, decay_grad_low)
-    input_w_grad = block_outer(conv_blocks, input_grad_low)
-    decay_b_grad = jnp.sum(decay_grad_low.astype(jnp.float32), axis=0)
-    input_b_grad = jnp.sum(input_grad_low.astype(jnp.float32), axis=0)
-    grad_conv = (
-        conv_direct
-        + block_back(decay_grad_low, decay_mats)
-        + block_back(input_grad_low, input_mats)
-    )
-    rim_back = from_behind(grad_conv[: KW - 1], "seq", -1)
-    grad_extended = jnp.concatenate([grad_conv, rim_back], axis=0)
-    ext_offsets = seq_offsets(lengths, shard_index * row_count, row_count + KW - 1)
-    grad_scan = taps_f[0] * grad_conv
-    tap_grads = [jnp.sum(grad_conv * scan_rows, axis=0)]
-    for lag_step in range(1, KW):
-        ahead = grad_extended[lag_step : lag_step + row_count]
-        ahead_ok = (ext_offsets[lag_step : lag_step + row_count] >= lag_step)[:, None]
-        grad_scan = grad_scan + jnp.where(ahead_ok, taps_f[lag_step] * ahead, 0.0)
-        lagged = padded_rows[KW - 1 - lag_step : KW - 1 - lag_step + row_count]
-        tap_grads.append(
-            jnp.sum(jnp.where((offsets >= lag_step)[:, None], grad_conv * lagged, 0.0), axis=0)
-        )
-    taps_grad = jnp.stack(tap_grads, axis=0)
-    taps_bias_grad = jnp.sum(grad_conv, axis=0)
-    scan_grad_low = grad_scan.astype(jnp.bfloat16)
-    scan_w_grad = matmul_tn(normed_first, scan_grad_low)
-    gatebr_grad = matmul_tn(normed_first, grad_gate_rows)
-    grad_first = reduce_features(
-        matmul_nt(scan_grad_low, gathered[1]) + matmul_nt(grad_gate_rows, gathered[2])
-    )
-    back_first, mix_grad = norm_back(tokens_f, scale_first, mix_f, grad_first)
-    tokens_grad = grad_resid + back_first
-    decay_total = decay_sums[0]
-    summed = (
-        lax.psum_scatter(mix_grad, "seq", scatter_dimension=0, tiled=True),
-        lax.psum_scatter(scan_w_grad, "seq", scatter_dimension=0, tiled=True),
-        lax.psum_scatter(gatebr_grad, "seq", scatter_dimension=0, tiled=True),
-        lax.psum_scatter(taps_grad, "seq", scatter_dimension=1, tiled=True),
-        lax.psum_scatter(taps_bias_grad, "seq", scatter_dimension=0, tiled=True),
-        lax.psum_scatter(decay_w_grad, "seq", scatter_dimension=1, tiled=True),
-        lax.psum_scatter(decay_b_grad, "seq", scatter_dimension=0, tiled=True),
-        lax.psum_scatter(input_w_grad, "seq", scatter_dimension=1, tiled=True),
-        lax.psum_scatter(input_b_grad, "seq", scatter_dimension=0, tiled=True),
-        lax.psum_scatter(logit_grad, "seq", scatter_dimension=0, tiled=True),
-        lax.psum_scatter(out_grad, "seq", scatter_dimension=1, tiled=True),
-        lax.psum_scatter(feed_grad, "seq", scatter_dimension=0, tiled=True),
-        lax.psum_scatter(gate_grad, "seq", scatter_dimension=0, tiled=True),
-        lax.psum_scatter(up_grad, "seq", scatter_dimension=0, tiled=True),
-        lax.psum_scatter(down_grad, "seq", scatter_dimension=1, tiled=True),
-        lax.psum_scatter(decay_total, "seq", scatter_dimension=0, tiled=True),
-    )
-    mean_decay = summed[15] / (row_count * seq_devices)
+    width = tokens.shape[1]
+    own_feed = lax.dynamic_slice(
+        gain_full[1:2], (0, lax.axis_index("tp") * width), (1, width)
+    )
+    feed_own = jnp.broadcast_to(own_feed, (8, width))
+    (
+        resid, scales, coefs, bo_part, gs_part,
+        low_pair, cot_pair, mid_pair, gate_pair, up_pair,
+    ) = feed_forward(
+        mixed, mix_w, tokens, feed_own, ffn_gate, up_w, down_w, cot_full
+    )
+    grad_resid, grad_branch, block_out, feed_grads, gate_own, up_own, down_own, _ = back_feed(
+        resid, scales, coefs, cotangent, feed_own, gs_part, bo_part,
+        (low_pair, cot_pair, mid_pair, gate_pair, up_pair),
+    )
+    gates_grad, sums, first_coefs, normed_pair, mixed_pair, branch_pair, scan_pair, gaterow_pair = (
+        recur_back(
+            grad_branch, mix_w, gate_rows, hidden_state, conv_rows, decay_rows, input_rows, scan_pad,
+            masks, par, gates_w, scale_first_rows, normed_first, mixed,
+        )
+    )
+
+    def own_parts(rows):
+        return rows.reshape(rows.shape[0], seq_devices, part).transpose(1, 0, 2)
+
+    small = own_parts(jnp.concatenate([sums, decay_sums[0:1]], 0)).reshape(seq_devices, -1)
+    tiles = [
+        jnp.stack(
+            [
+                gates_grad[g * BW : (g + 1) * BW, i * lanes + g * BW : i * lanes + (g + 1) * BW]
+                for g in range(groups)
+            ]
+        )
+        .reshape(groups, seq_devices, -1)
+        .transpose(1, 0, 2)
+        .reshape(seq_devices, -1)
+        for i in range(2)
+    ]
+    feed_part = feed_grads[0].reshape(seq_devices, -1)
+    flat_grads = jnp.concatenate([*tiles, small, feed_part], 1)
+    grad_rows = -(-flat_grads.shape[1] // (128 * 8)) * 8
+    grad_pack = jnp.pad(flat_grads, ((0, 0), (0, grad_rows * 128 - flat_grads.shape[1])))
+    own_mix = lax.dynamic_slice(gain_full[0:1], (0, lax.axis_index("tp") * width), (1, width))
+    tokens_grad, mix_grads, pack_sum, mix_own, scan_own, gaterow_own, _ = last_reduce(
+        scan_w, gate_w, grad_resid, tokens, first_coefs, scale_first_rows,
+        jnp.broadcast_to(own_mix, (8, width)), scan_pair[0], gaterow_pair[0],
+        grad_pack.reshape(seq_devices, grad_rows, 128),
+        (normed_pair, mixed_pair, branch_pair, scan_pair, gaterow_pair),
+    )
+    pack_sum = pack_sum.reshape(-1)
+    gate_size = groups * gate_cut // groups
+    cut_at = 2 * gate_size
+    small_sum = pack_sum[cut_at : cut_at + 9 * part].reshape(9, part)
+    feed_sum = pack_sum[cut_at + 9 * part : cut_at + 9 * part + mix_gain.shape[0]]
+    mix_sum = lax.dynamic_slice(
+        mix_grads[0], (shard_index * mix_gain.shape[0],), (mix_gain.shape[0],)
+    )
     return (
         block_out,
         tokens_grad,
-        summed[0],
-        summed[1],
-        summed[2],
-        summed[3],
-        summed[4],
-        summed[5],
-        summed[6],
-        summed[7],
-        summed[8],
-        summed[9],
-        summed[10],
-        summed[11],
-        summed[12],
-        summed[13],
-        summed[14],
-        mean_decay,
+        mix_sum,
+        scan_own,
+        gaterow_own,
+        small_sum[0:KW],
+        small_sum[KW],
+        pack_sum[:gate_size].reshape(groups, -1),
+        small_sum[KW + 1],
+        pack_sum[gate_size : 2 * gate_size].reshape(groups, -1),
+        small_sum[KW + 2],
+        small_sum[KW + 3],
+        mix_own.T,
+        feed_sum,
+        gate_own,
+        up_own,
+        down_own.T,
+        small_sum[KW + 4] / (row_count * seq_devices),
     )
 
 
@@ -1208,7 +2001,7 @@
         P("seq", "tp"),
     )
     return jax.shard_map(
-        shards_fast if mesh.shape['seq']==8 else shards_general,
+        shards_fast if (mesh.shape["seq"], mesh.shape["tp"]) == (PLANE, LINE) else shards_general,
         mesh=mesh,
         in_specs=placed,
         out_specs=(

time: 1990 us -> 845 us (0.42)
  waiting for transfers between devices: 1030 us -> 0 us
  Pallas kernels: 169 us -> 772 us
  local copies, waits for them, and re-layouts: 385 us -> 39.8 us
  matrix products: 146 us -> 0 us
  other arithmetic: 125 us -> 15.5 us
  blocking collectives: 91.2 us -> 0 us
    reduce_scatter x10 -> x0, waiting for transfers between devices: 844 us -> none  [the longest x4 376 us: reduce_features(): return lax.psum_scatter(values, 'tp', scatter_dimension=1, tiled=True)]
    pallas_call x0 -> x4, Pallas kernels: none -> 603 us  [the longest x1 237 us: recur_back(): pl.pallas_call(recur_back_kernel, out_shape=(struct((lanes, 2 * lanes), F...]
    slice x114 -> x11, local copies, waits for them, and re-layouts: 216 us -> 7.82 us  [the longest x1 1.84 us: shards_fast(): gates_grad[g * BW:(g + 1) * BW, i * lanes + g * BW:i * lanes + (g + 1) * BW]]
    dot_general x22 -> x0, matrix products: 146 us -> none  [the longest x6 52.7 us: matmul_tn(): lax.dot_general(left_side, right_side, (((0,), (0,)), ((), ())), preferre...]
    unnamed x18 -> x0, waiting for transfers between devices: 122 us -> none
    all_gather x2 -> x0, waiting for transfers between devices: 62 us -> none  [the longest x1 62 us: spread_rows(): return lax.all_gather(values, 'tp', axis=1, tiled=True)]
    pad x49 -> x0, local copies, waits for them, and re-layouts: 58.9 us -> none  [the longest x34 48.2 us: shards_fast(): lax.associative_scan(combine, (next_decay, grad_hidden), reverse=True, ax...]
    unnamed x2 -> x0, blocking collectives: 38.7 us -> none
  transfers between devices with their start and end apart: 17 -> 0, of which waited for: 13 -> 0; matrix products, arithmetic and copies ran while one was open for 28% -> 0% of each run, Pallas kernels for 0% -> 0%
where the time goes in v2:
time: 845 us; the launch traced here: 829 us
  Pallas kernels  772 us (91%)
  local copies, waits for them, and re-layouts  39.8 us (5%)
  other arithmetic  15.5 us (2%)
    pallas_call x1, Pallas kernels, recur_back(): pl.pallas_call(recur_back_kernel, out_shape=(struct((lanes, 2 * lanes), F...  237 us
    pallas_call x1, Pallas kernels, back_feed(): pl.pallas_call(back_kernel, out_shape=(struct((rows, width), F32), struct...  154 us
    pallas_call x1, Pallas kernels, feed_forward(): pl.pallas_call(feed_kernel, out_shape=(struct((rows, width), F32), struct...  134 us
    pallas_call x1, Pallas kernels, recur_forward(): pl.pallas_call(recur_kernel, out_shape=(struct((rows, features), BF16), s...  86.9 us
    pallas_call x1, Pallas kernels, gather_first(): pl.pallas_call(gather_kernel, out_shape=(struct((rows, width * LINE), BF1...  82 us
    pallas_call x1, Pallas kernels, last_reduce(): pl.pallas_call(last_kernel, out_shape=(struct((rows, width), F32), struct...  78.7 us

profile of v2, /device:TPU:0, one launch (start us, length us, event | category | flops | bytes accessed | tf_op | source)
XLA Modules:
  0.0 828.8 jit_solution(6969901285959568671)
XLA Ops:
  0.7 0.8 reduce-window.9
  1.5 0.7 bitcast_subtract_fusion
  2.2 0.8 reshape.328
  2.9 1.3 fusion.40.gains
  4.3 0.1 select_reduce_fusion
  4.4 0.8 reshape.329
  5.1 0.8 reshape.330
  5.9 2.8 concatenate.37
  8.7 0.6 pad_bitcast_fusion.1.pack
  9.3 1.6 compare_convert_fusion.masks
  10.9 82.0 %gather_first.1 = (bf16[768,2048]{1,0:T(8,128)(2,1)}, bf16[8,208,128]{2,1,0:T(8,128)(2,1)}, f32[4,8,8,128]{3,2,1,0:T(8,128)}, bf16[2048,640]{1,0:T(8,128)(2,1)},...) custom-call(bf16[768,512]{1,0:T(8,128)(2,1)} %tok.5, ...), custom_call_target="tpu_custom_call" | custom-call | tf_op jit(solution)/shard_map/gather_first/pallas_call | solution.py:672
  92.9 1.1 copy.63
  94.1 0.1 reshape.361
  94.1 0.1 reshape.357
  94.3 0.1 reshape.359
  94.7 0.1 reshape.356
  94.8 1.2 concatenate.44.par
  96.0 0.9 slice_reduce_fusion
  97.0 0.1 reshape_squeeze.6
  97.1 0.1 reshape.335
  97.3 0.6 broadcast_in_dim.36.gain
  97.9 0.6 broadcast_in_dim.38.gain
  98.5 0.6 pad.57.gain
  99.2 0.5 reshape.333
  99.9 0.5 reshape.334
  100.6 8.5 %fusion.24.gates_w = bf16[640,1280]{1,0:T(8,128)(2,1)} fusion(bf16[160,160]{1,0:T(8,128)(2,1)S(1)} %squeeze.43, bf16[160,160]{1,0:T(8,128)(2,1)S(1)} %squeeze.42, bf16[160,160]{1,0:T(8,128)(2,1)S(1)} %squeeze.41, bf16[160,160]{1,0:T(8,128)(2,1)S(1)} %squeeze.40, bf16[160,160]{1,0:T(8,128)(2,1)S(1)} %squeeze.39, bf16[160,160]{1,0:T(8,128)(2,1)S(1)} %squeeze.38, ...), kind=kLoop, calls=%fused_computation.32 | loop fusion | flops 40960000 | bytes 2048000 | tf_op jit(solution)/shard_map/concatenate | solution.py:1878
  109.0 86.9 %recur_forward.1 = (bf16[768,2048]{1,0:T(8,128)(2,1)}, f32[776,640]{1,0:T(8,128)}, f32[768,640]{1,0:T(8,128)}, bf16[768,640]{1,0:T(8,128)(2,1)}, f32[768,640]{1,...) custom-call(bf16[768,2048]{1,0:T(8,128)(2,1)} %get-tuple-element.69., ...), custom_call_target="tpu_custom_call" | custom-call | tf_op jit(solution)/shard_map/recur_forward/pallas_call | solution.py:917
  195.9 0.7 slice.177
  196.7 133.8 %feed_forward.1 = (f32[768,512]{1,0:T(8,128)}, f32[768,128]{1,0:T(8,128)}, f32[768,128]{1,0:T(8,128)}, bf16[6,4,128,512]{3,2,1,0:T(8,128)(2,1)}, bf16[6,4,128,51...) custom-call(bf16[768,640]{1,0:T(8,128)(2,1)} %get-tuple-element.74.m, ...), custom_call_target="tpu_custom_call" | custom-call | tf_op jit(solution)/shard_map/feed_forward/pallas_call | solution.py:1254
  330.5 154.0 %back_feed.1 = (f32[768,512]{1,0:T(8,128)}, bf16[768,2048]{1,0:T(8,128)(2,1)}, f32[768,512]{1,0:T(8,128)}, f32[8,512]{1,0:T(8,128)}, f32[256,1536]{1,0:T(8,128)}...) custom-call(f32[768,512]{1,0:T(8,128)} %get-tuple-element.80.resid, ...), custom_call_target="tpu_custom_call" | custom-call | tf_op jit(solution)/shard_map/back_feed/pallas_call | solution.py:1437
  484.5 0.7 slice_reduce_fusion.1
  485.3 3.0 copy.54
  488.3 236.8 %recur_back.1 = (f32[640,1280]{1,0:T(8,128)}, f32[8,640]{1,0:T(8,128)}, f32[768,128]{1,0:T(8,128)}, bf16[2,768,2048]{2,1,0:T(8,128)(2,1)}, bf16[2,768,640]{2,1,0...) custom-call(bf16[768,2048]{1,0:T(8,128)(2,1)} %get-tuple-element.92.low.lo, ...), custom_call_target="tpu_custom_call" | custom-call | tf_op jit(solution)/shard_map/recur_back/pallas_call | solution.py:1665
  725.1 0.9 pad_maximum_fusion.2
  726.2 2.2 slice_bitcast_fusion.1.scan_low
  728.4 1.0 slice_bitcast_fusion.gate_low
  729.4 1.8 fusion.43
  731.3 0.1 stack.35
  731.4 0.1 stack.38
  731.5 0.1 stack.37
  731.6 0.1 stack.36
  731.8 0.1 stack.33
  731.9 0.1 stack.32
  732.0 0.1 stack.31
  732.1 0.1 stack.30
  732.3 0.1 concatenate.46
  732.5 1.1 copy.62
  733.5 78.7 %last_reduce.1 = (f32[768,512]{1,0:T(8,128)}, f32[8,512]{1,0:T(8,128)}, f32[208,128]{1,0:T(8,128)}, f32[256,640]{1,0:T(8,128)}, f32[256,640]{1,0:T(8,128)}, /*in...) custom-call(bf16[2048,640]{1,0:T(8,128)(2,1)} %get-tuple-element.70.scan_w, bf16[2048,640]{1,0:T(8,128)(2,1)} %get-tuple-element.71.gate_w, ...), custom_call_target="tpu_custom_call" | custom-call | tf_op jit(solution)/shard_map/last_reduce/pallas_call | solution.py:1799
  812.3 1.4 slice.210
  813.7 0.7 slice.179
  814.4 0.6 fusion.42
  815.0 0.7 slice.205
  815.7 0.7 slice.181
  816.3 1.4 slice_multiply_fusion
  817.8 0.9 fusion.47
  818.7 0.6 reshape.355
  819.3 0.6 reshape.354
  820.0 2.2 copy.53
  822.1 1.1 copy.73
  823.3 1.1 copy.74
  824.4 0.8 copy.75
  825.3 0.8 copy.76
  826.1 1.1 copy.77
  827.3 1.1 copy.78
  (48 shorter events, 1.3 us)
Async XLA Ops:
  725.1 3.3 copy-start
  812.3 9.8 %copy-start.3 = (f32[768,512]{1,0:T(8,128)S(1)}, f32[768,512]{1,0:T(8,128)}, u32[]{:S(2)}) copy-start(f32[768,512]{1,0:T(8,128)} %get-tuple-element.223) | copy-start | bytes 4718596
  812.3 11.0 %copy-start.4 = (f32[768,512]{1,0:T(8,128)S(1)}, f32[768,512]{1,0:T(8,128)}, u32[]{:S(2)}) copy-start(f32[768,512]{1,0:T(8,128)} %get-tuple-element.224) | copy-start | bytes 4718596
  822.1 2.3 copy-start.6
  823.3 2.0 copy-start.5
  823.3 2.8 copy-start.2
  824.4 2.8 copy-start.1

commit v3 on v2

--- a/solution.py
+++ b/solution.py
@@ -2,6 +2,7 @@
 
 import jax
 import jax.numpy as jnp
+import numpy as np
 from jax import lax
 from jax.experimental import pallas as pl
 from jax.experimental.pallas import tpu as pltpu
@@ -512,12 +513,14 @@
         self.got(3)
         self.copy(8).start()
 
-    def finish(self):
+    def arrive(self):
         for i in range(4, 9):
             self.got(i)
+        self.keep().wait()
+
+    def drain(self):
         for i in range(9):
             self.copy(i).wait_send()
-        self.keep().wait()
 
 
 class Spread:
@@ -582,82 +585,6 @@
     lax.fori_loop(0, chunks, lambda c, carry: (body(c), carry)[1], 0)
 
 
-def gather_kernel(
-    tok, pack, gains, scan, gate, mix, ffn,
-    tok_all, pack_all, gains_all, scan_all, gate_all, mix_all, ffn_all,
-    line_send, line_recv, gain_send, gain_recv, plane_send, plane_recv, small_send, small_recv, local,
-):
-    s, z = lax.axis_index("seq"), lax.axis_index("tp")
-    chunks, width = tok.shape[0] // CHUNK, tok.shape[1]
-    line = LineGather(
-        s, z,
-        lambda c: tok.at[chunk_rows(c)],
-        lambda o, c: tok_all.at[chunk_rows(c), feature_columns(o, width)],
-        line_send, line_recv,
-    )
-    gain_line = LineGather(
-        s, z, lambda c: gains_all.at[z], lambda o, c: gains_all.at[o], gain_send, gain_recv
-    )
-    planes = []
-    for i, (own, full, make) in enumerate(
-        (
-            (scan, scan_all, rows_of),
-            (gate, gate_all, rows_of),
-            (mix, mix_all, columns_of),
-            (ffn, ffn_all, rows_of),
-        )
-    ):
-        size = own.shape[1] if make is columns_of else own.shape[0]
-        block, half = make(full, size)
-        planes.append(
-            PlaneGather(s, z, own, block, half, plane_send.at[i], plane_recv.at[i], local.at[i])
-        )
-    packs = Spread(s, z, lambda p: pack_all.at[p], small_send.at[0], small_recv.at[0])
-    gain_plane = Spread(s, z, lambda p: gains_all.at[z, p], small_send.at[1], small_recv.at[1])
-    keeps = [
-        pltpu.make_async_copy(gains, gains_all.at[z, s], local.at[4]),
-        pltpu.make_async_copy(pack, pack_all.at[s], local.at[5]),
-        pltpu.make_async_copy(tok, tok_all.at[:, feature_columns(z, width)], local.at[6]),
-    ]
-    for keep in keeps:
-        keep.start()
-    meet(s, z)
-    for keep in keeps[:2]:
-        keep.wait()
-    gain_plane.start()
-    packs.start()
-    for c in range(chunks):
-        line.start(c)
-    for plane in planes:
-        plane.start()
-    gain_plane.finish()
-    packs.finish()
-    gain_line.start(0)
-    for c in range(chunks):
-        line.forward(1, c)
-    gain_line.forward(1, 0)
-    planes[0].turn()
-    for c in range(chunks):
-        line.forward(2, c)
-    gain_line.forward(2, 0)
-    planes[1].turn()
-    planes[0].last()
-    planes[2].turn()
-    planes[1].last()
-    planes[3].turn()
-    planes[2].last()
-    for c in range(chunks):
-        line.forward(3, c)
-    gain_line.forward(3, 0)
-    planes[3].last()
-    for plane in planes:
-        plane.finish()
-    for c in range(chunks):
-        line.drain(c)
-    gain_line.drain(0)
-    keeps[2].wait()
-
-
 def dma(*shape):
     return pltpu.SemaphoreType.DMA(shape)
 
@@ -666,30 +593,8 @@
     return jax.ShapeDtypeStruct(shape, kind)
 
 
-def gather_first(tok, pack, gains, scan, gate, mix, ffn):
-    rows, width = tok.shape
-    chunks = rows // CHUNK
-    return pl.pallas_call(
-        gather_kernel,
-        out_shape=(
-            struct((rows, width * LINE), BF16),
-            struct((PLANE,) + pack.shape, pack.dtype),
-            struct((LINE, PLANE) + gains.shape, F32),
-            struct((scan.shape[0] * PLANE, scan.shape[1]), BF16),
-            struct((gate.shape[0] * PLANE, gate.shape[1]), BF16),
-            struct((mix.shape[0], mix.shape[1] * PLANE), BF16),
-            struct((ffn.shape[0] * PLANE, ffn.shape[1]), BF16),
-        ),
-        in_specs=[ANY] * 7,
-        out_specs=[ANY] * 7,
-        scratch_shapes=[
-            dma(2, LINE - 1, chunks), dma(2, LINE - 1, chunks),
-            dma(2, LINE - 1, 1), dma(2, LINE - 1, 1),
-            dma(4, 9), dma(4, 9), dma(2, 7), dma(2, 7), dma(7),
-        ],
-        compiler_params=pltpu.CompilerParams(collective_id=0, has_side_effects=True),
-        name="gather_first",
-    )(tok, pack, gains, scan, gate, mix, ffn)
+def vm(*shape, kind=BF16):
+    return pltpu.VMEM(shape, kind)
 
 
 def sigmoid(values):
@@ -757,45 +662,126 @@
     return [values[:, i * LANE : (i + 1) * LANE] for i in range(values.shape[1] // LANE)]
 
 
-def recur_kernel(
-    tok_all, scan_w, gate_w, gates_w, par, gain, masks, cot, up, down,
+def first_kernel(
+    tok, cot, small, gains, gate_blocks, scan, gate, mix, ffn, up, down, masks,
+    row_order, tile, cells, lane_order,
     normed, scan_rows, gate_rows, conv, decay_rows, input_rows, hidden, mixed, scales, decay_sum,
-    cot_all, up_all, down_all,
-    kept, driven, slots,
-    line_send, line_recv, plane_send, plane_recv, small_send, small_recv, halo_send, halo_recv, local,
+    par, gates_w, gain_own, scan_w, gate_w, mix_all, ffn_all, up_all, down_all, cot_all,
+    tok_all, small_all, gains_all, blocks_all, gain_full, kept, driven, slots,
+    tok_send, tok_recv, cot_send, cot_recv, gain_send, gain_recv, plane_send, plane_recv,
+    small_send, small_recv, carry_send, carry_recv, halo_send, halo_recv, local,
 ):
     s, z = lax.axis_index("seq"), lax.axis_index("tp")
-    rows, features = tok_all.shape
-    chunks, width, lanes = rows // CHUNK, cot.shape[1], gate_w.shape[1]
-    line = LineGather(
-        s, z,
-        lambda c: cot.at[chunk_rows(c)],
-        lambda o, c: cot_all.at[chunk_rows(c), feature_columns(o, width)],
-        line_send, line_recv,
-    )
-    planes = [
-        PlaneGather(
-            s, z, up, *rows_of(up_all, up.shape[0]), plane_send.at[0], plane_recv.at[0], local.at[0]
-        ),
-        PlaneGather(
-            s, z, down, *columns_of(down_all, down.shape[1]), plane_send.at[1], plane_recv.at[1],
-            local.at[1],
+    rows, width = tok.shape
+    chunks, features, lanes = rows // CHUNK, width * LINE, gate.shape[1]
+    part = gate_blocks.shape[0]
+
+    def line_of(own, full, send, recv):
+        return LineGather(
+            s, z,
+            lambda c: own.at[chunk_rows(c)],
+            lambda o, c: full.at[chunk_rows(c), feature_columns(o, width)],
+            send, recv,
+        )
+
+    toks = line_of(tok, tok_all, tok_send, tok_recv)
+    cots = line_of(cot, cot_all, cot_send, cot_recv)
+    gain_line = LineGather(
+        s, z, lambda c: gains_all.at[z], lambda o, c: gains_all.at[o], gain_send, gain_recv
+    )
+    planes = []
+    for i, (own, full, make) in enumerate(
+        (
+            (scan, scan_w, rows_of),
+            (gate, gate_w, rows_of),
+            (mix, mix_all, columns_of),
+            (ffn, ffn_all, rows_of),
+            (up, up_all, rows_of),
+            (down, down_all, columns_of),
+        )
+    ):
+        size = own.shape[1] if make is columns_of else own.shape[0]
+        planes.append(
+            PlaneGather(s, z, own, *make(full, size), plane_send.at[i], plane_recv.at[i], local.at[i])
+        )
+    spreads = [
+        Spread(s, z, lambda p: gains_all.at[z, p], small_send.at[0], small_recv.at[0]),
+        Spread(s, z, lambda p: small_all.at[p], small_send.at[1], small_recv.at[1]),
+        Spread(
+            s, z, lambda p: blocks_all.at[pl.ds(pl.multiple_of(p * part, 16), part)],
+            small_send.at[2], small_recv.at[2],
         ),
     ]
-    keep = pltpu.make_async_copy(cot, cot_all.at[:, feature_columns(z, width)], local.at[2])
+    keep = pltpu.make_async_copy(cot, cot_all.at[:, feature_columns(z, width)], local.at[6])
     keep.start()
+    tok_all[:, feature_columns(z, width)] = tok[...]
+    gains_all[z, s] = gains[...]
+    small_all[s] = small[...]
+    blocks_all[pl.ds(pl.multiple_of(s * part, 16), part), :] = gate_blocks[...]
     meet(s, z)
+    for spread in spreads:
+        spread.start()
     for c in range(chunks):
-        line.start(c)
-    for plane in planes:
+        toks.start(c)
+    for plane in planes[:2]:
         plane.start()
+    for spread in spreads:
+        spread.finish()
+    gain_line.start(0)
+    for c in range(chunks):
+        toks.forward(1, c)
+    gain_line.forward(1, 0)
+    planes[2].start()
+    planes[3].start()
+    placed = dot(
+        jnp.concatenate([small_all[p] for p in range(PLANE)], axis=1), lane_order[...]
+    )
+    par[...] = placed
+    falling = jnp.exp(-placed[7:8, :])
+    par[7:8, :] = CD * jnp.log1p(falling)
+    par[8:9, :] = CD * falling / (1.0 + falling)
+    half = blocks_all.shape[1] // 2
+    for i in range(2):
+        wide = dot(blocks_all[:, i * half : (i + 1) * half], tile[...]).astype(BF16)
+        gates_w[:, i * lanes : (i + 1) * lanes] = dot(row_order[...], wide).astype(BF16) * cells[...]
+    planes[0].turn()
+    planes[1].turn()
+    for c in range(chunks):
+        toks.forward(2, c)
+    gain_line.forward(2, 0)
+    planes[0].last()
+    planes[1].last()
+    planes[4].start()
+    gain_line.forward(3, 0)
+    pick = lax.broadcasted_iota(jnp.int32, (LANE, LANE), 0)
+    place = lax.broadcasted_iota(jnp.int32, (LANE, LANE), 1)
+    cut = LANE // 2
+    even = jnp.concatenate(
+        [gains_all[o, p] for o in range(LINE) for p in range(0, PLANE, 2)], axis=0
+    ).astype(BF16)
+    odd = jnp.concatenate(
+        [gains_all[o, p] for o in range(LINE) for p in range(1, PLANE, 2)], axis=0
+    ).astype(BF16)
+    for i in range(2):
+        from_even = (pick == place + i * cut) & (place < cut)
+        from_odd = (pick == place + (i - 1) * cut) & (place >= cut)
+        spots = dot(even, from_even.astype(F32).astype(BF16)) + dot(
+            odd, from_odd.astype(F32).astype(BF16)
+        )
+        for q in range(spots.shape[0] // 8):
+            gain_full[i : i + 1, q * LANE : (q + 1) * LANE] = spots[8 * q : 8 * q + 1, :]
+    gain_own[0:2, :] = gain_full[0:2, feature_columns(z, width)]
+    planes[0].arrive()
+    planes[1].arrive()
 
     def project(c):
+        toks.forward(3, c)
+        cots.start(c)
         at = chunk_rows(c)
         x = tok_all[at, :].astype(F32)
         scale = lax.rsqrt(jnp.sum(x * x, axis=1, keepdims=True) / features + EPSILON)
         scales[at, :] = jnp.broadcast_to(scale, (CHUNK, LANE))
-        low = (x * scale * gain[0:1, :]).astype(BF16)
+        low = (x * scale * gain_full[0:1, :]).astype(BF16)
         normed[at, :] = low
         scan_rows[pl.ds(pl.multiple_of(c * CHUNK + 8, 8), CHUNK), :] = dot(low, scan_w[...])
         gate_rows[at, :] = dot(low, gate_w[...])
@@ -812,6 +798,9 @@
     def _():
         scan_rows[0:8, :] = jnp.zeros((8, lanes), F32)
 
+    planes[2].turn()
+    planes[3].turn()
+    planes[5].start()
     decay_sum[...] = jnp.zeros_like(decay_sum)
     pl.when(jnp.logical_not(first))(lambda: halo.wait_recv())
 
@@ -839,9 +828,12 @@
         put(kept, at, goes_on * decay)
         put(driven, at, multiplier * sigmoid(inputs) * low.astype(F32))
         decay_sum[0:1, :] += jnp.sum(decay, axis=0, keepdims=True)
-        line.forward(1, c)
+        cots.forward(1, c)
 
     each_chunk(chunks, gates)
+    planes[2].last()
+    planes[3].last()
+    planes[4].turn()
     count = rows // SUBS
 
     def total_of(step, carry):
@@ -866,9 +858,8 @@
         whole = (whole[0] * here, here * whole[1] + value[sub : sub + 1, :])
     slots[s, 0:1, :] = whole[0]
     slots[s, 1:2, :] = whole[1]
-    spread = Spread(s, z, lambda p: slots.at[p], small_send, small_recv)
+    spread = Spread(s, z, lambda p: slots.at[p], carry_send, carry_recv)
     spread.start()
-    planes[0].turn()
     spread.finish()
     entry = jnp.zeros((1, lanes), F32)
     for place in range(PLANE - 1):
@@ -894,28 +885,32 @@
         now = get(driven, at)
         hidden[pl.ds(pl.multiple_of(c * CHUNK + 8, 8), CHUNK), :] = now
         mixed[at, :] = (gelu_of(gate_rows[at, :]) * now).astype(BF16)
-        line.forward(2, c)
+        cots.forward(2, c)
 
     each_chunk(chunks, mix)
-    planes[1].turn()
-    planes[0].last()
+    planes[4].last()
+    planes[5].turn()
     for c in range(chunks):
-        line.forward(3, c)
-    planes[1].last()
+        cots.forward(3, c)
+    planes[5].last()
+    for plane in planes[2:]:
+        plane.arrive()
     for plane in planes:
-        plane.finish()
+        plane.drain()
     for c in range(chunks):
-        line.drain(c)
+        toks.drain(c)
+        cots.drain(c)
+    gain_line.drain(0)
     pl.when(jnp.logical_not(final))(lambda: halo.wait_send())
     keep.wait()
 
 
-def recur_forward(tok_all, scan_w, gate_w, gates_w, par, gain, masks, cot, up, down):
-    rows, features = tok_all.shape
-    lanes = gate_w.shape[1]
+def first_half(tok, cot, small, gains, gate_blocks, scan, gate, mix, ffn, up, down, masks, consts):
+    rows, width = tok.shape
+    features, lanes = width * LINE, gate.shape[1]
     chunks = rows // CHUNK
     return pl.pallas_call(
-        recur_kernel,
+        first_kernel,
         out_shape=(
             struct((rows, features), BF16),
             struct((rows + 8, lanes), F32),
@@ -927,25 +922,36 @@
             struct((rows, lanes), BF16),
             struct((rows, LANE), F32),
             struct((8, lanes), F32),
-            struct((rows, features), BF16),
+            struct((16, lanes), F32),
+            struct((lanes, 2 * lanes), BF16),
+            struct((8, width), F32),
+            struct((features, lanes), BF16),
+            struct((features, lanes), BF16),
+            struct((mix.shape[0], mix.shape[1] * PLANE), BF16),
+            struct((ffn.shape[0] * PLANE, ffn.shape[1]), BF16),
             struct((up.shape[0] * PLANE, up.shape[1]), BF16),
             struct((down.shape[0], down.shape[1] * PLANE), BF16),
+            struct((rows, features), BF16),
         ),
-        in_specs=[VM] * 7 + [ANY] * 3,
-        out_specs=[VM] * 10 + [ANY] * 3,
+        in_specs=[VM] * 16,
+        out_specs=[VM] * 15 + [ANY] * 5,
         scratch_shapes=[
-            pltpu.VMEM((lanes // LANE, rows, LANE), F32),
-            pltpu.VMEM((lanes // LANE, rows, LANE), F32),
-            pltpu.VMEM((PLANE, 8, lanes), F32),
+            vm(rows, features),
+            vm(PLANE, *small.shape), vm(LINE, PLANE, *gains.shape, kind=F32),
+            vm(PLANE * gate_blocks.shape[0], gate_blocks.shape[1]), vm(8, features, kind=F32),
+            vm(lanes // LANE, rows, LANE, kind=F32), vm(lanes // LANE, rows, LANE, kind=F32),
+            vm(PLANE, 8, lanes, kind=F32),
             dma(2, LINE - 1, chunks), dma(2, LINE - 1, chunks),
-            dma(2, 9), dma(2, 9), dma(7), dma(7),
-            pltpu.SemaphoreType.DMA, pltpu.SemaphoreType.DMA, dma(3),
+            dma(2, LINE - 1, chunks), dma(2, LINE - 1, chunks),
+            dma(2, LINE - 1, 1), dma(2, LINE - 1, 1),
+            dma(6, 9), dma(6, 9), dma(3, 7), dma(3, 7), dma(7), dma(7),
+            pltpu.SemaphoreType.DMA, pltpu.SemaphoreType.DMA, dma(7),
         ],
         compiler_params=pltpu.CompilerParams(
-            collective_id=1, has_side_effects=True, vmem_limit_bytes=58 << 20
+            collective_id=0, has_side_effects=True, vmem_limit_bytes=60 << 20
         ),
-        name="recur_forward",
-    )(tok_all, scan_w, gate_w, gates_w, par, gain, masks, cot, up, down)
+        name="first_half",
+    )(tok, cot, small, gains, gate_blocks, scan, gate, mix, ffn, up, down, masks, *consts)
 
 
 class LineReduce:
@@ -1150,7 +1156,7 @@
         sums = squares[0, c] + squares[1, c] + squares[2, c] + squares[3, c]
         scale = lax.rsqrt(as_columns(sums) / features + EPSILON)
         scales[at, :] = scale
-        low[at, feature_columns(z, width)] = (resid[at, :] * scale[:, 0:1] * gain[0:1, :]).astype(
+        low[at, feature_columns(z, width)] = (resid[at, :] * scale[:, 0:1] * gain[1:2, :]).astype(
             BF16
         )
         line.start(c)
@@ -1236,10 +1242,6 @@
             copy.wait()
 
     each_chunk(chunks, close)
-
-
-def vm(*shape, kind=BF16):
-    return pltpu.VMEM(shape, kind)
 
 
 def feed_forward(mixed, mix_w, tok, gain, gate_w, up_w, down_w, cot):
@@ -1373,7 +1375,7 @@
         up = acc[...] + part[c, z].astype(F32)
         scale, values = scales[at, 0:1], resid[at, :]
         gain_grad[0:1, :] += jnp.sum(up * values * scale, axis=0, keepdims=True)
-        total = cot[at, :].astype(F32) + scale * gain[0:1, :] * up - values * coefs[at, 0:1]
+        total = cot[at, :].astype(F32) + scale * gain[1:2, :] * up - values * coefs[at, 0:1]
         grad[at, :] = total
         low[at, feature_columns(z, width)] = total.astype(BF16)
         line.start(c)
@@ -1469,23 +1471,21 @@
 def recur_back_kernel(
     low, mix_w, gate_rows, hidden, conv, decay_rows, input_rows, scan_rows, masks, par, gates_w, scales,
     normed_src, mixed_src, low_src,
-    gates_grad, sums, coefs, normed_pair, mixed_pair, low_pair, scan_pair, gate_pair,
+    gates_grad, sums, coefs, normed_twin, mixed_twin, low_twin, scan_pair, gate_pair,
     kept, grads, spilled, both, conv_grad, scan_low, gate_low, slots, inners,
     small_send, small_recv, halo_send, halo_recv, in_send, in_recv,
-    own_sem, give_send, give_recv, keep_sem, twin_send, twin_recv,
+    own_sem, give_send, give_recv, twin_send, twin_recv,
 ):
     s, z = lax.axis_index("seq"), lax.axis_index("tp")
     rows, features = low.shape
     lanes = gate_rows.shape[1]
     chunks = rows // CHUNK
-    wholes = []
-    for i, (src, out) in enumerate(
-        ((normed_src, normed_pair), (mixed_src, mixed_pair), (low_src, low_pair))
-    ):
-        wholes.append(pltpu.make_async_copy(src, out.at[0], keep_sem.at[i]))
-        wholes.append(
-            remote(src, out.at[1], twin_send.at[i], twin_recv.at[i], (flip(s, 0), z))
-        )
+    wholes = [
+        remote(src, out, twin_send.at[i], twin_recv.at[i], (flip(s, 0), z))
+        for i, (src, out) in enumerate(
+            ((normed_src, normed_twin), (mixed_src, mixed_twin), (low_src, low_twin))
+        )
+    ]
     pairs = [
         Halves(s, z, src, out, own_sem.at[i], give_send.at[i], give_recv.at[i])
         for i, (src, out) in enumerate(((scan_low, scan_pair), (gate_low, gate_pair)))
@@ -1668,7 +1668,8 @@
             struct((lanes, 2 * lanes), F32),
             struct((8, lanes), F32),
             struct((rows, LANE), F32),
-            pair(features), pair(lanes), pair(features), pair(lanes), pair(lanes),
+            struct((rows, features), BF16), struct((rows, lanes), BF16), struct((rows, features), BF16),
+            pair(lanes), pair(lanes),
         ),
         in_specs=[VM] * 12 + [ANY] * 3,
         out_specs=[VM] * 3 + [ANY] * 5,
@@ -1679,7 +1680,7 @@
             vm(PLANE, 8, lanes, kind=F32), vm(LINE, chunks, 8, LANE, kind=F32),
             dma(7), dma(7), pltpu.SemaphoreType.DMA, pltpu.SemaphoreType.DMA,
             dma(LINE - 1, chunks), dma(LINE - 1, chunks),
-            dma(2, chunks), dma(2, chunks), dma(2, chunks), dma(3), dma(3), dma(3),
+            dma(2, chunks), dma(2, chunks), dma(2, chunks), dma(3), dma(3),
         ],
         compiler_params=pltpu.CompilerParams(
             collective_id=4, has_side_effects=True, vmem_limit_bytes=60 << 20
@@ -1693,7 +1694,7 @@
 
 def last_kernel(
     scan_w, gate_w, grad, tok, coefs, scales, gain, scan_low, gate_low, pack,
-    normed_pair, mixed_pair, low_pair, scan_pair, gate_pair,
+    normed, normed_twin, mixed, mixed_twin, low, low_twin, scan_pair, gate_pair,
     tokens_grad, gain_grad, pack_sum, mix_own, scan_own, gate_own, lands,
     part, land, acc, left, right, stages, pack_land, gain_land,
     red_send, red_recv, w_send, w_recv, w_back, load_sem, pack_send, pack_recv, gain_send, gain_recv,
@@ -1705,7 +1706,9 @@
         pltpu.make_async_copy(src, dst, load_sem.at[i])
         for i, (src, dst) in enumerate(
             (
-                (low_pair, left.at[0]), (mixed_pair, right.at[0]), (normed_pair, left.at[1]),
+                (low, left.at[0, :rows]), (low_twin, left.at[0, rows:]),
+                (mixed, right.at[0, :rows]), (mixed_twin, right.at[0, rows:]),
+                (normed, left.at[1, :rows]), (normed_twin, left.at[1, rows:]),
                 (scan_pair, right.at[1]), (gate_pair, right.at[2]),
             )
         )
@@ -1807,7 +1810,7 @@
             struct((part, lanes), F32),
             struct((3, 3, part, lanes), BF16),
         ),
-        in_specs=[VM] * 10 + [ANY] * 5,
+        in_specs=[VM] * 10 + [ANY] * 8,
         out_specs=[VM] * 6 + [ANY],
         scratch_shapes=[
             vm(chunks, LINE, CHUNK, width), vm(chunks, LINE + 1, CHUNK, width),
@@ -1815,7 +1818,7 @@
             vm(2, 2 * rows, features), vm(3, 2 * rows, lanes), vm(3, 3, part, lanes),
             vm(*pack.shape, kind=F32), vm(PLANE, 8, width, kind=F32),
             dma(LINE, chunks), dma(LINE + 1, chunks),
-            dma(3, 3), dma(3, 3), dma(3, 3), dma(5), dma(7), dma(7), dma(7), dma(7),
+            dma(3, 3), dma(3, 3), dma(3, 3), dma(8), dma(7), dma(7), dma(7), dma(7),
         ],
         compiler_params=pltpu.CompilerParams(
             collective_id=5, has_side_effects=True, vmem_limit_bytes=63 << 20
@@ -1823,8 +1826,24 @@
         name="last_reduce",
     )(
         scan_w, gate_w, grad, tok, coefs, scales, gain, scan_low, gate_low, pack,
-        *[pair.reshape(2 * rows, pair.shape[2]) for pair in pairs],
-    )
+        *pairs[:6],
+        *[pair.reshape(2 * rows, pair.shape[2]) for pair in pairs[6:]],
+    )
+
+
+def placements(lanes, groups, seq_devices):
+    cut, part = BW // seq_devices, lanes // seq_devices
+    rows = np.arange(lanes)
+    source = (rows % BW) // cut * part + rows // BW * cut + rows % cut
+    row_order = (source[:, None] == rows[None, :]).astype(np.float32)
+    tile = (np.arange(2 * LANE)[:, None] == rows[None, :] % BW).astype(np.float32)
+    cells = (rows[:, None] // BW == rows[None, :] // BW).astype(np.float32)
+    spots = np.arange(seq_devices * LANE)
+    lane_order = (
+        (rows[None, :] // part == spots[:, None] // LANE)
+        & (rows[None, :] % part == spots[:, None] % LANE)
+    ).astype(np.float32)
+    return tuple(jnp.asarray(m, BF16) for m in (row_order, tile, cells, lane_order))
 
 
 def shards_fast(
@@ -1832,7 +1851,7 @@
     input_gate, input_bias, decay_logit, mixer_out, feed_gain, gate_weight, up_weight, down_weight,
     lengths, cotangent,
 ):
-    row_count = tokens.shape[0]
+    row_count, width = tokens.shape
     seq_devices = lax.axis_size("seq")
     shard_index = lax.axis_index("seq")
     ext_offsets = seq_offsets(lengths, shard_index * row_count, row_count + 8)
@@ -1841,81 +1860,36 @@
     lanes = scan_branch.shape[1]
     part = lanes // seq_devices
     groups = lanes // BW
-    flat = jnp.concatenate(
+    consts = placements(lanes, groups, seq_devices)
+    small = jnp.concatenate(
         [
-            kernel_taps.reshape(-1), kernel_bias, decay_bias, input_bias, decay_logit,
-            decay_gate.reshape(-1), input_gate.reshape(-1),
+            kernel_taps, kernel_bias[None], decay_bias[None], input_bias[None], decay_logit[None],
+            jnp.zeros((8, part), BF16),
         ]
     )
-    pack_rows = -(-flat.shape[0] // (128 * 16)) * 16
-    pack = jnp.pad(flat, (0, pack_rows * 128 - flat.shape[0])).reshape(pack_rows, 128)
+    small = jnp.pad(small, ((0, 0), (0, LANE - part)))
     gains = jnp.pad(
         jnp.concatenate([mix_gain, feed_gain]).astype(F32)[None, :], ((0, 7), (0, 0))
     )
-    tok_all, pack_all, gains_all, scan_w, gate_w, mix_w, ffn_gate = gather_first(
-        tokens, pack, gains, scan_branch, gate_branch, mixer_out, gate_weight
-    )
-    pack_all = pack_all.reshape(seq_devices, -1)
-    at = 0
-
-    def take(rows):
-        nonlocal at
-        piece = pack_all[:, at : at + rows * part].reshape(seq_devices, rows, part)
-        at += rows * part
-        return piece.transpose(1, 0, 2).reshape(rows, lanes).astype(F32)
-
-    taps_f = take(KW)
-    biases = take(3)
-    logit_f = take(1)
-    gate_cut = groups * BW * BW // seq_devices
-    mats = [
-        pack_all[:, at + i * gate_cut : at + (i + 1) * gate_cut]
-        .reshape(seq_devices, groups, BW // seq_devices, BW)
-        .transpose(1, 0, 2, 3)
-        .reshape(groups, BW, BW)
-        for i in range(2)
-    ]
-    gates_w = jnp.concatenate(
-        [
-            jnp.concatenate(
-                [jnp.pad(m[g], ((0, 0), (g * BW, lanes - (g + 1) * BW))) for g in range(groups)], 0
-            )
-            for m in mats
-        ],
-        1,
-    )
-    par = jnp.concatenate(
-        [
-            taps_f, biases, CD * jax.nn.softplus(-logit_f), CD * jax.nn.sigmoid(-logit_f),
-            jnp.zeros((7, lanes), F32),
-        ],
-        0,
-    )
-    half = gains.shape[1] // 2
-    gain_full = gains_all[:, :, 0, :].reshape(-1, 2, half).transpose(1, 0, 2).reshape(2, -1)
-    gain_full = jnp.pad(gain_full, ((0, 6), (0, 0)))
+    pad = ((0, 0), (0, 2 * LANE - BW))
+    gate_blocks = jnp.concatenate(
+        [jnp.pad(m.reshape(part, BW), pad) for m in (decay_gate, input_gate)], 1
+    )
     (
         normed_first, scan_pad, gate_rows, conv_rows, decay_rows, input_rows, hidden_state, mixed,
-        scale_first_rows, decay_sums, cot_full, up_w, down_w,
-    ) = recur_forward(
-        tok_all, scan_w, gate_w, gates_w, par, gain_full, masks, cotangent, up_weight, down_weight
-    )
-    width = tokens.shape[1]
-    own_feed = lax.dynamic_slice(
-        gain_full[1:2], (0, lax.axis_index("tp") * width), (1, width)
-    )
-    feed_own = jnp.broadcast_to(own_feed, (8, width))
-    (
-        resid, scales, coefs, bo_part, gs_part,
-        low_pair, cot_pair, mid_pair, gate_pair, up_pair,
-    ) = feed_forward(
-        mixed, mix_w, tokens, feed_own, ffn_gate, up_w, down_w, cot_full
+        scale_first_rows, decay_sums, par, gates_w, gain_own, scan_w, gate_w, mix_w, ffn_gate, up_w, down_w, cot_full,
+    ) = first_half(
+        tokens, cotangent, small, gains, gate_blocks, scan_branch, gate_branch, mixer_out, gate_weight,
+        up_weight, down_weight, masks, consts,
+    )
+    resid, scales, coefs, bo_part, gs_part, low_pair, cot_pair, mid_pair, gate_pair, up_pair = (
+        feed_forward(mixed, mix_w, tokens, gain_own, ffn_gate, up_w, down_w, cot_full)
     )
     grad_resid, grad_branch, block_out, feed_grads, gate_own, up_own, down_own, _ = back_feed(
-        resid, scales, coefs, cotangent, feed_own, gs_part, bo_part,
+        resid, scales, coefs, cotangent, gain_own, gs_part, bo_part,
         (low_pair, cot_pair, mid_pair, gate_pair, up_pair),
     )
-    gates_grad, sums, first_coefs, normed_pair, mixed_pair, branch_pair, scan_pair, gaterow_pair = (
+    gates_grad, sums, first_coefs, normed_twin, mixed_twin, branch_twin, scan_pair, gaterow_pair = (
         recur_back(
             grad_branch, mix_w, gate_rows, hidden_state, conv_rows, decay_rows, input_rows, scan_pad,
             masks, par, gates_w, scale_first_rows, normed_first, mixed,
@@ -1942,15 +1916,17 @@
     flat_grads = jnp.concatenate([*tiles, small, feed_part], 1)
     grad_rows = -(-flat_grads.shape[1] // (128 * 8)) * 8
     grad_pack = jnp.pad(flat_grads, ((0, 0), (0, grad_rows * 128 - flat_grads.shape[1])))
-    own_mix = lax.dynamic_slice(gain_full[0:1], (0, lax.axis_index("tp") * width), (1, width))
     tokens_grad, mix_grads, pack_sum, mix_own, scan_own, gaterow_own, _ = last_reduce(
         scan_w, gate_w, grad_resid, tokens, first_coefs, scale_first_rows,
-        jnp.broadcast_to(own_mix, (8, width)), scan_pair[0], gaterow_pair[0],
+        gain_own, scan_pair[0], gaterow_pair[0],
         grad_pack.reshape(seq_devices, grad_rows, 128),
-        (normed_pair, mixed_pair, branch_pair, scan_pair, gaterow_pair),
+        (
+            normed_first, normed_twin, mixed, mixed_twin, grad_branch, branch_twin, scan_pair,
+            gaterow_pair,
+        ),
     )
     pack_sum = pack_sum.reshape(-1)
-    gate_size = groups * gate_cut // groups
+    gate_size = part * BW
     cut_at = 2 * gate_size
     small_sum = pack_sum[cut_at : cut_at + 9 * part].reshape(9, part)
     feed_sum = pack_sum[cut_at + 9 * part : cut_at + 9 * part + mix_gain.shape[0]]

time: 845 us -> 624 us (0.74)
  the two profiles are of different devices: /device:TPU:0 before, /device:TPU:8 now
where the time goes in v3:
time: 624 us; the launch traced here: 617 us
  Pallas kernels  579 us (93%)
  local copies, waits for them, and re-layouts  28.8 us (5%)
  other arithmetic  7.39 us (1%)
    pallas_call x1, Pallas kernels, back_feed(): pl.pallas_call(back_kernel, out_shape=(struct((rows, width), F32), struct...  160 us
    pallas_call x1, Pallas kernels, first_half(): pl.pallas_call(first_kernel, out_shape=(struct((rows, features), BF16), s...  150 us
    pallas_call x1, Pallas kernels, feed_forward(): pl.pallas_call(feed_kernel, out_shape=(struct((rows, width), F32), struct...  137 us
    pallas_call x1, Pallas kernels, last_reduce(): pl.pallas_call(last_kernel, out_shape=(struct((rows, width), F32), struct...  90.6 us
    pallas_call x1, Pallas kernels, recur_back(): pl.pallas_call(recur_back_kernel, out_shape=(struct((lanes, 2 * lanes), F...  42.1 us

profile of v3, /device:TPU:8, one launch (start us, length us, event | category | flops | bytes accessed | tf_op | source)
XLA Modules:
  0.0 616.5 jit_solution(16018518380577199521)
XLA Ops:
  0.7 0.8 reduce-window.9
  1.5 0.7 bitcast_subtract_fusion
  2.2 0.8 concatenate.28
  2.9 0.6 pad.21.small
  3.5 1.3 fusion.6.gains
  4.9 0.1 select_reduce_fusion
  5.0 0.8 reshape.190
  5.8 0.8 reshape.191
  6.7 0.7 fusion.2.gate_blocks
  7.3 1.6 compare_convert_fusion.masks
  8.9 150.1 %first_half.1 = (bf16[768,2048]{1,0:T(8,128)(2,1)}, f32[776,640]{1,0:T(8,128)}, f32[768,640]{1,0:T(8,128)}, bf16[768,640]{1,0:T(8,128)(2,1)}, f32[768,640]{1,0:T...) custom-call(bf16[768,512]{1,0:T(8,128)(2,1)} %tok.5, ...), custom_call_target="tpu_custom_call" | custom-call | tf_op jit(solution)/shard_map/first_half/pallas_call | solution.py:912
  159.0 0.7 slice.95
  159.7 136.7 %feed_forward.1 = (f32[768,512]{1,0:T(8,128)}, f32[768,128]{1,0:T(8,128)}, f32[768,128]{1,0:T(8,128)}, bf16[6,4,128,512]{3,2,1,0:T(8,128)(2,1)}, bf16[6,4,128,51...) custom-call(bf16[768,640]{1,0:T(8,128)(2,1)} %get-tuple-element.69.m, ...), custom_call_target="tpu_custom_call" | custom-call | tf_op jit(solution)/shard_map/feed_forward/pallas_call | solution.py:1256
  296.4 159.7 %back_feed.1 = (f32[768,512]{1,0:T(8,128)}, bf16[768,2048]{1,0:T(8,128)(2,1)}, f32[768,512]{1,0:T(8,128)}, f32[8,512]{1,0:T(8,128)}, f32[256,1536]{1,0:T(8,128)}...) custom-call(f32[768,512]{1,0:T(8,128)} %get-tuple-element.76.resid, ...), custom_call_target="tpu_custom_call" | custom-call | tf_op jit(solution)/shard_map/back_feed/pallas_call | solution.py:1439
  456.1 42.1 %recur_back.1 = (f32[640,1280]{1,0:T(8,128)}, f32[8,640]{1,0:T(8,128)}, f32[768,128]{1,0:T(8,128)}, bf16[768,2048]{1,0:T(8,128)(2,1)}, bf16[768,640]{1,0:T(8,128...) custom-call(bf16[768,2048]{1,0:T(8,128)(2,1)} %get-tuple-element.90.low.low_src, ...), custom_call_target="tpu_custom_call" | custom-call | tf_op jit(solution)/shard_map/recur_back/pallas_call | solution.py:1665
  498.2 0.7 slice_reduce_fusion
  498.9 0.1 reshape_squeeze.3
  499.0 0.7 pad_maximum_fusion.2
  499.7 0.1 reshape.201
  499.8 0.1 reshape.202
  499.9 1.8 fusion.8
  501.7 0.1 stack.35
  501.9 0.1 stack.38
  502.0 0.1 stack.37
  502.1 0.1 stack.36
  502.3 0.1 stack.33
  502.4 0.1 stack.32
  502.5 0.1 stack.31
  502.6 0.1 stack.30
  502.8 0.1 concatenate.34
  502.9 0.0 copy-start.4
  502.9 0.1 pad_bitcast_fusion
  503.0 1.1 copy.53
  504.0 0.0 copy-start
  504.0 0.6 copy-done.4
  504.6 1.6 copy.49
  506.2 0.0 copy-done
  506.2 2.6 slice_bitcast_fusion
  508.9 90.6 %last_reduce.1 = (f32[768,512]{1,0:T(8,128)}, f32[8,512]{1,0:T(8,128)}, f32[208,128]{1,0:T(8,128)}, f32[256,640]{1,0:T(8,128)}, f32[256,640]{1,0:T(8,128)}, /*in...) custom-call(bf16[2048,640]{1,0:T(8,128)(2,1)} %get-tuple-element.87.scan_w, bf16[2048,640]{1,0:T(8,128)(2,1)} %get-tuple-element.88.gate_w, ...), custom_call_target="tpu_custom_call" | custom-call | tf_op jit(solution)/shard_map/last_reduce/pallas_call | solution.py:1802
  599.5 0.0 copy-start.3
  599.5 1.4 slice.113
  600.8 0.7 slice.97
  601.6 0.6 dynamic-slice_bitcast_fusion
  602.1 0.7 slice.108
  602.8 0.7 slice.99
  603.5 1.4 slice_multiply_fusion
  604.9 0.9 fusion.9
  605.8 0.6 reshape.208
  606.5 0.6 reshape.207
  607.1 0.0 copy-start.5
  607.1 2.3 copy.48
  609.4 0.0 copy-done.3
  609.4 1.1 copy.61
  610.5 0.0 copy-done.5
  610.5 0.0 copy-start.7
  610.5 1.1 copy.62
  611.7 0.4 copy-done.7
  612.1 0.8 copy.63
  612.9 0.0 copy-done.6
  612.9 0.8 copy.64
  613.8 0.0 copy-done.2
  613.8 1.1 copy.65
  614.9 0.0 copy-done.1
  614.9 1.1 copy.66
  (9 shorter events, 0.1 us)
Async XLA Ops:
  502.9 1.7 copy-start.4
  504.0 2.2 copy-start
  599.5 9.9 %copy-start.3 = (f32[768,512]{1,0:T(8,128)S(1)}, f32[768,512]{1,0:T(8,128)}, u32[]{:S(2)}) copy-start(f32[768,512]{1,0:T(8,128)} %get-tuple-element.209) | copy-start | bytes 4718596
  607.1 3.4 copy-start.5
  610.5 1.5 copy-start.7
  610.5 2.4 copy-start.6
  612.1 1.7 copy-start.2
  612.9 2.0 copy-start.1

commit v4 on v3

--- a/solution.py
+++ b/solution.py
@@ -663,13 +663,15 @@
 
 
 def first_kernel(
-    tok, cot, small, gains, gate_blocks, scan, gate, mix, ffn, up, down, masks,
+    tok, cot, small, gains, gate_blocks, scan, gate, mix, ffn, masks,
     row_order, tile, cells, lane_order,
-    normed, scan_rows, gate_rows, conv, decay_rows, input_rows, hidden, mixed, scales, decay_sum,
-    par, gates_w, gain_own, scan_w, gate_w, mix_all, ffn_all, up_all, down_all, cot_all,
+    normed_out, scan_rows_out, gate_rows_out, conv_out, decay_rows_out, input_rows_out, hidden_out,
+    mixed_out, scan_w_out, gate_w_out, gates_w_out,
+    scales, decay_sum, par, gain_own, mix_all, ffn_all, cot_all,
+    normed, scan_rows, gate_rows, conv, decay_rows, input_rows, hidden, mixed, scan_w, gate_w, gates_w,
     tok_all, small_all, gains_all, blocks_all, gain_full, kept, driven, slots,
     tok_send, tok_recv, cot_send, cot_recv, gain_send, gain_recv, plane_send, plane_recv,
-    small_send, small_recv, carry_send, carry_recv, halo_send, halo_recv, local,
+    small_send, small_recv, carry_send, carry_recv, halo_send, halo_recv, local, out_sem,
 ):
     s, z = lax.axis_index("seq"), lax.axis_index("tp")
     rows, width = tok.shape
@@ -696,8 +698,6 @@
             (gate, gate_w, rows_of),
             (mix, mix_all, columns_of),
             (ffn, ffn_all, rows_of),
-            (up, up_all, rows_of),
-            (down, down_all, columns_of),
         )
     ):
         size = own.shape[1] if make is columns_of else own.shape[0]
@@ -714,6 +714,19 @@
     ]
     keep = pltpu.make_async_copy(cot, cot_all.at[:, feature_columns(z, width)], local.at[6])
     keep.start()
+    outs = {
+        name: pltpu.make_async_copy(src, dst, out_sem.at[i])
+        for i, (name, src, dst) in enumerate(
+            (
+                ("normed", normed, normed_out), ("scan_rows", scan_rows, scan_rows_out),
+                ("gate_rows", gate_rows, gate_rows_out), ("conv", conv, conv_out),
+                ("decay_rows", decay_rows, decay_rows_out), ("input_rows", input_rows, input_rows_out),
+                ("hidden", hidden, hidden_out), ("mixed", mixed, mixed_out),
+                ("scan_w", scan_w, scan_w_out), ("gate_w", gate_w, gate_w_out),
+                ("gates_w", gates_w, gates_w_out),
+            )
+        )
+    }
     tok_all[:, feature_columns(z, width)] = tok[...]
     gains_all[z, s] = gains[...]
     small_all[s] = small[...]
@@ -751,8 +764,9 @@
     gain_line.forward(2, 0)
     planes[0].last()
     planes[1].last()
-    planes[4].start()
     gain_line.forward(3, 0)
+    for c in range(chunks):
+        cots.start(c)
     pick = lax.broadcasted_iota(jnp.int32, (LANE, LANE), 0)
     place = lax.broadcasted_iota(jnp.int32, (LANE, LANE), 1)
     cut = LANE // 2
@@ -773,10 +787,11 @@
     gain_own[0:2, :] = gain_full[0:2, feature_columns(z, width)]
     planes[0].arrive()
     planes[1].arrive()
+    for name in ("scan_w", "gate_w", "gates_w"):
+        outs[name].start()
 
     def project(c):
         toks.forward(3, c)
-        cots.start(c)
         at = chunk_rows(c)
         x = tok_all[at, :].astype(F32)
         scale = lax.rsqrt(jnp.sum(x * x, axis=1, keepdims=True) / features + EPSILON)
@@ -800,9 +815,10 @@
 
     planes[2].turn()
     planes[3].turn()
-    planes[5].start()
     decay_sum[...] = jnp.zeros_like(decay_sum)
     pl.when(jnp.logical_not(first))(lambda: halo.wait_recv())
+    for name in ("normed", "scan_rows", "gate_rows"):
+        outs[name].start()
 
     def gates(c):
         at = chunk_rows(c)
@@ -831,9 +847,10 @@
         cots.forward(1, c)
 
     each_chunk(chunks, gates)
+    for name in ("conv", "decay_rows", "input_rows"):
+        outs[name].start()
     planes[2].last()
     planes[3].last()
-    planes[4].turn()
     count = rows // SUBS
 
     def total_of(step, carry):
@@ -888,11 +905,10 @@
         cots.forward(2, c)
 
     each_chunk(chunks, mix)
-    planes[4].last()
-    planes[5].turn()
+    for name in ("hidden", "mixed"):
+        outs[name].start()
     for c in range(chunks):
         cots.forward(3, c)
-    planes[5].last()
     for plane in planes[2:]:
         plane.arrive()
     for plane in planes:
@@ -903,9 +919,11 @@
     gain_line.drain(0)
     pl.when(jnp.logical_not(final))(lambda: halo.wait_send())
     keep.wait()
-
-
-def first_half(tok, cot, small, gains, gate_blocks, scan, gate, mix, ffn, up, down, masks, consts):
+    for copy in outs.values():
+        copy.wait()
+
+
+def first_half(tok, cot, small, gains, gate_blocks, scan, gate, mix, ffn, masks, consts):
     rows, width = tok.shape
     features, lanes = width * LINE, gate.shape[1]
     chunks = rows // CHUNK
@@ -920,23 +938,24 @@
             struct((rows, lanes), F32),
             struct((rows + 8, lanes), F32),
             struct((rows, lanes), BF16),
+            struct((features, lanes), BF16),
+            struct((features, lanes), BF16),
+            struct((lanes, 2 * lanes), BF16),
             struct((rows, LANE), F32),
             struct((8, lanes), F32),
             struct((16, lanes), F32),
-            struct((lanes, 2 * lanes), BF16),
             struct((8, width), F32),
-            struct((features, lanes), BF16),
-            struct((features, lanes), BF16),
             struct((mix.shape[0], mix.shape[1] * PLANE), BF16),
             struct((ffn.shape[0] * PLANE, ffn.shape[1]), BF16),
-            struct((up.shape[0] * PLANE, up.shape[1]), BF16),
-            struct((down.shape[0], down.shape[1] * PLANE), BF16),
             struct((rows, features), BF16),
         ),
-        in_specs=[VM] * 16,
-        out_specs=[VM] * 15 + [ANY] * 5,
+        in_specs=[VM] * 14,
+        out_specs=[ANY] * 11 + [VM] * 4 + [ANY] * 3,
         scratch_shapes=[
-            vm(rows, features),
+            vm(rows, features), vm(rows + 8, lanes, kind=F32), vm(rows, lanes, kind=F32),
+            vm(rows, lanes), vm(rows, lanes, kind=F32), vm(rows, lanes, kind=F32),
+            vm(rows + 8, lanes, kind=F32), vm(rows, lanes), vm(features, lanes), vm(features, lanes),
+            vm(lanes, 2 * lanes), vm(rows, features),
             vm(PLANE, *small.shape), vm(LINE, PLANE, *gains.shape, kind=F32),
             vm(PLANE * gate_blocks.shape[0], gate_blocks.shape[1]), vm(8, features, kind=F32),
             vm(lanes // LANE, rows, LANE, kind=F32), vm(lanes // LANE, rows, LANE, kind=F32),
@@ -944,14 +963,60 @@
             dma(2, LINE - 1, chunks), dma(2, LINE - 1, chunks),
             dma(2, LINE - 1, chunks), dma(2, LINE - 1, chunks),
             dma(2, LINE - 1, 1), dma(2, LINE - 1, 1),
-            dma(6, 9), dma(6, 9), dma(3, 7), dma(3, 7), dma(7), dma(7),
-            pltpu.SemaphoreType.DMA, pltpu.SemaphoreType.DMA, dma(7),
+            dma(4, 9), dma(4, 9), dma(3, 7), dma(3, 7), dma(7), dma(7),
+            pltpu.SemaphoreType.DMA, pltpu.SemaphoreType.DMA, dma(7), dma(11),
         ],
         compiler_params=pltpu.CompilerParams(
             collective_id=0, has_side_effects=True, vmem_limit_bytes=60 << 20
         ),
         name="first_half",
-    )(tok, cot, small, gains, gate_blocks, scan, gate, mix, ffn, up, down, masks, *consts)
+    )(tok, cot, small, gains, gate_blocks, scan, gate, mix, ffn, masks, *consts)
+
+
+class WeightGrads:
+    def __init__(self, s, z, stage, land, own, send, recv, back):
+        self.s, self.z = s, z
+        self.stage, self.land, self.own = stage, land, own
+        self.send, self.recv, self.back_sem = send, recv, back
+
+    def owner(self, k):
+        return flip_all(self.s, 2 * (k + 1)) if k < 3 else self.s
+
+    def stage_of(self, k):
+        size = self.own.shape[0]
+        return self.stage.at[pl.ds(k * size, size)]
+
+    def copy(self, k):
+        return remote(
+            self.stage_of(k), self.land.at[k], self.send.at[k], self.recv.at[k],
+            (self.owner(k), self.z),
+        )
+
+    def block(self, k, left, right):
+        size = self.own.shape[0]
+        columns = feature_columns(self.owner(k), size)
+        value = dot_tn(left[:, columns], right[...])
+        if k == 3:
+            self.own[...] = value
+        else:
+            self.stage_of(k)[...] = value.astype(BF16)
+            self.copy(k).start()
+
+    def finish(self):
+        backs = [
+            pltpu.make_async_copy(self.land.at[k], self.stage_of(k), self.back_sem.at[k])
+            for k in range(3)
+        ]
+        for k in range(3):
+            self.copy(k).wait()
+            backs[k].start()
+        for back in backs:
+            back.wait()
+        self.own[...] += (
+            self.stage_of(0)[...].astype(F32)
+            + self.stage_of(1)[...].astype(F32)
+            + self.stage_of(2)[...].astype(F32)
+        )
 
 
 class LineReduce:
@@ -959,52 +1024,61 @@
         self.s, self.z, self.part, self.land = s, z, part, land
         self.send, self.recv = send, recv
 
-    def copy(self, way, me, o, c):
-        target = me + 1 - 2 * way
-        slot = LINE if way == 1 and o == target else o
+    def copy(self, o, target, slot, c):
         return remote(
             self.part.at[c, o],
             self.land.at[c, slot],
             self.send.at[o, c],
             self.recv.at[slot, c],
-            (self.s, self.z + 1 - 2 * way),
+            (self.s, self.z + target),
         )
 
     def got(self, slot, c):
         part = self.land.at[c, slot]
         remote(part, part, self.send.at[0, c], self.recv.at[slot, c], (self.s, self.z)).wait_recv()
 
-    def hop(self, level, c):
-        for way in range(2):
-            me = level if way == 0 else LINE - 1 - level
-            order = range(LINE - 1, me - 1, -1) if way == 0 else range(me + 1)
-
-            def work(way=way, me=me, order=order):
-                for o in order:
-                    slot = LINE if way == 1 and o == me else o
-                    if level > 0:
-                        self.got(slot, c)
-                    if o != me:
-                        if level > 0:
-                            self.part[c, o] = (
-                                self.part[c, o].astype(F32) + self.land[c, slot].astype(F32)
-                            ).astype(BF16)
-                        self.copy(way, me, o, c).start()
+    def start(self, c):
+        end = LINE - 1
+        pl.when(self.z == 0)(lambda: self.copy(end, 1, LINE, c).start())
+        pl.when(self.z == end)(lambda: self.copy(0, -1, LINE, c).start())
+        pl.when(self.z == 0)(lambda: self.copy(2, 2, 1, c).start())
+        pl.when(self.z == end)(lambda: self.copy(1, -2, 3, c).start())
+        for me in range(LINE):
+
+            def work(me=me):
+                if me < end:
+                    self.copy(me + 1, 1, 0, c).start()
+                if me > 0:
+                    self.copy(me - 1, -1, 2, c).start()
 
             pl.when(self.z == me)(work)
 
-    def landed(self, c, into):
-        @pl.when(self.z == 0)
-        def _():
-            into[...] = self.land[c, LINE].astype(F32)
-
-        @pl.when(self.z > 0)
-        def _():
-            into[...] = self.land[c, self.z].astype(F32)
-
-        @pl.when((self.z > 0) & (self.z < LINE - 1))
-        def _():
-            into[...] += self.land[c, LINE].astype(F32)
+    def forward(self, c):
+        end = LINE - 1
+        for me, o, step, slot in ((1, end, 2, 1), (2, 0, -2, 3)):
+
+            def work(o=o, step=step, slot=slot):
+                self.got(LINE, c)
+                self.part[c, o] = (
+                    self.part[c, o].astype(F32) + self.land[c, LINE].astype(F32)
+                ).astype(BF16)
+                self.copy(o, step, slot, c).start()
+
+            pl.when(self.z == me)(work)
+
+    def total(self, c, into):
+        slots = ((2, 3), (0, 2, 3), (0, 1, 2), (0, 1))
+        for me in range(LINE):
+
+            def work(me=me):
+                for slot in slots[me]:
+                    self.got(slot, c)
+                value = self.land[c, slots[me][0]].astype(F32)
+                for slot in slots[me][1:]:
+                    value = value + self.land[c, slot].astype(F32)
+                into[...] = value
+
+            pl.when(self.z == me)(work)
 
     def drain(self, c):
         for o in range(LINE):
@@ -1085,32 +1159,46 @@
 
 
 def feed_kernel(
-    mixed, mix_w, tok, gain, gate_w, up_w, down_w, cot,
-    resid, scales, coefs, bo_part, gs_part, low_pair, cot_pair, mid_pair, gate_pair, up_pair,
-    part, land, low, cots, mid, g_gate, g_up, bo_out, gs_out, gate_v, up_v, down_v,
-    acc, bo_acc, gs_acc, inner, squares, inners,
-    red_send, red_recv, line_send, line_recv, sq_send, sq_recv, in_send, in_recv,
-    own_sem, give_send, give_recv, out_sem, load_sem,
+    mixed, mix_w, tok, cot, gain, up, down, gate_w, cot_all,
+    resid, grad, gain_grad, down_own, ffn_own, lands, grad_all, bo_part, low_pair, cot_pair, mid_pair, gate_pair, up_pair,
+    part, land, low, low_grad, cots, mid, g_gate, g_up, bo_out, gate_v, up_v, down_v,
+    acc, inner, scales, squares, inners,
+    red_send, red_recv, gs_send, gs_recv, line_send, line_recv, grad_send, grad_recv,
+    sq_send, sq_recv, in_send, in_recv, plane_send, plane_recv, local,
+    own_sem, give_send, give_recv, out_sem, load_sem, w_send, w_recv, w_back,
 ):
     s, z = lax.axis_index("seq"), lax.axis_index("tp")
     rows, width = tok.shape
     chunks, features = rows // CHUNK, width * LINE
     loads = [
-        pltpu.make_async_copy(src, dst, load_sem.at[i])
-        for i, (src, dst) in enumerate(
-            ((gate_w, gate_v), (up_w, up_v), (down_w, down_v), (cot, cots))
-        )
+        pltpu.make_async_copy(gate_w, gate_v, load_sem.at[0]),
+        pltpu.make_async_copy(cot_all, cots, load_sem.at[1]),
     ]
     for load in loads:
         load.start()
     meet(s, z)
     red = LineReduce(s, z, part, land, red_send, red_recv)
-    line = LineGather(
-        s, z,
-        lambda c: low.at[chunk_rows(c), feature_columns(z, width)],
-        lambda o, c: low.at[chunk_rows(c), feature_columns(o, width)],
-        line_send, line_recv,
-    )
+    red_gs = LineReduce(s, z, part, land, gs_send, gs_recv)
+
+    def line_of(full, send, recv):
+        return LineGather(
+            s, z,
+            lambda c: full.at[chunk_rows(c), feature_columns(z, width)],
+            lambda o, c: full.at[chunk_rows(c), feature_columns(o, width)],
+            send, recv,
+        )
+
+    line = line_of(low, line_send, line_recv)
+    grads = line_of(low_grad, grad_send, grad_recv)
+    planes = [
+        PlaneGather(
+            s, z, up, *rows_of(up_v, up.shape[0]), plane_send.at[0], plane_recv.at[0], local.at[0]
+        ),
+        PlaneGather(
+            s, z, down, *columns_of(down_v, down.shape[1]), plane_send.at[1], plane_recv.at[1],
+            local.at[1],
+        ),
+    ]
     square_spread = LineSpread(s, z, lambda o, c: squares.at[o, c], sq_send, sq_recv)
     inner_spread = LineSpread(s, z, lambda o, c: inners.at[o, c], in_send, in_recv)
     pairs = [
@@ -1119,12 +1207,14 @@
             ((low, low_pair), (cots, cot_pair), (mid, mid_pair), (g_gate, gate_pair), (g_up, up_pair))
         )
     ]
-
-    def outs(c):
-        return [
-            pltpu.make_async_copy(bo_out.at[c], bo_part.at[c], out_sem.at[0, c]),
-            pltpu.make_async_copy(gs_out.at[c], gs_part.at[c], out_sem.at[1, c]),
-        ]
+    gain_grad[...] = jnp.zeros_like(gain_grad)
+
+    def bo_copy(c):
+        return pltpu.make_async_copy(bo_out.at[c], bo_part.at[c], out_sem.at[0, c])
+
+    def grad_copy(c):
+        at = chunk_rows(c)
+        return pltpu.make_async_copy(low_grad.at[at], grad_all.at[at], out_sem.at[1, c])
 
     def project(c):
         values = dot(mixed[chunk_rows(c), :], mix_w[...])
@@ -1136,15 +1226,16 @@
             def _(here=here):
                 resid[chunk_rows(c), :] = here
 
-        red.hop(0, c)
+        red.start(c)
 
     for c in range(AHEAD):
         project(c)
+    for plane in planes:
+        plane.start()
 
     def reduced(c):
         at = chunk_rows(c)
-        red.hop(3, c)
-        red.landed(c, acc)
+        red.total(c, acc)
         values = tok[at, :].astype(F32) + (resid[at, :] + acc[...])
         resid[at, :] = values
         squares[z, c] = as_row(jnp.sum(values * values, axis=1, keepdims=True))
@@ -1169,9 +1260,9 @@
         act, slope = gelu_pair(gate_pre)
         here = (act * up_pre).astype(BF16)
         mid[at, cols] = here
-        grad = dot_nt(cots[at, :], down_v[cols, :])
-        gate_grad = (grad * up_pre * slope).astype(BF16)
-        up_grad = (grad * act).astype(BF16)
+        back = dot_nt(cots[at, :], down_v[cols, :])
+        gate_grad = (back * up_pre * slope).astype(BF16)
+        up_grad = (back * act).astype(BF16)
         g_gate[at, cols] = gate_grad
         g_up[at, cols] = up_grad
         products = jnp.sum(
@@ -1182,73 +1273,165 @@
         else:
             inner[...] += products
 
-    def backward(cut, g):
+    def backward(g):
         at = group_rows(g)
-        cols = slice(cut * CUT, (cut + 1) * CUT)
-        block = dot(mid[at, cols], down_v[cols, :])
-        back = dot_nt(g_gate[at, cols], gate_v[:, cols]) + dot_nt(g_up[at, cols], up_v[:, cols])
-        if cut == 0:
-            bo_acc[...] = block
-            gs_acc[...] = back
-            return
-        block = bo_acc[...] + block
-        back = gs_acc[...] + back
+        back = dot_nt(g_gate[at, :], gate_v[...]) + dot_nt(g_up[at, :], up_v[...])
+        for k in range(GROUP // CHUNK):
+            c = g * (GROUP // CHUNK) + k
+            here = slice(k * CHUNK, (k + 1) * CHUNK)
+            red.drain(c)
+            for o in range(LINE):
+                part[c, o] = back[here, o * width : (o + 1) * width].astype(BF16)
+            red_gs.start(c)
+            inners[z, c] = as_row(inner[here, :])
+            inner_spread.start(c)
+        block = dot(mid[at, :], down_v[...])
         for k in range(GROUP // CHUNK):
             c = g * (GROUP // CHUNK) + k
             here = slice(k * CHUNK, (k + 1) * CHUNK)
             for o in range(LINE):
                 bo_out[c, o] = block[here, o * width : (o + 1) * width].astype(BF16)
-                gs_out[c, o] = back[here, o * width : (o + 1) * width].astype(BF16)
-            inners[z, c] = as_row(inner[here, :])
-            inner_spread.start(c)
             for pair in pairs:
                 pair.start(c)
-            for copy in outs(c):
+            bo_copy(c).start()
+
+    def turned(c):
+        at = chunk_rows(c)
+        red_gs.total(c, acc)
+        inner_spread.finish(c)
+        sums = inners[0, c] + inners[1, c] + inners[2, c] + inners[3, c]
+        scale = scales[at, :]
+        coef = scale * scale * as_columns(sums) / features
+        above = acc[...] + part[c, z].astype(F32)
+        scale, values = scale[:, 0:1], resid[at, :]
+        gain_grad[0:1, :] += jnp.sum(above * values * scale, axis=0, keepdims=True)
+        total = cot[at, :].astype(F32) + scale * gain[1:2, :] * above - values * coef[:, 0:1]
+        grad[at, :] = total
+        low_grad[at, feature_columns(z, width)] = total.astype(BF16)
+        grads.start(c)
+
+    def twice(start, body):
+        def both(t):
+            pl.when((t >= start) & (lax.rem(t - start, 2) == 0) & (t < start + chunks))(
+                lambda: (body(t - start), body(t - start + 1)) and None
+            )
+
+        return both
+
+    def whole(c):
+        grads.forward(3, c)
+        grad_copy(c).start()
+
+    left, rights = down_v, (gate_v, up_v)
+
+    def fill(i, src, dst):
+        return [
+            pltpu.make_async_copy(
+                src.at[half], dst.at[pl.ds(half * rows, rows)], load_sem.at[2 + 2 * i + half]
+            )
+            for half in range(2)
+        ]
+
+    fills = [
+        fill(0, cot_pair, left), fill(1, mid_pair, rights[0]),
+        fill(2, low_pair, left), fill(3, gate_pair, rights[1]),
+    ]
+    weights = [
+        WeightGrads(s, z, stage, lands.at[i], own, w_send.at[i], w_recv.at[i], w_back.at[i])
+        for i, (stage, own) in enumerate(((mid, down_own), (g_gate, ffn_own)))
+    ]
+
+    def ready_pairs(c):
+        for pair in pairs:
+            pair.drain(c)
+
+    def weigh(step):
+        @pl.when(step == 0)
+        def _():
+            each_chunk(chunks, ready_pairs)
+            for plane in planes:
+                plane.drain()
+            for i in (0, 1, 3):
+                for copy in fills[i]:
+                    copy.start()
+            for i in (0, 1):
+                for copy in fills[i]:
+                    copy.wait()
+            for k in range(4):
+                weights[0].block(k, left, rights[0].at[pl.ds(0, 2 * rows)])
+            for copy in fills[2]:
                 copy.start()
+
+        @pl.when(step == 1)
+        def _():
+            for i in (2, 3):
+                for copy in fills[i]:
+                    copy.wait()
+            for k in range(4):
+                weights[1].block(k, left, rights[1].at[pl.ds(0, 2 * rows)])
+
+    gs_one = twice(6, lambda c: red_gs.forward(c))
+    gs_three = twice(7, turned)
+    to_one = twice(8, lambda c: grads.forward(1, c))
+    to_two = twice(9, lambda c: grads.forward(2, c))
+    to_three = twice(10, whole)
 
     def turn(t, carry):
         g, odd = (t - 4) // 2, lax.rem(t, 2) == 1
-        ready = t >= 4
-        pl.when(t == 3)(lambda: [load.wait() for load in loads] and None)
-        in_range(t, chunks, lambda c: red.hop(1, c))
+        ready = (t >= 4) & (t < chunks + 4)
+
+        @pl.when(t == 2)
+        def _():
+            for plane in planes:
+                plane.turn()
+
+        @pl.when(t == 4)
+        def _():
+            for plane in planes:
+                plane.last()
+            for plane in planes:
+                plane.arrive()
+            for load in loads:
+                load.wait()
+
+        in_range(t, chunks, lambda c: red.forward(c))
+        gs_one(t)
         in_range(t - 2, chunks, lambda c: line.forward(1, c))
         in_range(t - 3, chunks, lambda c: line.forward(3, c))
+        to_one(t)
+        to_three(t)
         pl.when(ready & jnp.logical_not(odd))(lambda: forward(0, g))
-        pl.when(ready & odd)(lambda: forward(1, g))
+        gs_three(t)
         in_range(t - 1, chunks, reduced)
         in_range(t - 1, chunks, scaled)
         in_range(t - 2, chunks, lambda c: line.forward(2, c))
-        pl.when(ready & jnp.logical_not(odd))(lambda: backward(0, g))
-        in_range(t, chunks, lambda c: red.hop(2, c))
+        to_two(t)
+        pl.when(ready & jnp.logical_not(odd))(lambda: forward(1, g))
+        weigh(t - chunks - 4)
         in_range(t + AHEAD, chunks, project)
-        pl.when(ready & odd)(lambda: backward(1, g))
+        pl.when(ready & odd)(lambda: backward(g))
         return carry
 
-    lax.fori_loop(0, chunks + 4, turn, 0)
+    lax.fori_loop(0, chunks + 9, turn, 0)
 
     def close(c):
-        at = chunk_rows(c)
-        inner_spread.finish(c)
-        sums = inners[0, c] + inners[1, c] + inners[2, c] + inners[3, c]
-        scale = scales[at, :]
-        coefs[at, :] = scale * scale * as_columns(sums) / features
-        red.drain(c)
+        red_gs.drain(c)
         line.drain(c)
+        grads.drain(c)
         square_spread.drain(c)
         inner_spread.drain(c)
-        for pair in pairs:
-            pair.drain(c)
-        for copy in outs(c):
-            copy.wait()
+        bo_copy(c).wait()
+        grad_copy(c).wait()
 
     each_chunk(chunks, close)
-
-
-def feed_forward(mixed, mix_w, tok, gain, gate_w, up_w, down_w, cot):
+    for weight in weights:
+        weight.finish()
+
+
+def feed_both(mixed, mix_w, tok, cot, gain, up, down, gate_w, cot_all):
     rows, width = tok.shape
     features, hidden = width * LINE, gate_w.shape[1]
     chunks = rows // CHUNK
-    blocks = struct((chunks, LINE, CHUNK, width), BF16)
 
     def pair(size):
         return struct((2, rows, size), BF16)
@@ -1257,224 +1440,51 @@
         feed_kernel,
         out_shape=(
             struct((rows, width), F32),
-            struct((rows, LANE), F32),
-            struct((rows, LANE), F32),
-            blocks, blocks,
+            struct((rows, width), F32),
+            struct((8, width), F32),
+            struct((features // PLANE, hidden), F32),
+            struct((features // PLANE, hidden), F32),
+            struct((2, 3, features // PLANE, hidden), BF16),
+            struct((rows, features), BF16),
+            struct((chunks, LINE, CHUNK, width), BF16),
             pair(features), pair(features), pair(hidden), pair(hidden), pair(hidden),
         ),
-        in_specs=[VM] * 4 + [ANY] * 4,
-        out_specs=[VM] * 3 + [ANY] * 7,
+        in_specs=[VM] * 7 + [ANY] * 2,
+        out_specs=[VM] * 5 + [ANY] * 8,
         scratch_shapes=[
             vm(chunks, LINE, CHUNK, width), vm(chunks, LINE + 1, CHUNK, width),
-            vm(rows, features), vm(rows, features),
+            vm(rows, features), vm(rows, features), vm(rows, features),
             vm(rows, hidden), vm(rows, hidden), vm(rows, hidden),
-            vm(chunks, LINE, CHUNK, width), vm(chunks, LINE, CHUNK, width),
+            vm(chunks, LINE, CHUNK, width),
             vm(features, hidden), vm(features, hidden), vm(hidden, features),
-            vm(CHUNK, width, kind=F32), vm(GROUP, features, kind=F32),
-            vm(GROUP, features, kind=F32), vm(GROUP, 1, kind=F32),
+            vm(CHUNK, width, kind=F32), vm(GROUP, 1, kind=F32), vm(rows, LANE, kind=F32),
             vm(LINE, chunks, 8, LANE, kind=F32), vm(LINE, chunks, 8, LANE, kind=F32),
-            dma(LINE, chunks), dma(LINE + 1, chunks),
+            dma(LINE, chunks), dma(LINE + 1, chunks), dma(LINE, chunks), dma(LINE + 1, chunks),
+            dma(2, LINE - 1, chunks), dma(2, LINE - 1, chunks),
             dma(2, LINE - 1, chunks), dma(2, LINE - 1, chunks),
             dma(LINE - 1, chunks), dma(LINE - 1, chunks),
             dma(LINE - 1, chunks), dma(LINE - 1, chunks),
-            dma(5, chunks), dma(5, chunks), dma(5, chunks), dma(2, chunks), dma(4),
+            dma(2, 9), dma(2, 9), dma(2),
+            dma(5, chunks), dma(5, chunks), dma(5, chunks), dma(2, chunks), dma(10),
+            dma(2, 3), dma(2, 3), dma(2, 3),
         ],
         compiler_params=pltpu.CompilerParams(
-            collective_id=2, has_side_effects=True, vmem_limit_bytes=63 << 20
+            collective_id=2, has_side_effects=True, vmem_limit_bytes=64 << 20
         ),
-        name="feed_forward",
-    )(mixed, mix_w, tok, gain, gate_w, up_w, down_w, cot)
-
-
-class WeightGrads:
-    def __init__(self, s, z, stage, land, own, send, recv, back):
-        self.s, self.z = s, z
-        self.stage, self.land, self.own = stage, land, own
-        self.send, self.recv, self.back_sem = send, recv, back
-
-    def owner(self, k):
-        return flip_all(self.s, 2 * (k + 1)) if k < 3 else self.s
-
-    def copy(self, k):
-        return remote(
-            self.stage.at[k], self.land.at[k], self.send.at[k], self.recv.at[k],
-            (self.owner(k), self.z),
-        )
-
-    def block(self, k, left, right):
-        size = self.own.shape[0]
-        columns = feature_columns(self.owner(k), size)
-        value = dot_tn(left[:, columns], right[...])
-        if k == 3:
-            self.own[...] = value
-        else:
-            self.stage[k] = value.astype(BF16)
-            self.copy(k).start()
-
-    def finish(self):
-        backs = [
-            pltpu.make_async_copy(self.land.at[k], self.stage.at[k], self.back_sem.at[k])
-            for k in range(3)
-        ]
-        for k in range(3):
-            self.copy(k).wait()
-            backs[k].start()
-        for back in backs:
-            back.wait()
-        self.own[...] += (
-            self.stage[0].astype(F32) + self.stage[1].astype(F32) + self.stage[2].astype(F32)
-        )
-
-
-def back_kernel(
-    resid, scales, coefs, cot, gain, gs_part, bo_part, low_pair, cot_pair, mid_pair, gate_pair, up_pair,
-    grad, grad_all, out, gain_grad, gate_own, up_own, down_own, lands,
-    part, land, part_bo, land_bo, low, acc, left, right, stages,
-    red_send, red_recv, bo_send, bo_recv, line_send, line_recv, w_send, w_recv, w_back, load_sem, out_sem,
-):
-    s, z = lax.axis_index("seq"), lax.axis_index("tp")
-    rows, width = cot.shape
-    chunks = rows // CHUNK
-    loads = [
-        pltpu.make_async_copy(src, dst, load_sem.at[i])
-        for i, (src, dst) in enumerate(
-            (
-                (gs_part, part), (bo_part, part_bo),
-                (cot_pair, left.at[0]), (mid_pair, right.at[0]),
-                (low_pair, left.at[1]), (gate_pair, right.at[1]),
-            )
-        )
-    ]
-    late = pltpu.make_async_copy(up_pair, right.at[0], load_sem.at[6])
-    for load in loads:
-        load.start()
-    meet(s, z)
-    red = LineReduce(s, z, part, land, red_send, red_recv)
-    red_bo = LineReduce(s, z, part_bo, land_bo, bo_send, bo_recv)
-    line = LineGather(
-        s, z,
-        lambda c: low.at[chunk_rows(c), feature_columns(z, width)],
-        lambda o, c: low.at[chunk_rows(c), feature_columns(o, width)],
-        line_send, line_recv,
-    )
-    weights = [
-        WeightGrads(s, z, stages.at[i], lands.at[i], own, w_send.at[i], w_recv.at[i], w_back.at[i])
-        for i, own in enumerate((down_own, gate_own, up_own))
-    ]
-    gain_grad[...] = jnp.zeros_like(gain_grad)
-    loads[0].wait()
-    for c in range(AHEAD):
-        red.hop(0, c)
-    for load in loads[1:]:
-        load.wait()
-
-    def reduced(c):
-        at = chunk_rows(c)
-        red.hop(3, c)
-        red.landed(c, acc)
-        up = acc[...] + part[c, z].astype(F32)
-        scale, values = scales[at, 0:1], resid[at, :]
-        gain_grad[0:1, :] += jnp.sum(up * values * scale, axis=0, keepdims=True)
-        total = cot[at, :].astype(F32) + scale * gain[1:2, :] * up - values * coefs[at, 0:1]
-        grad[at, :] = total
-        low[at, feature_columns(z, width)] = total.astype(BF16)
-        line.start(c)
-
-    def result(c):
-        at = chunk_rows(c)
-        red_bo.hop(3, c)
-        red_bo.landed(c, acc)
-        out[at, :] = resid[at, :] + (acc[...] + part_bo[c, z].astype(F32))
-
-    def keep(c):
-        at = chunk_rows(c)
-        return pltpu.make_async_copy(low.at[at], grad_all.at[at], out_sem.at[c])
-
-    def arrived(c):
-        line.forward(3, c)
-        keep(c).start()
-
-    def weigh(t):
-        for k in range(4):
-            pl.when(t == k)(lambda k=k: weights[0].block(k, left.at[0], right.at[0]))
-            pl.when(t == 4 + k)(lambda k=k: weights[1].block(k, left.at[1], right.at[1]))
-            pl.when(t == 8 + k)(lambda k=k: weights[2].block(k, left.at[1], right.at[0]))
-        pl.when(t == 4)(lambda: late.start())
-        pl.when(t == 7)(lambda: late.wait())
-
-    def turn(t, carry):
-        in_range(t, chunks, lambda c: red.hop(1, c))
-        in_range(t - 2, chunks, lambda c: line.forward(1, c))
-        in_range(t - 3, chunks, arrived)
-        in_range(t - 5, chunks, lambda c: red_bo.hop(1, c))
-        weigh(t)
-        in_range(t - 1, chunks, reduced)
-        in_range(t - 2, chunks, lambda c: line.forward(2, c))
-        in_range(t - 6, chunks, result)
-        in_range(t, chunks, lambda c: red.hop(2, c))
-        in_range(t - 5, chunks, lambda c: red_bo.hop(2, c))
-        in_range(t + AHEAD, chunks, lambda c: red.hop(0, c))
-        in_range(t - 3, chunks, lambda c: red_bo.hop(0, c))
-        return carry
-
-    lax.fori_loop(0, chunks + 7, turn, 0)
-    for weight in weights:
-        weight.finish()
-
-    def close(c):
-        red.drain(c)
-        red_bo.drain(c)
-        line.drain(c)
-        keep(c).wait()
-
-    each_chunk(chunks, close)
-
-
-def back_feed(resid, scales, coefs, cot, gain, gs_part, bo_part, pairs):
-    rows, width = cot.shape
-    features, hidden = width * LINE, pairs[2].shape[2]
-    chunks, part = rows // CHUNK, features // PLANE
-    blocks = vm(chunks, LINE, CHUNK, width)
-    landing = vm(chunks, LINE + 1, CHUNK, width)
-    return pl.pallas_call(
-        back_kernel,
-        out_shape=(
-            struct((rows, width), F32),
-            struct((rows, features), BF16),
-            struct((rows, width), F32),
-            struct((8, width), F32),
-            struct((part, hidden), F32),
-            struct((part, hidden), F32),
-            struct((part, hidden), F32),
-            struct((3, 3, part, hidden), BF16),
-        ),
-        in_specs=[VM] * 5 + [ANY] * 7,
-        out_specs=[VM, ANY] + [VM] * 5 + [ANY],
-        scratch_shapes=[
-            blocks, landing, blocks, landing,
-            vm(rows, features), vm(CHUNK, width, kind=F32),
-            vm(2, 2 * rows, features), vm(2, 2 * rows, hidden), vm(3, 3, part, hidden),
-            dma(LINE, chunks), dma(LINE + 1, chunks), dma(LINE, chunks), dma(LINE + 1, chunks),
-            dma(2, LINE - 1, chunks), dma(2, LINE - 1, chunks),
-            dma(3, 3), dma(3, 3), dma(3, 3), dma(7), dma(chunks),
-        ],
-        compiler_params=pltpu.CompilerParams(
-            collective_id=3, has_side_effects=True, vmem_limit_bytes=63 << 20
-        ),
-        name="back_feed",
-    )(
-        resid, scales, coefs, cot, gain, gs_part, bo_part,
-        *[pair.reshape(2 * rows, pair.shape[2]) for pair in pairs],
-    )
+        name="feed_both",
+    )(mixed, mix_w, tok, cot, gain, up, down, gate_w, cot_all)
 
 
 def recur_back_kernel(
     low, mix_w, gate_rows, hidden, conv, decay_rows, input_rows, scan_rows, masks, par, gates_w, scales,
-    normed_src, mixed_src, low_src,
-    gates_grad, sums, coefs, normed_twin, mixed_twin, low_twin, scan_pair, gate_pair,
-    kept, grads, spilled, both, conv_grad, scan_low, gate_low, slots, inners,
+    resid, normed_src, mixed_src, low_src, bo_part, feed_pair, feed_up_pair,
+    gates_grad, sums, coefs, out, up_own,
+    normed_twin, mixed_twin, low_twin, scan_pair, gate_pair, lands,
+    kept, grads, both, conv_grad, scan_low, gate_low, slots, inners,
+    part, land, acc, left, right, stages,
     small_send, small_recv, halo_send, halo_recv, in_send, in_recv,
     own_sem, give_send, give_recv, twin_send, twin_recv,
+    bo_send, bo_recv, w_send, w_recv, w_back, load_sem,
 ):
     s, z = lax.axis_index("seq"), lax.axis_index("tp")
     rows, features = low.shape
@@ -1491,10 +1501,34 @@
         for i, (src, out) in enumerate(((scan_low, scan_pair), (gate_low, gate_pair)))
     ]
     inner_spread = LineSpread(s, z, lambda o, c: inners.at[o, c], in_send, in_recv)
+    loads = [
+        pltpu.make_async_copy(src, dst, load_sem.at[i])
+        for i, (src, dst) in enumerate(
+            (
+                (bo_part, part), (feed_pair, left), (feed_up_pair, right),
+            )
+        )
+    ]
+    for load in loads:
+        load.start()
     meet(s, z)
     for whole in wholes:
         whole.start()
     sums[...] = jnp.zeros_like(sums)
+    red = LineReduce(s, z, part, land, bo_send, bo_recv)
+    weight = WeightGrads(s, z, stages, lands, up_own, w_send, w_recv, w_back)
+    loads[0].wait()
+    for c in range(chunks):
+        red.start(c)
+
+    def result(c):
+        at = chunk_rows(c)
+        red.total(c, acc)
+        out[at, :] = resid[at, :] + (acc[...] + part[c, z].astype(F32))
+
+    def sum_on(t):
+        in_range(t, chunks, lambda c: red.forward(c))
+        in_range(t - 2, chunks, result)
 
     def start(g):
         at = group_rows(g)
@@ -1600,7 +1634,12 @@
         sums[5:6, :] += jnp.sum(grad_rows.astype(F32), axis=0, keepdims=True)
         sums[6:7, :] += jnp.sum(grad_input.astype(F32), axis=0, keepdims=True)
         sums[7:8, :] += jnp.sum(scaled, axis=0, keepdims=True)
-
+        for k in range(4):
+            pl.when(c == k)(lambda k=k: weight.block(k, left, right))
+        sum_on(c)
+
+    for load in loads[1:3]:
+        load.wait()
     each_chunk(chunks, gates)
     halo = remote(
         conv_grad.at[pl.ds(0, 8)], conv_grad.at[pl.ds(rows, 8)], halo_send, halo_recv,
@@ -1634,8 +1673,10 @@
         ] + gate_low[at, :].astype(F32) * gate_rows[at, :]
         inners[z, c] = as_row(jnp.sum(products, axis=1, keepdims=True))
         inner_spread.start(c)
+        sum_on(c + chunks)
 
     each_chunk(chunks, finish)
+    weight.finish()
 
     def close(c):
         at = chunk_rows(c)
@@ -1644,6 +1685,7 @@
         scale = scales[at, :]
         coefs[at, :] = scale * scale * as_columns(total) / features
         inner_spread.drain(c)
+        red.drain(c)
         for pair in pairs:
             pair.drain(c)
 
@@ -1654,10 +1696,10 @@
 
 
 def recur_back(low, mix_w, gate_rows, hidden, conv, decay_rows, input_rows, scan_rows, masks, par,
-               gates_w, scales, normed, mixed):
+               gates_w, scales, resid, normed, mixed, bo_part, pairs):
     rows, features = low.shape
-    lanes = gate_rows.shape[1]
-    chunks = rows // CHUNK
+    lanes, width = gate_rows.shape[1], resid.shape[1]
+    chunks, hidden_size, part = rows // CHUNK, pairs[1].shape[2], features // PLANE
 
     def pair(size):
         return struct((2, rows, size), BF16)
@@ -1668,27 +1710,34 @@
             struct((lanes, 2 * lanes), F32),
             struct((8, lanes), F32),
             struct((rows, LANE), F32),
+            struct((rows, width), F32),
+            struct((part, hidden_size), F32),
             struct((rows, features), BF16), struct((rows, lanes), BF16), struct((rows, features), BF16),
             pair(lanes), pair(lanes),
+            struct((3, part, hidden_size), BF16),
         ),
-        in_specs=[VM] * 12 + [ANY] * 3,
-        out_specs=[VM] * 3 + [ANY] * 5,
+        in_specs=[VM] * 13 + [ANY] * 6,
+        out_specs=[VM] * 5 + [ANY] * 6,
         scratch_shapes=[
             vm(lanes // LANE, rows, LANE, kind=F32), vm(lanes // LANE, rows, LANE, kind=F32),
-            vm(8, LANE, kind=F32),
             vm(rows, 2 * lanes), vm(rows + 8, lanes, kind=F32), vm(rows, lanes), vm(rows, lanes),
             vm(PLANE, 8, lanes, kind=F32), vm(LINE, chunks, 8, LANE, kind=F32),
+            vm(chunks, LINE, CHUNK, width), vm(chunks, LINE + 1, CHUNK, width),
+            vm(CHUNK, width, kind=F32),
+            vm(2 * rows, features), vm(2 * rows, hidden_size), vm(3 * part, hidden_size),
             dma(7), dma(7), pltpu.SemaphoreType.DMA, pltpu.SemaphoreType.DMA,
             dma(LINE - 1, chunks), dma(LINE - 1, chunks),
             dma(2, chunks), dma(2, chunks), dma(2, chunks), dma(3), dma(3),
+            dma(LINE, chunks), dma(LINE + 1, chunks), dma(3), dma(3), dma(3), dma(3),
         ],
         compiler_params=pltpu.CompilerParams(
-            collective_id=4, has_side_effects=True, vmem_limit_bytes=60 << 20
+            collective_id=4, has_side_effects=True, vmem_limit_bytes=64 << 20
         ),
         name="recur_back",
     )(
         low, mix_w, gate_rows, hidden, conv, decay_rows, input_rows, scan_rows, masks, par, gates_w,
-        scales, normed, mixed, low,
+        scales, resid, normed, mixed, low, bo_part,
+        *[pair.reshape(2 * rows, pair.shape[2]) for pair in pairs],
     )
 
 
@@ -1740,12 +1789,11 @@
             here = slice(k * CHUNK, (k + 1) * CHUNK)
             for o in range(LINE):
                 part[c, o] = values[here, o * width : (o + 1) * width].astype(BF16)
-            red.hop(0, c)
+            red.start(c)
 
     def reduced(c):
         at = chunk_rows(c)
-        red.hop(3, c)
-        red.landed(c, acc)
+        red.total(c, acc)
         up = acc[...] + part[c, z].astype(F32)
         scale, values = scales[at, 0:1], tok[at, :].astype(F32)
         gain_land[s, 0:1, :] += jnp.sum(up * values * scale, axis=0, keepdims=True)
@@ -1759,16 +1807,15 @@
 
     def weigh(t):
         for k in range(4):
-            pl.when(t == k)(lambda k=k: weights[1].block((k + 3) % 4, left.at[1], right.at[1]))
-            pl.when(t == k)(lambda k=k: weights[2].block((k + 3) % 4, left.at[1], right.at[2]))
+            pl.when(t == k)(lambda k=k: weights[1].block(k, left.at[1], right.at[1]))
+            pl.when(t == k)(lambda k=k: weights[2].block(k, left.at[1], right.at[2]))
             pl.when(t == 4 + k // 2)(lambda k=k: weights[0].block(k, left.at[0], right.at[0]))
 
     def turn(t, carry):
-        in_range(t, chunks, lambda c: red.hop(1, c))
+        in_range(t, chunks, lambda c: red.forward(c))
         pl.when((lax.rem(t, 2) == 0) & (t < chunks - 2))(lambda: project(t // 2 + 1))
         weigh(t)
         in_range(t - 1, chunks, reduced)
-        in_range(t, chunks, lambda c: red.hop(2, c))
         return carry
 
     lax.fori_loop(0, chunks + 1, turn, 0)
@@ -1815,7 +1862,8 @@
         scratch_shapes=[
             vm(chunks, LINE, CHUNK, width), vm(chunks, LINE + 1, CHUNK, width),
             vm(CHUNK, width, kind=F32),
-            vm(2, 2 * rows, features), vm(3, 2 * rows, lanes), vm(3, 3, part, lanes),
+            vm(2, 2 * rows, features), vm(3, 2 * rows, lanes),
+            vm(3, 3 * part, lanes),
             vm(*pack.shape, kind=F32), vm(PLANE, 8, width, kind=F32),
             dma(LINE, chunks), dma(LINE + 1, chunks),
             dma(3, 3), dma(3, 3), dma(3, 3), dma(8), dma(7), dma(7), dma(7), dma(7),
@@ -1877,23 +1925,24 @@
     )
     (
         normed_first, scan_pad, gate_rows, conv_rows, decay_rows, input_rows, hidden_state, mixed,
-        scale_first_rows, decay_sums, par, gates_w, gain_own, scan_w, gate_w, mix_w, ffn_gate, up_w, down_w, cot_full,
+        scan_w, gate_w, gates_w, scale_first_rows, decay_sums, par, gain_own, mix_w, ffn_gate, cot_full,
     ) = first_half(
         tokens, cotangent, small, gains, gate_blocks, scan_branch, gate_branch, mixer_out, gate_weight,
-        up_weight, down_weight, masks, consts,
-    )
-    resid, scales, coefs, bo_part, gs_part, low_pair, cot_pair, mid_pair, gate_pair, up_pair = (
-        feed_forward(mixed, mix_w, tokens, gain_own, ffn_gate, up_w, down_w, cot_full)
-    )
-    grad_resid, grad_branch, block_out, feed_grads, gate_own, up_own, down_own, _ = back_feed(
-        resid, scales, coefs, cotangent, gain_own, gs_part, bo_part,
-        (low_pair, cot_pair, mid_pair, gate_pair, up_pair),
-    )
-    gates_grad, sums, first_coefs, normed_twin, mixed_twin, branch_twin, scan_pair, gaterow_pair = (
-        recur_back(
-            grad_branch, mix_w, gate_rows, hidden_state, conv_rows, decay_rows, input_rows, scan_pad,
-            masks, par, gates_w, scale_first_rows, normed_first, mixed,
-        )
+        masks, consts,
+    )
+    (
+        resid, grad_resid, feed_grads, down_own, gate_own, _, grad_branch, bo_part,
+        low_pair, cot_pair, mid_pair, gate_pair, up_pair,
+    ) = feed_both(
+        mixed, mix_w, tokens, cotangent, gain_own, up_weight, down_weight, ffn_gate, cot_full
+    )
+    (
+        gates_grad, sums, first_coefs, block_out, up_own,
+        normed_twin, mixed_twin, branch_twin, scan_pair, gaterow_pair, _,
+    ) = recur_back(
+        grad_branch, mix_w, gate_rows, hidden_state, conv_rows, decay_rows, input_rows, scan_pad,
+        masks, par, gates_w, scale_first_rows, resid, normed_first, mixed, bo_part,
+        (low_pair, up_pair),
     )
 
     def own_parts(rows):

time: 624 us -> 570 us (0.913)
  the two profiles are of different devices: /device:TPU:8 before, /device:TPU:0 now
where the time goes in v4:
time: 570 us; the launch traced here: 561 us
  Pallas kernels  523 us (92%)
  local copies, waits for them, and re-layouts  29.4 us (5%)
  other arithmetic  7.41 us (1%)
    pallas_call x1, Pallas kernels, feed_both(): pl.pallas_call(feed_kernel, out_shape=(struct((rows, width), F32), struct...  256 us
    pallas_call x1, Pallas kernels, first_half(): pl.pallas_call(first_kernel, out_shape=(struct((rows, features), BF16), s...  119 us
    pallas_call x1, Pallas kernels, recur_back(): pl.pallas_call(recur_back_kernel, out_shape=(struct((lanes, 2 * lanes), F...  78.4 us
    pallas_call x1, Pallas kernels, last_reduce(): pl.pallas_call(last_kernel, out_shape=(struct((rows, width), F32), struct...  69.8 us
    unnamed x26, local copies, waits for them, and re-layouts  12.3 us

profile of v4, /device:TPU:0, one launch (start us, length us, event | category | flops | bytes accessed | tf_op | source)
XLA Modules:
  0.0 560.8 jit_solution(769598561883072189)
XLA Ops:
  0.7 0.8 reduce-window.9
  1.5 0.7 bitcast_subtract_fusion
  2.2 0.8 concatenate.28
  2.9 0.6 pad.21.small
  3.5 1.3 fusion.6.gains
  4.9 0.1 select_reduce_fusion
  5.0 0.8 reshape.181
  5.8 0.8 reshape.182
  6.7 0.7 fusion.2.gate_blocks
  7.3 1.6 compare_convert_fusion.masks
  8.9 118.7 %first_half.1 = (bf16[768,2048]{1,0:T(8,128)(2,1)}, f32[776,640]{1,0:T(8,128)}, f32[768,640]{1,0:T(8,128)}, bf16[768,640]{1,0:T(8,128)(2,1)}, f32[768,640]{1,0:T...) custom-call(bf16[768,512]{1,0:T(8,128)(2,1)} %tok.5, ...), custom_call_target="tpu_custom_call" | custom-call | tf_op jit(solution)/shard_map/first_half/pallas_call | solution.py:930
  127.6 1.3 slice.95
  128.9 256.1 %feed_both.1 = (f32[768,512]{1,0:T(8,128)}, f32[768,512]{1,0:T(8,128)}, f32[8,512]{1,0:T(8,128)}, f32[256,1536]{1,0:T(8,128)}, f32[256,1536]{1,0:T(8,128)}, /*in...) custom-call(bf16[768,640]{1,0:T(8,128)(2,1)} %get-tuple-element.61.m, ...), custom_call_target="tpu_custom_call" | custom-call | tf_op jit(solution)/shard_map/feed_both/pallas_call | solution.py:1439
  385.0 78.4 %recur_back.1 = (f32[640,1280]{1,0:T(8,128)}, f32[8,640]{1,0:T(8,128)}, f32[768,128]{1,0:T(8,128)}, f32[768,512]{1,0:T(8,128)}, f32[256,1536]{1,0:T(8,128)}, /*i...) custom-call(bf16[768,2048]{1,0:T(8,128)(2,1)} %get-tuple-element.66., ...), custom_call_target="tpu_custom_call" | custom-call | tf_op jit(solution)/shard_map/recur_back/pallas_call | solution.py:1707
  463.5 0.7 slice_reduce_fusion
  464.2 0.1 reshape_squeeze.3
  464.3 0.7 pad_maximum_fusion.2
  465.1 0.1 reshape.189
  465.2 0.1 reshape.190
  465.2 1.8 fusion.8
  467.1 0.1 stack.35
  467.2 0.1 stack.38
  467.3 0.1 stack.37
  467.4 0.1 stack.36
  467.6 0.1 stack.33
  467.7 0.1 stack.32
  467.8 0.1 stack.31
  468.0 0.1 stack.30
  468.1 0.1 concatenate.34
  468.3 0.1 pad_bitcast_fusion
  468.3 1.1 copy.53
  469.4 0.0 copy-start
  469.4 0.6 copy-done.4
  470.0 1.6 copy.49
  471.6 0.0 copy-done
  471.6 2.6 slice_bitcast_fusion
  474.2 69.8 %last_reduce.1 = (f32[768,512]{1,0:T(8,128)}, f32[8,512]{1,0:T(8,128)}, f32[208,128]{1,0:T(8,128)}, f32[256,640]{1,0:T(8,128)}, f32[256,640]{1,0:T(8,128)}, /*in...) custom-call(bf16[2048,640]{1,0:T(8,128)(2,1)} %get-tuple-element.82.scan_w, bf16[2048,640]{1,0:T(8,128)(2,1)} %get-tuple-element.83.gate_w, ...), custom_call_target="tpu_custom_call" | custom-call | tf_op jit(solution)/shard_map/last_reduce/pallas_call | solution.py:1849
  544.0 0.0 copy-start.3
  544.0 1.4 slice.113
  545.4 0.7 slice.97
  546.1 0.6 dynamic-slice_bitcast_fusion
  546.7 0.7 slice.108
  547.4 0.7 slice.99
  548.0 1.5 slice_multiply_fusion
  549.5 0.9 fusion.9
  550.4 0.6 reshape.196
  551.0 0.6 reshape.195
  551.7 0.0 copy-start.5
  551.7 2.3 copy.48
  553.9 0.0 copy-done.3
  553.9 1.1 copy.61
  555.1 0.0 copy-done.5
  555.1 0.0 copy-start.7
  555.1 0.0 copy-start.6
  555.1 1.1 copy.62
  556.2 0.4 copy-done.7
  556.6 0.0 copy-start.1
  556.6 0.8 copy.63
  557.5 0.0 copy-done.6
  557.5 0.8 copy.64
  558.3 0.0 copy-done.1
  558.3 1.1 copy.65
  559.5 0.0 copy-done.2
  559.5 1.1 copy.66
  (8 shorter events, 0.1 us)
Async XLA Ops:
  468.2 1.7 copy-start.4
  469.4 2.2 copy-start
  544.0 10.0 %copy-start.3 = (f32[768,512]{1,0:T(8,128)S(1)}, f32[768,512]{1,0:T(8,128)}, u32[]{:S(2)}) copy-start(f32[768,512]{1,0:T(8,128)} %get-tuple-element.193) | copy-start | bytes 4718596
  551.7 3.4 copy-start.5
  555.1 1.5 copy-start.7
  555.1 2.4 copy-start.6
  556.6 1.7 copy-start.1
  557.5 2.0 copy-start.2

commit v5 on v4

--- a/solution.py
+++ b/solution.py
@@ -974,49 +974,64 @@
 
 
 class WeightGrads:
-    def __init__(self, s, z, stage, land, own, send, recv, back):
+    def __init__(self, s, z, stage, land, adds, add_land, own, send, recv, load):
         self.s, self.z = s, z
-        self.stage, self.land, self.own = stage, land, own
-        self.send, self.recv, self.back_sem = send, recv, back
-
-    def owner(self, k):
-        return flip_all(self.s, 2 * (k + 1)) if k < 3 else self.s
+        self.stage, self.land, self.adds, self.add_land = stage, land, adds, add_land
+        self.own, self.send, self.recv, self.load = own, send, recv, load
+        self.size = own.shape[0]
+        self.near = (flip(s, 1), flip(s, 2))
 
     def stage_of(self, k):
-        size = self.own.shape[0]
-        return self.stage.at[pl.ds(k * size, size)]
+        return self.stage.at[pl.ds(k * self.size, self.size)]
 
     def copy(self, k):
-        return remote(
-            self.stage_of(k), self.land.at[k], self.send.at[k], self.recv.at[k],
-            (self.owner(k), self.z),
-        )
-
-    def block(self, k, left, right):
-        size = self.own.shape[0]
-        columns = feature_columns(self.owner(k), size)
-        value = dot_tn(left[:, columns], right[...])
-        if k == 3:
-            self.own[...] = value
+        half = self.size // 2
+        if k < 2:
+            src, dst = self.stage_of(k), self.land.at[k]
         else:
-            self.stage_of(k)[...] = value.astype(BF16)
-            self.copy(k).start()
+            src = self.stage.at[pl.ds(2 * self.size + (k - 2) * half, half)]
+            dst = self.add_land.at[pl.ds((k - 2) * half, half)]
+        return remote(src, dst, self.send.at[k], self.recv.at[k], (self.near[k % 2], self.z))
+
+    def product(self, owner, left, right):
+        return dot_tn(left[:, feature_columns(owner, self.size)], right[...])
+
+    def across(self, left, right):
+        self.stage_of(2)[...] = self.product(flip(self.near[0], 2), left, right).astype(BF16)
+        self.copy(2).start()
+        self.copy(3).start()
+
+    def beside(self, k, left, right):
+        half = self.size // 2
+        value = self.product(self.near[k], left, right)
+        mine, other = (pl.ds(half, half), slice(half, None)), slice(0, half)
+        if k == 1:
+            mine, other = (pl.ds(0, half), slice(0, half)), slice(half, None)
+        self.copy(3 - k).wait_recv()
+        back = pltpu.make_async_copy(
+            self.add_land.at[mine[0]], self.adds.at[mine[0]], self.load.at[2 + k]
+        )
+        back.start()
+        self.stage_of(k)[other, :] = value[other].astype(BF16)
+        back.wait()
+        self.stage_of(k)[mine[1], :] = (value[mine[1]] + self.adds[mine[0], :].astype(F32)).astype(BF16)
+        self.copy(k).start()
+
+    def mine(self, left, right):
+        self.own[...] = self.product(self.s, left, right)
 
     def finish(self):
-        backs = [
-            pltpu.make_async_copy(self.land.at[k], self.stage_of(k), self.back_sem.at[k])
-            for k in range(3)
-        ]
-        for k in range(3):
+        backs = []
+        for k in range(2):
             self.copy(k).wait()
+            self.copy(2 + k).wait_send()
+            backs.append(
+                pltpu.make_async_copy(self.land.at[k], self.stage_of(k), self.load.at[k])
+            )
             backs[k].start()
         for back in backs:
             back.wait()
-        self.own[...] += (
-            self.stage_of(0)[...].astype(F32)
-            + self.stage_of(1)[...].astype(F32)
-            + self.stage_of(2)[...].astype(F32)
-        )
+        self.own[...] += self.stage_of(0)[...].astype(F32) + self.stage_of(1)[...].astype(F32)
 
 
 class LineReduce:
@@ -1066,7 +1081,7 @@
 
             pl.when(self.z == me)(work)
 
-    def total(self, c, into):
+    def total(self, c, into, more=False):
         slots = ((2, 3), (0, 2, 3), (0, 1, 2), (0, 1))
         for me in range(LINE):
 
@@ -1076,7 +1091,7 @@
                 value = self.land[c, slots[me][0]].astype(F32)
                 for slot in slots[me][1:]:
                     value = value + self.land[c, slot].astype(F32)
-                into[...] = value
+                into[...] = into[...] + value if more else value
 
             pl.when(self.z == me)(work)
 
@@ -1151,6 +1166,7 @@
 
 CUT = 768
 AHEAD = 2
+THIRDS = 3
 GROUP = 2 * CHUNK
 
 
@@ -1160,12 +1176,12 @@
 
 def feed_kernel(
     mixed, mix_w, tok, cot, gain, up, down, gate_w, cot_all,
-    resid, grad, gain_grad, down_own, ffn_own, lands, grad_all, bo_part, low_pair, cot_pair, mid_pair, gate_pair, up_pair,
+    resid, grad, gain_grad, down_own, lands, adds, grad_all, bo_part, low_pair, cot_pair, mid_pair, gate_pair, up_pair,
     part, land, low, low_grad, cots, mid, g_gate, g_up, bo_out, gate_v, up_v, down_v,
     acc, inner, scales, squares, inners,
     red_send, red_recv, gs_send, gs_recv, line_send, line_recv, grad_send, grad_recv,
     sq_send, sq_recv, in_send, in_recv, plane_send, plane_recv, local,
-    own_sem, give_send, give_recv, out_sem, load_sem, w_send, w_recv, w_back,
+    own_sem, give_send, give_recv, out_sem, load_sem, w_send, w_recv, w_load,
 ):
     s, z = lax.axis_index("seq"), lax.axis_index("tp")
     rows, width = tok.shape
@@ -1322,53 +1338,36 @@
         grads.forward(3, c)
         grad_copy(c).start()
 
-    left, rights = down_v, (gate_v, up_v)
-
-    def fill(i, src, dst):
-        return [
-            pltpu.make_async_copy(
-                src.at[half], dst.at[pl.ds(half * rows, rows)], load_sem.at[2 + 2 * i + half]
-            )
-            for half in range(2)
-        ]
-
+    left, right = down_v, gate_v.at[pl.ds(0, 2 * rows)]
     fills = [
-        fill(0, cot_pair, left), fill(1, mid_pair, rights[0]),
-        fill(2, low_pair, left), fill(3, gate_pair, rights[1]),
+        pltpu.make_async_copy(
+            src.at[half], dst.at[pl.ds(half * rows, rows)], load_sem.at[2 + 2 * i + half]
+        )
+        for i, (src, dst) in enumerate(((cot_pair, left), (mid_pair, right)))
+        for half in range(2)
     ]
-    weights = [
-        WeightGrads(s, z, stage, lands.at[i], own, w_send.at[i], w_recv.at[i], w_back.at[i])
-        for i, (stage, own) in enumerate(((mid, down_own), (g_gate, ffn_own)))
-    ]
+    weight = WeightGrads(
+        s, z, mid, lands, g_up.at[pl.ds(0, features // PLANE)], adds, down_own, w_send, w_recv, w_load
+    )
 
     def ready_pairs(c):
         for pair in pairs:
             pair.drain(c)
 
-    def weigh(step):
-        @pl.when(step == 0)
-        def _():
-            each_chunk(chunks, ready_pairs)
-            for plane in planes:
-                plane.drain()
-            for i in (0, 1, 3):
-                for copy in fills[i]:
-                    copy.start()
-            for i in (0, 1):
-                for copy in fills[i]:
-                    copy.wait()
-            for k in range(4):
-                weights[0].block(k, left, rights[0].at[pl.ds(0, 2 * rows)])
-            for copy in fills[2]:
-                copy.start()
-
-        @pl.when(step == 1)
-        def _():
-            for i in (2, 3):
-                for copy in fills[i]:
-                    copy.wait()
-            for k in range(4):
-                weights[1].block(k, left, rights[1].at[pl.ds(0, 2 * rows)])
+    def weigh_one():
+        each_chunk(chunks, ready_pairs)
+        for plane in planes:
+            plane.drain()
+        for copy in fills:
+            copy.start()
+        for copy in fills:
+            copy.wait()
+        weight.across(left, right)
+        weight.mine(left, right)
+
+    def weigh_two():
+        weight.beside(0, left, right)
+        weight.beside(1, left, right)
 
     gs_one = twice(6, lambda c: red_gs.forward(c))
     gs_three = twice(7, turned)
@@ -1407,9 +1406,10 @@
         in_range(t - 2, chunks, lambda c: line.forward(2, c))
         to_two(t)
         pl.when(ready & jnp.logical_not(odd))(lambda: forward(1, g))
-        weigh(t - chunks - 4)
+        pl.when(t == chunks + 4)(weigh_one)
         in_range(t + AHEAD, chunks, project)
         pl.when(ready & odd)(lambda: backward(g))
+        pl.when(t == chunks + 5)(weigh_two)
         return carry
 
     lax.fori_loop(0, chunks + 9, turn, 0)
@@ -1424,8 +1424,7 @@
         grad_copy(c).wait()
 
     each_chunk(chunks, close)
-    for weight in weights:
-        weight.finish()
+    weight.finish()
 
 
 def feed_both(mixed, mix_w, tok, cot, gain, up, down, gate_w, cot_all):
@@ -1443,14 +1442,14 @@
             struct((rows, width), F32),
             struct((8, width), F32),
             struct((features // PLANE, hidden), F32),
-            struct((features // PLANE, hidden), F32),
-            struct((2, 3, features // PLANE, hidden), BF16),
+            struct((2, features // PLANE, hidden), BF16),
+            struct((features // PLANE, hidden), BF16),
             struct((rows, features), BF16),
             struct((chunks, LINE, CHUNK, width), BF16),
             pair(features), pair(features), pair(hidden), pair(hidden), pair(hidden),
         ),
         in_specs=[VM] * 7 + [ANY] * 2,
-        out_specs=[VM] * 5 + [ANY] * 8,
+        out_specs=[VM] * 4 + [ANY] * 9,
         scratch_shapes=[
             vm(chunks, LINE, CHUNK, width), vm(chunks, LINE + 1, CHUNK, width),
             vm(rows, features), vm(rows, features), vm(rows, features),
@@ -1466,7 +1465,7 @@
             dma(LINE - 1, chunks), dma(LINE - 1, chunks),
             dma(2, 9), dma(2, 9), dma(2),
             dma(5, chunks), dma(5, chunks), dma(5, chunks), dma(2, chunks), dma(10),
-            dma(2, 3), dma(2, 3), dma(2, 3),
+            dma(4), dma(4), dma(4),
         ],
         compiler_params=pltpu.CompilerParams(
             collective_id=2, has_side_effects=True, vmem_limit_bytes=64 << 20
@@ -1476,15 +1475,17 @@
 
 
 def recur_back_kernel(
-    low, mix_w, gate_rows, hidden, conv, decay_rows, input_rows, scan_rows, masks, par, gates_w, scales,
-    resid, normed_src, mixed_src, low_src, bo_part, feed_pair, feed_up_pair,
-    gates_grad, sums, coefs, out, up_own,
-    normed_twin, mixed_twin, low_twin, scan_pair, gate_pair, lands,
-    kept, grads, both, conv_grad, scan_low, gate_low, slots, inners,
-    part, land, acc, left, right, stages,
+    masks, par, gates_w,
+    low_src, mix_w_src, gate_rows_src, hidden_src, decay_rows_src, conv_src, input_rows_src, scan_rows_src,
+    scales, resid, normed_src, mixed_src, bo_part, feed_pair, feed_up_pair, feed_gate_pair,
+    gates_grad, sums, coefs, out, up_own, third_own,
+    normed_twin, mixed_twin, low_twin, scan_pair, gate_pair, lands, third_lands, adds, third_adds,
+    kept, grads, both, conv_grad, gate_low, slots, inners,
+    low, mix_w, gate_rows, hidden, decay_rows, conv, input_rows, scan_rows,
+    part, land, left, right, right_third, stages, stages_third, add_v, third_add_v,
     small_send, small_recv, halo_send, halo_recv, in_send, in_recv,
     own_sem, give_send, give_recv, twin_send, twin_recv,
-    bo_send, bo_recv, w_send, w_recv, w_back, load_sem,
+    bo_send, bo_recv, w_send, w_recv, w_load, load_sem,
 ):
     s, z = lax.axis_index("seq"), lax.axis_index("tp")
     rows, features = low.shape
@@ -1498,37 +1499,56 @@
     ]
     pairs = [
         Halves(s, z, src, out, own_sem.at[i], give_send.at[i], give_recv.at[i])
-        for i, (src, out) in enumerate(((scan_low, scan_pair), (gate_low, gate_pair)))
+        for i, (src, out) in enumerate(
+            ((both.at[:, pl.ds(0, lanes)], scan_pair), (gate_low, gate_pair))
+        )
     ]
     inner_spread = LineSpread(s, z, lambda o, c: inners.at[o, c], in_send, in_recv)
+    third = right_third.shape[1]
     loads = [
         pltpu.make_async_copy(src, dst, load_sem.at[i])
         for i, (src, dst) in enumerate(
             (
                 (bo_part, part), (feed_pair, left), (feed_up_pair, right),
+                (feed_gate_pair.at[:, pl.ds(0, third)], right_third),
+                (low_src, low), (mix_w_src, mix_w), (gate_rows_src, gate_rows),
+                (hidden_src, hidden), (decay_rows_src, decay_rows), (conv_src, conv),
+                (input_rows_src, input_rows), (scan_rows_src, scan_rows), (resid, out),
+                (scales, coefs),
             )
         )
     ]
-    for load in loads:
+    for load in loads[:1] + loads[4:] + loads[1:4]:
         load.start()
     meet(s, z)
     for whole in wholes:
         whole.start()
     sums[...] = jnp.zeros_like(sums)
     red = LineReduce(s, z, part, land, bo_send, bo_recv)
-    weight = WeightGrads(s, z, stages, lands, up_own, w_send, w_recv, w_back)
+    weights = [
+        WeightGrads(s, z, *refs, w_send.at[i], w_recv.at[i], w_load.at[i])
+        for i, refs in enumerate(
+            (
+                (stages, lands, add_v, adds, up_own),
+                (stages_third, third_lands, third_add_v, third_adds, third_own),
+            )
+        )
+    ]
     loads[0].wait()
     for c in range(chunks):
         red.start(c)
 
     def result(c):
         at = chunk_rows(c)
-        red.total(c, acc)
-        out[at, :] = resid[at, :] + (acc[...] + part[c, z].astype(F32))
+        red.total(c, out.at[at], True)
+        out[at, :] += part[c, z].astype(F32)
 
     def sum_on(t):
         in_range(t, chunks, lambda c: red.forward(c))
         in_range(t - 2, chunks, result)
+
+    for load in loads[4:9]:
+        load.wait()
 
     def start(g):
         at = group_rows(g)
@@ -1572,6 +1592,10 @@
     slots[s, 1:2, :] = whole[1]
     spread = Spread(s, z, lambda p: slots.at[p], small_send, small_recv)
     spread.start()
+    for load in loads[1:4]:
+        load.wait()
+    weights[0].across(left, right)
+    weights[1].across(left, right_third)
     spread.finish()
     entry = jnp.zeros((1, lanes), F32)
     for place in range(PLANE - 1, 0, -1):
@@ -1634,11 +1658,15 @@
         sums[5:6, :] += jnp.sum(grad_rows.astype(F32), axis=0, keepdims=True)
         sums[6:7, :] += jnp.sum(grad_input.astype(F32), axis=0, keepdims=True)
         sums[7:8, :] += jnp.sum(scaled, axis=0, keepdims=True)
-        for k in range(4):
-            pl.when(c == k)(lambda k=k: weight.block(k, left, right))
+        pl.when(c == 0)(lambda: weights[0].beside(0, left, right))
+        pl.when(c == 1)(lambda: weights[0].beside(1, left, right))
+        pl.when(c == 2)(lambda: weights[1].beside(0, left, right_third))
+        pl.when(c == 3)(lambda: weights[1].beside(1, left, right_third))
+        pl.when(c == 4)(lambda: weights[0].mine(left, right))
+        pl.when(c == 5)(lambda: weights[1].mine(left, right_third))
         sum_on(c)
 
-    for load in loads[1:3]:
+    for load in loads[9:]:
         load.wait()
     each_chunk(chunks, gates)
     halo = remote(
@@ -1666,7 +1694,7 @@
                 par[lag : lag + 1, :] * block[lag : lag + CHUNK, :]
             )
         grad = total.astype(BF16)
-        scan_low[at, :] = grad
+        both[at, 0:lanes] = grad
         pairs[0].start(c)
         products = grad.astype(F32) * scan_rows[
             pl.ds(pl.multiple_of(c * CHUNK + 8, 8), CHUNK), :
@@ -1676,13 +1704,14 @@
         sum_on(c + chunks)
 
     each_chunk(chunks, finish)
-    weight.finish()
+    for weight in weights:
+        weight.finish()
 
     def close(c):
         at = chunk_rows(c)
         inner_spread.finish(c)
         total = inners[0, c] + inners[1, c] + inners[2, c] + inners[3, c]
-        scale = scales[at, :]
+        scale = coefs[at, :]
         coefs[at, :] = scale * scale * as_columns(total) / features
         inner_spread.drain(c)
         red.drain(c)
@@ -1700,6 +1729,7 @@
     rows, features = low.shape
     lanes, width = gate_rows.shape[1], resid.shape[1]
     chunks, hidden_size, part = rows // CHUNK, pairs[1].shape[2], features // PLANE
+    two = hidden_size // THIRDS * (THIRDS - 1)
 
     def pair(size):
         return struct((2, rows, size), BF16)
@@ -1712,53 +1742,64 @@
             struct((rows, LANE), F32),
             struct((rows, width), F32),
             struct((part, hidden_size), F32),
+            struct((part, two), F32),
             struct((rows, features), BF16), struct((rows, lanes), BF16), struct((rows, features), BF16),
             pair(lanes), pair(lanes),
-            struct((3, part, hidden_size), BF16),
+            struct((2, part, hidden_size), BF16),
+            struct((2, part, two), BF16),
+            struct((part, hidden_size), BF16),
+            struct((part, two), BF16),
         ),
-        in_specs=[VM] * 13 + [ANY] * 6,
-        out_specs=[VM] * 5 + [ANY] * 6,
+        in_specs=[VM] * 3 + [ANY] * 16,
+        out_specs=[VM] * 6 + [ANY] * 9,
         scratch_shapes=[
             vm(lanes // LANE, rows, LANE, kind=F32), vm(lanes // LANE, rows, LANE, kind=F32),
-            vm(rows, 2 * lanes), vm(rows + 8, lanes, kind=F32), vm(rows, lanes), vm(rows, lanes),
+            vm(rows, 2 * lanes), vm(rows + 8, lanes, kind=F32), vm(rows, lanes),
             vm(PLANE, 8, lanes, kind=F32), vm(LINE, chunks, 8, LANE, kind=F32),
+            vm(rows, features), vm(lanes, features), vm(rows, lanes, kind=F32),
+            vm(rows + 8, lanes, kind=F32), vm(rows, lanes, kind=F32), vm(rows, lanes),
+            vm(rows, lanes, kind=F32), vm(rows + 8, lanes, kind=F32),
             vm(chunks, LINE, CHUNK, width), vm(chunks, LINE + 1, CHUNK, width),
-            vm(CHUNK, width, kind=F32),
-            vm(2 * rows, features), vm(2 * rows, hidden_size), vm(3 * part, hidden_size),
+            vm(2 * rows, features), vm(2 * rows, hidden_size), vm(2 * rows, two),
+            vm(3 * part, hidden_size), vm(3 * part, two),
+            vm(part, hidden_size), vm(part, two),
             dma(7), dma(7), pltpu.SemaphoreType.DMA, pltpu.SemaphoreType.DMA,
             dma(LINE - 1, chunks), dma(LINE - 1, chunks),
             dma(2, chunks), dma(2, chunks), dma(2, chunks), dma(3), dma(3),
-            dma(LINE, chunks), dma(LINE + 1, chunks), dma(3), dma(3), dma(3), dma(3),
+            dma(LINE, chunks), dma(LINE + 1, chunks), dma(2, 4), dma(2, 4), dma(2, 4), dma(14),
         ],
         compiler_params=pltpu.CompilerParams(
             collective_id=4, has_side_effects=True, vmem_limit_bytes=64 << 20
         ),
         name="recur_back",
     )(
-        low, mix_w, gate_rows, hidden, conv, decay_rows, input_rows, scan_rows, masks, par, gates_w,
-        scales, resid, normed, mixed, low, bo_part,
+        masks, par, gates_w, low, mix_w, gate_rows, hidden, decay_rows, conv, input_rows, scan_rows,
+        scales, resid, normed, mixed, bo_part,
         *[pair.reshape(2 * rows, pair.shape[2]) for pair in pairs],
     )
 
 
 def last_kernel(
-    scan_w, gate_w, grad, tok, coefs, scales, gain, scan_low, gate_low, pack,
+    scan_w, gate_w, grad, tok, coefs, scales, gain, pack,
     normed, normed_twin, mixed, mixed_twin, low, low_twin, scan_pair, gate_pair,
-    tokens_grad, gain_grad, pack_sum, mix_own, scan_own, gate_own, lands,
-    part, land, acc, left, right, stages, pack_land, gain_land,
-    red_send, red_recv, w_send, w_recv, w_back, load_sem, pack_send, pack_recv, gain_send, gain_recv,
+    feed_pair, feed_gate_pair,
+    tokens_grad, gain_grad, pack_sum, mix_own, scan_own, gate_own, third_own, lands, third_lands, adds, third_adds,
+    part, land, acc, left, right, right_third, stages, stages_third, add_v, third_add_v, pack_land, gain_land,
+    red_send, red_recv, w_send, w_recv, w_load, load_sem, pack_send, pack_recv, gain_send, gain_recv,
 ):
     s, z = lax.axis_index("seq"), lax.axis_index("tp")
     rows, width = tok.shape
     chunks = rows // CHUNK
+    third = right_third.shape[1]
     loads = [
         pltpu.make_async_copy(src, dst, load_sem.at[i])
         for i, (src, dst) in enumerate(
             (
-                (low, left.at[0, :rows]), (low_twin, left.at[0, rows:]),
+                (scan_pair, right.at[1]), (gate_pair, right.at[2]),
+                (normed, left.at[1, :rows]), (normed_twin, left.at[1, rows:]),
                 (mixed, right.at[0, :rows]), (mixed_twin, right.at[0, rows:]),
-                (normed, left.at[1, :rows]), (normed_twin, left.at[1, rows:]),
-                (scan_pair, right.at[1]), (gate_pair, right.at[2]),
+                (low, left.at[0, :rows]), (low_twin, left.at[0, rows:]), (feed_pair, left.at[2]),
+                (feed_gate_pair.at[:, pl.ds(2 * third, third)], right_third),
             )
         )
     ]
@@ -1776,14 +1817,23 @@
         copy.start()
     red = LineReduce(s, z, part, land, red_send, red_recv)
     weights = [
-        WeightGrads(s, z, stages.at[i], lands.at[i], own, w_send.at[i], w_recv.at[i], w_back.at[i])
+        WeightGrads(
+            s, z, stages.at[i], lands.at[i], add_v.at[i], adds.at[i], own,
+            w_send.at[i], w_recv.at[i], w_load.at[i],
+        )
         for i, own in enumerate((mix_own, scan_own, gate_own))
     ]
+    weights.append(
+        WeightGrads(
+            s, z, stages_third, third_lands, third_add_v, third_adds, third_own,
+            w_send.at[3], w_recv.at[3], w_load.at[3],
+        )
+    )
     gain_land[s] = jnp.zeros_like(gain_grad)
 
     def project(g):
         at = group_rows(g)
-        values = dot_nt(scan_low[at, :], scan_w[...]) + dot_nt(gate_low[at, :], gate_w[...])
+        values = dot_nt(right[1, at, :], scan_w[...]) + dot_nt(right[2, at, :], gate_w[...])
         for k in range(GROUP // CHUNK):
             c = g * (GROUP // CHUNK) + k
             here = slice(k * CHUNK, (k + 1) * CHUNK)
@@ -1801,19 +1851,30 @@
             grad[at, :] + scale * gain[0:1, :] * up - values * coefs[at, 0:1]
         )
 
+    for load in loads[:2]:
+        load.wait()
     project(0)
-    for load in loads:
+
+    for g in range(1, chunks * CHUNK // GROUP):
+        project(g)
+    for load in loads[2:]:
         load.wait()
+    factors = (
+        (left.at[0], right.at[0]), (left.at[1], right.at[1]), (left.at[1], right.at[2]),
+        (left.at[2], right_third),
+    )
+    for weight, pair in zip(weights[::-1], factors[::-1]):
+        weight.across(*pair)
+    for weight, pair in zip(weights[::-1], factors[::-1]):
+        weight.beside(0, *pair)
+        weight.beside(1, *pair)
 
     def weigh(t):
-        for k in range(4):
-            pl.when(t == k)(lambda k=k: weights[1].block(k, left.at[1], right.at[1]))
-            pl.when(t == k)(lambda k=k: weights[2].block(k, left.at[1], right.at[2]))
-            pl.when(t == 4 + k // 2)(lambda k=k: weights[0].block(k, left.at[0], right.at[0]))
+        for i in range(4):
+            pl.when(t == i)(lambda i=i: weights[i].mine(*factors[i]))
 
     def turn(t, carry):
         in_range(t, chunks, lambda c: red.forward(c))
-        pl.when((lax.rem(t, 2) == 0) & (t < chunks - 2))(lambda: project(t // 2 + 1))
         weigh(t)
         in_range(t - 1, chunks, reduced)
         return carry
@@ -1842,7 +1903,7 @@
     each_chunk(chunks, red.drain)
 
 
-def last_reduce(scan_w, gate_w, grad, tok, coefs, scales, gain, scan_low, gate_low, pack, pairs):
+def last_reduce(scan_w, gate_w, grad, tok, coefs, scales, gain, pack, pairs):
     rows, width = tok.shape
     features, lanes = width * LINE, scan_w.shape[1]
     chunks, part = rows // CHUNK, features // PLANE
@@ -1855,25 +1916,30 @@
             struct((part, lanes), F32),
             struct((part, lanes), F32),
             struct((part, lanes), F32),
-            struct((3, 3, part, lanes), BF16),
+            struct((part, pairs[9].shape[2] // THIRDS), F32),
+            struct((3, 2, part, lanes), BF16),
+            struct((2, part, pairs[9].shape[2] // THIRDS), BF16),
+            struct((3, part, lanes), BF16),
+            struct((part, pairs[9].shape[2] // THIRDS), BF16),
         ),
-        in_specs=[VM] * 10 + [ANY] * 8,
-        out_specs=[VM] * 6 + [ANY],
+        in_specs=[VM] * 8 + [ANY] * 10,
+        out_specs=[VM] * 7 + [ANY] * 4,
         scratch_shapes=[
             vm(chunks, LINE, CHUNK, width), vm(chunks, LINE + 1, CHUNK, width),
             vm(CHUNK, width, kind=F32),
-            vm(2, 2 * rows, features), vm(3, 2 * rows, lanes),
-            vm(3, 3 * part, lanes),
+            vm(3, 2 * rows, features), vm(3, 2 * rows, lanes), vm(2 * rows, pairs[9].shape[2] // THIRDS),
+            vm(3, 3 * part, lanes), vm(3 * part, pairs[9].shape[2] // THIRDS),
+            vm(3, part, lanes), vm(part, pairs[9].shape[2] // THIRDS),
             vm(*pack.shape, kind=F32), vm(PLANE, 8, width, kind=F32),
             dma(LINE, chunks), dma(LINE + 1, chunks),
-            dma(3, 3), dma(3, 3), dma(3, 3), dma(8), dma(7), dma(7), dma(7), dma(7),
+            dma(4, 4), dma(4, 4), dma(4, 4), dma(10), dma(7), dma(7), dma(7), dma(7),
         ],
         compiler_params=pltpu.CompilerParams(
             collective_id=5, has_side_effects=True, vmem_limit_bytes=63 << 20
         ),
         name="last_reduce",
     )(
-        scan_w, gate_w, grad, tok, coefs, scales, gain, scan_low, gate_low, pack,
+        scan_w, gate_w, grad, tok, coefs, scales, gain, pack,
         *pairs[:6],
         *[pair.reshape(2 * rows, pair.shape[2]) for pair in pairs[6:]],
     )
@@ -1931,18 +1997,18 @@
         masks, consts,
     )
     (
-        resid, grad_resid, feed_grads, down_own, gate_own, _, grad_branch, bo_part,
+        resid, grad_resid, feed_grads, down_own, _, _, grad_branch, bo_part,
         low_pair, cot_pair, mid_pair, gate_pair, up_pair,
     ) = feed_both(
         mixed, mix_w, tokens, cotangent, gain_own, up_weight, down_weight, ffn_gate, cot_full
     )
     (
-        gates_grad, sums, first_coefs, block_out, up_own,
-        normed_twin, mixed_twin, branch_twin, scan_pair, gaterow_pair, _,
+        gates_grad, sums, first_coefs, block_out, up_own, third_b,
+        normed_twin, mixed_twin, branch_twin, scan_pair, gaterow_pair, *_,
     ) = recur_back(
         grad_branch, mix_w, gate_rows, hidden_state, conv_rows, decay_rows, input_rows, scan_pad,
         masks, par, gates_w, scale_first_rows, resid, normed_first, mixed, bo_part,
-        (low_pair, up_pair),
+        (low_pair, up_pair, gate_pair),
     )
 
     def own_parts(rows):
@@ -1965,13 +2031,13 @@
     flat_grads = jnp.concatenate([*tiles, small, feed_part], 1)
     grad_rows = -(-flat_grads.shape[1] // (128 * 8)) * 8
     grad_pack = jnp.pad(flat_grads, ((0, 0), (0, grad_rows * 128 - flat_grads.shape[1])))
-    tokens_grad, mix_grads, pack_sum, mix_own, scan_own, gaterow_own, _ = last_reduce(
+    tokens_grad, mix_grads, pack_sum, mix_own, scan_own, gaterow_own, third_c, *_ = last_reduce(
         scan_w, gate_w, grad_resid, tokens, first_coefs, scale_first_rows,
-        gain_own, scan_pair[0], gaterow_pair[0],
+        gain_own,
         grad_pack.reshape(seq_devices, grad_rows, 128),
         (
             normed_first, normed_twin, mixed, mixed_twin, grad_branch, branch_twin, scan_pair,
-            gaterow_pair,
+            gaterow_pair, low_pair, gate_pair,
         ),
     )
     pack_sum = pack_sum.reshape(-1)
@@ -1997,7 +2063,7 @@
         small_sum[KW + 3],
         mix_own.T,
         feed_sum,
-        gate_own,
+        jnp.concatenate([third_b, third_c], axis=1),
         up_own,
         down_own.T,
         small_sum[KW + 4] / (row_count * seq_devices),

time: 570 us -> 530 us (0.930)
  Pallas kernels: 523 us -> 486 us
    pallas_call x1, Pallas kernels: 256 us -> 224 us  [feed_both(): pl.pallas_call(feed_kernel, out_shape=(struct((rows, width), F32), struct...]
    pallas_call x1, Pallas kernels: 78.4 us -> 69.5 us  [recur_back(): pl.pallas_call(recur_back_kernel, out_shape=(struct((lanes, 2 * lanes), F...]
    unnamed x26 -> x21, local copies, waits for them, and re-layouts: 12.3 us -> 11.4 us
where the time goes in v5:
time: 530 us; the launch traced here: 523 us
  Pallas kernels  486 us (92%)
  local copies, waits for them, and re-layouts  25.7 us (5%)
  other arithmetic  10.2 us (2%)
    pallas_call x1, Pallas kernels, feed_both(): pl.pallas_call(feed_kernel, out_shape=(struct((rows, width), F32), struct...  224 us
    pallas_call x1, Pallas kernels, first_half(): pl.pallas_call(first_kernel, out_shape=(struct((rows, features), BF16), s...  119 us
    pallas_call x1, Pallas kernels, last_reduce(): pl.pallas_call(last_kernel, out_shape=(struct((rows, width), F32), struct...  72.9 us
    pallas_call x1, Pallas kernels, recur_back(): pl.pallas_call(recur_back_kernel, out_shape=(struct((lanes, 2 * lanes), F...  69.5 us
    unnamed x21, local copies, waits for them, and re-layouts  11.4 us

profile of v5, /device:TPU:0, one launch (start us, length us, event | category | flops | bytes accessed | tf_op | source)
XLA Modules:
  0.0 522.6 jit_solution(453085084475686070)
XLA Ops:
  0.7 0.8 reduce-window.9
  1.5 0.7 bitcast_subtract_fusion
  2.2 0.8 concatenate.31
  2.9 0.6 pad.21.small
  3.5 1.3 fusion.6.gains
  4.9 0.1 select_reduce_fusion
  5.0 0.8 reshape.188
  5.8 0.8 reshape.189
  6.7 0.7 fusion.2.gate_blocks
  7.3 1.6 compare_convert_fusion.masks
  8.9 118.7 %first_half.1 = (bf16[768,2048]{1,0:T(8,128)(2,1)}, f32[776,640]{1,0:T(8,128)}, f32[768,640]{1,0:T(8,128)}, bf16[768,640]{1,0:T(8,128)(2,1)}, f32[768,640]{1,0:T...) custom-call(bf16[768,512]{1,0:T(8,128)(2,1)} %tok.5, ...), custom_call_target="tpu_custom_call" | custom-call | tf_op jit(solution)/shard_map/first_half/pallas_call | solution.py:930
  127.6 1.3 slice.87
  128.9 224.5 %feed_both.1 = (f32[768,512]{1,0:T(8,128)}, f32[768,512]{1,0:T(8,128)}, f32[8,512]{1,0:T(8,128)}, f32[256,1536]{1,0:T(8,128)}, bf16[2,256,1536]{2,1,0:T(8,128)(2...) custom-call(bf16[768,640]{1,0:T(8,128)(2,1)} %get-tuple-element.65.m, ...), custom_call_target="tpu_custom_call" | custom-call | tf_op jit(solution)/shard_map/feed_both/pallas_call | solution.py:1438
  353.4 69.5 %recur_back.1 = (f32[640,1280]{1,0:T(8,128)}, f32[8,640]{1,0:T(8,128)}, f32[768,128]{1,0:T(8,128)}, f32[768,512]{1,0:T(8,128)}, f32[256,1536]{1,0:T(8,128)}, /*i...) custom-call(f32[776,8]{1,0:T(8,128)} %compare_convert_fusion.masks, ...), custom_call_target="tpu_custom_call" | custom-call | tf_op jit(solution)/shard_map/recur_back/pallas_call | solution.py:1737
  422.9 0.7 slice_reduce_fusion
  423.6 0.1 reshape_squeeze.3
  423.7 0.7 pad_maximum_fusion.3
  424.4 0.1 reshape.195
  424.5 0.1 reshape.196
  424.6 1.8 fusion.8
  426.5 0.1 stack.35
  426.6 0.1 stack.38
  426.7 0.1 stack.37
  426.8 0.1 stack.36
  427.0 0.1 stack.33
  427.1 0.1 stack.32
  427.2 0.1 stack.31
  427.3 0.1 stack.30
  427.5 0.1 concatenate.37
  427.6 0.1 pad_bitcast_fusion
  427.7 1.1 copy.53
  428.8 72.9 %last_reduce.1 = (f32[768,512]{1,0:T(8,128)}, f32[8,512]{1,0:T(8,128)}, f32[208,128]{1,0:T(8,128)}, f32[256,640]{1,0:T(8,128)}, f32[256,640]{1,0:T(8,128)}, /*in...) custom-call(bf16[2048,640]{1,0:T(8,128)(2,1)} %get-tuple-element.85., ...), custom_call_target="tpu_custom_call" | custom-call | tf_op jit(solution)/shard_map/last_reduce/pallas_call | solution.py:1910
  501.6 1.3 slice.105
  502.9 0.7 slice.89
  503.6 0.6 dynamic-slice_bitcast_fusion
  504.2 0.7 slice.100
  504.9 0.7 slice.91
  505.5 1.4 slice_multiply_fusion
  507.0 0.9 fusion.9
  507.9 0.6 reshape.202
  508.5 0.6 reshape.201
  509.2 0.0 copy-start
  509.2 2.8 pad_maximum_fusion
  511.9 0.0 copy-start.2
  511.9 2.3 copy.48
  514.2 0.0 copy-done
  514.2 1.6 copy.49
  515.8 0.0 copy-done.2
  515.8 0.0 copy-start.3
  515.8 1.1 copy.60
  517.0 0.8 copy-done.3
  517.8 0.0 copy-start.5
  517.8 0.0 copy-start.4
  517.8 1.1 copy.61
  519.0 0.4 copy-done.5
  519.4 0.0 copy-start.1
  519.4 0.8 copy.62
  520.2 0.0 copy-done.4
  520.2 0.8 copy.63
  521.0 0.0 copy-done.1
  521.0 1.1 copy.64
  (6 shorter events, 0.1 us)
Async XLA Ops:
  509.2 5.1 copy-start
  511.9 3.9 copy-start.2
  515.8 2.0 copy-start.3
  517.8 1.5 copy-start.5
  517.8 2.4 copy-start.4
  519.4 1.7 copy-start.1

commit v6 on v5

--- a/solution.py
+++ b/solution.py
@@ -744,8 +744,6 @@
     for c in range(chunks):
         toks.forward(1, c)
     gain_line.forward(1, 0)
-    planes[2].start()
-    planes[3].start()
     placed = dot(
         jnp.concatenate([small_all[p] for p in range(PLANE)], axis=1), lane_order[...]
     )
@@ -759,6 +757,8 @@
         gates_w[:, i * lanes : (i + 1) * lanes] = dot(row_order[...], wide).astype(BF16) * cells[...]
     planes[0].turn()
     planes[1].turn()
+    planes[2].start()
+    planes[3].start()
     for c in range(chunks):
         toks.forward(2, c)
     gain_line.forward(2, 0)
@@ -792,6 +792,7 @@
 
     def project(c):
         toks.forward(3, c)
+        pl.when(c >= 2)(lambda: cots.forward(1, c - 2))
         at = chunk_rows(c)
         x = tok_all[at, :].astype(F32)
         scale = lax.rsqrt(jnp.sum(x * x, axis=1, keepdims=True) / features + EPSILON)
@@ -844,7 +845,8 @@
         put(kept, at, goes_on * decay)
         put(driven, at, multiplier * sigmoid(inputs) * low.astype(F32))
         decay_sum[0:1, :] += jnp.sum(decay, axis=0, keepdims=True)
-        cots.forward(1, c)
+        pl.when(c < 2)(lambda: cots.forward(1, c + chunks - 2))
+        pl.when(c >= 2)(lambda: cots.forward(2, c - 2))
 
     each_chunk(chunks, gates)
     for name in ("conv", "decay_rows", "input_rows"):
@@ -902,7 +904,7 @@
         now = get(driven, at)
         hidden[pl.ds(pl.multiple_of(c * CHUNK + 8, 8), CHUNK), :] = now
         mixed[at, :] = (gelu_of(gate_rows[at, :]) * now).astype(BF16)
-        cots.forward(2, c)
+        pl.when(c < 2)(lambda: cots.forward(2, c + chunks - 2))
 
     each_chunk(chunks, mix)
     for name in ("hidden", "mixed"):
@@ -1053,9 +1055,16 @@
         remote(part, part, self.send.at[0, c], self.recv.at[slot, c], (self.s, self.z)).wait_recv()
 
     def start(self, c):
+        self.start_ends(c)
+        self.start_rest(c)
+
+    def start_ends(self, c):
         end = LINE - 1
         pl.when(self.z == 0)(lambda: self.copy(end, 1, LINE, c).start())
         pl.when(self.z == end)(lambda: self.copy(0, -1, LINE, c).start())
+
+    def start_rest(self, c):
+        end = LINE - 1
         pl.when(self.z == 0)(lambda: self.copy(2, 2, 1, c).start())
         pl.when(self.z == end)(lambda: self.copy(1, -2, 3, c).start())
         for me in range(LINE):
@@ -1401,15 +1410,15 @@
         to_three(t)
         pl.when(ready & jnp.logical_not(odd))(lambda: forward(0, g))
         gs_three(t)
+        pl.when(t == chunks + 5)(weigh_one)
         in_range(t - 1, chunks, reduced)
         in_range(t - 1, chunks, scaled)
         in_range(t - 2, chunks, lambda c: line.forward(2, c))
         to_two(t)
         pl.when(ready & jnp.logical_not(odd))(lambda: forward(1, g))
-        pl.when(t == chunks + 4)(weigh_one)
         in_range(t + AHEAD, chunks, project)
         pl.when(ready & odd)(lambda: backward(g))
-        pl.when(t == chunks + 5)(weigh_two)
+        pl.when(t == chunks + 6)(weigh_two)
         return carry
 
     lax.fori_loop(0, chunks + 9, turn, 0)
@@ -1536,7 +1545,9 @@
     ]
     loads[0].wait()
     for c in range(chunks):
-        red.start(c)
+        red.start_ends(c)
+    for c in range(chunks):
+        red.start_rest(c)
 
     def result(c):
         at = chunk_rows(c)
@@ -1839,7 +1850,7 @@
             here = slice(k * CHUNK, (k + 1) * CHUNK)
             for o in range(LINE):
                 part[c, o] = values[here, o * width : (o + 1) * width].astype(BF16)
-            red.start(c)
+            red.start_ends(c)
 
     def reduced(c):
         at = chunk_rows(c)
@@ -1857,6 +1868,8 @@
 
     for g in range(1, chunks * CHUNK // GROUP):
         project(g)
+    for c in range(chunks):
+        red.start_rest(c)
     for load in loads[2:]:
         load.wait()
     factors = (
@@ -1872,6 +1885,7 @@
     def weigh(t):
         for i in range(4):
             pl.when(t == i)(lambda i=i: weights[i].mine(*factors[i]))
+            pl.when(t == chunks - 1 + i // 2)(lambda i=i: weights[3 - i].finish())
 
     def turn(t, carry):
         in_range(t, chunks, lambda c: red.forward(c))
@@ -1891,8 +1905,6 @@
     for bits in range(1, PLANE):
         total = total + pack_land[flip_all(s, bits)]
     pack_sum[...] = total
-    for weight in weights:
-        weight.finish()
     gain_spread.finish()
     total = gain_land[0]
     for place in range(1, PLANE):

time: 530 us -> 524 us (0.989)
  Pallas kernels: 486 us -> 479 us
where the time goes in v6:
time: 524 us; the launch traced here: 516 us
  Pallas kernels  479 us (91%)
  local copies, waits for them, and re-layouts  25.7 us (5%)
  other arithmetic  10.2 us (2%)
    pallas_call x1, Pallas kernels, feed_both(): pl.pallas_call(feed_kernel, out_shape=(struct((rows, width), F32), struct...  221 us
    pallas_call x1, Pallas kernels, first_half(): pl.pallas_call(first_kernel, out_shape=(struct((rows, features), BF16), s...  117 us
    pallas_call x1, Pallas kernels, last_reduce(): pl.pallas_call(last_kernel, out_shape=(struct((rows, width), F32), struct...  72.1 us
    pallas_call x1, Pallas kernels, recur_back(): pl.pallas_call(recur_back_kernel, out_shape=(struct((lanes, 2 * lanes), F...  69.4 us
    unnamed x21, local copies, waits for them, and re-layouts  11.4 us

profile of v6, /device:TPU:0, one launch (start us, length us, event | category | flops | bytes accessed | tf_op | source)
XLA Modules:
  0.0 516.5 jit_solution(16295304598310426536)
XLA Ops:
  0.7 0.8 reduce-window.9
  1.5 0.7 bitcast_subtract_fusion
  2.2 0.8 concatenate.31
  2.9 0.6 pad.21.small
  3.5 1.3 fusion.6.gains
  4.9 0.1 select_reduce_fusion
  5.0 0.8 reshape.188
  5.8 0.8 reshape.189
  6.7 0.7 fusion.2.gate_blocks
  7.3 1.6 compare_convert_fusion.masks
  8.9 116.8 %first_half.1 = (bf16[768,2048]{1,0:T(8,128)(2,1)}, f32[776,640]{1,0:T(8,128)}, f32[768,640]{1,0:T(8,128)}, bf16[768,640]{1,0:T(8,128)(2,1)}, f32[768,640]{1,0:T...) custom-call(bf16[768,512]{1,0:T(8,128)(2,1)} %tok.5, ...), custom_call_target="tpu_custom_call" | custom-call | tf_op jit(solution)/shard_map/first_half/pallas_call | solution.py:932
  125.7 1.3 slice.87
  127.0 221.1 %feed_both.1 = (f32[768,512]{1,0:T(8,128)}, f32[768,512]{1,0:T(8,128)}, f32[8,512]{1,0:T(8,128)}, f32[256,1536]{1,0:T(8,128)}, bf16[2,256,1536]{2,1,0:T(8,128)(2...) custom-call(bf16[768,640]{1,0:T(8,128)(2,1)} %get-tuple-element.65.m, ...), custom_call_target="tpu_custom_call" | custom-call | tf_op jit(solution)/shard_map/feed_both/pallas_call | solution.py:1447
  348.1 69.4 %recur_back.1 = (f32[640,1280]{1,0:T(8,128)}, f32[8,640]{1,0:T(8,128)}, f32[768,128]{1,0:T(8,128)}, f32[768,512]{1,0:T(8,128)}, f32[256,1536]{1,0:T(8,128)}, /*i...) custom-call(f32[776,8]{1,0:T(8,128)} %compare_convert_fusion.masks, ...), custom_call_target="tpu_custom_call" | custom-call | tf_op jit(solution)/shard_map/recur_back/pallas_call | solution.py:1748
  417.5 0.7 slice_reduce_fusion
  418.2 0.1 reshape_squeeze.3
  418.3 0.7 pad_maximum_fusion.3
  419.1 0.1 reshape.195
  419.2 0.1 reshape.196
  419.3 1.8 fusion.8
  421.1 0.1 stack.35
  421.2 0.1 stack.38
  421.3 0.1 stack.37
  421.5 0.1 stack.36
  421.6 0.1 stack.33
  421.7 0.1 stack.32
  421.9 0.1 stack.31
  422.0 0.1 stack.30
  422.1 0.1 concatenate.37
  422.3 0.1 pad_bitcast_fusion
  422.3 1.1 copy.53
  423.4 72.1 %last_reduce.1 = (f32[768,512]{1,0:T(8,128)}, f32[8,512]{1,0:T(8,128)}, f32[208,128]{1,0:T(8,128)}, f32[256,640]{1,0:T(8,128)}, f32[256,640]{1,0:T(8,128)}, /*in...) custom-call(bf16[2048,640]{1,0:T(8,128)(2,1)} %get-tuple-element.85., ...), custom_call_target="tpu_custom_call" | custom-call | tf_op jit(solution)/shard_map/last_reduce/pallas_call | solution.py:1922
  495.5 1.3 slice.105
  496.7 0.7 slice.89
  497.5 0.6 dynamic-slice_bitcast_fusion
  498.0 0.7 slice.100
  498.7 0.7 slice.91
  499.4 1.4 slice_multiply_fusion
  500.8 0.9 fusion.9
  501.7 0.6 reshape.202
  502.4 0.6 reshape.201
  503.0 0.0 copy-start
  503.0 2.8 pad_maximum_fusion
  505.8 0.0 copy-start.2
  505.8 2.3 copy.48
  508.1 0.0 copy-done
  508.1 1.6 copy.49
  509.7 0.0 copy-done.2
  509.7 0.0 copy-start.3
  509.7 1.1 copy.60
  510.8 0.8 copy-done.3
  511.7 0.0 copy-start.5
  511.7 0.0 copy-start.4
  511.7 1.1 copy.61
  512.8 0.4 copy-done.5
  513.2 0.0 copy-start.1
  513.2 0.8 copy.62
  514.0 0.0 copy-done.4
  514.0 0.8 copy.63
  514.9 0.0 copy-done.1
  514.9 1.1 copy.64
  (6 shorter events, 0.1 us)
Async XLA Ops:
  503.0 5.1 copy-start
  505.8 3.9 copy-start.2
  509.7 2.0 copy-start.3
  511.7 1.5 copy-start.5
  511.7 2.4 copy-start.4
  513.2 1.7 copy-start.1

commit v7 on v6

--- a/solution.py
+++ b/solution.py
@@ -1307,7 +1307,11 @@
             red.drain(c)
             for o in range(LINE):
                 part[c, o] = back[here, o * width : (o + 1) * width].astype(BF16)
-            red_gs.start(c)
+            red_gs.start_ends(c)
+        for k in range(GROUP // CHUNK):
+            c = g * (GROUP // CHUNK) + k
+            here = slice(k * CHUNK, (k + 1) * CHUNK)
+            red_gs.start_rest(c)
             inners[z, c] = as_row(inner[here, :])
             inner_spread.start(c)
         block = dot(mid[at, :], down_v[...])

time: 524 us -> 525 us (level)
  no operation moved by 1% of the time
where the time goes in v7:
time: 525 us; the launch traced here: 517 us
  Pallas kernels  480 us (91%)
  local copies, waits for them, and re-layouts  25.7 us (5%)
  other arithmetic  10.2 us (2%)
    pallas_call x1, Pallas kernels, feed_both(): pl.pallas_call(feed_kernel, out_shape=(struct((rows, width), F32), struct...  222 us
    pallas_call x1, Pallas kernels, first_half(): pl.pallas_call(first_kernel, out_shape=(struct((rows, features), BF16), s...  117 us
    pallas_call x1, Pallas kernels, last_reduce(): pl.pallas_call(last_kernel, out_shape=(struct((rows, width), F32), struct...  72.1 us
    pallas_call x1, Pallas kernels, recur_back(): pl.pallas_call(recur_back_kernel, out_shape=(struct((lanes, 2 * lanes), F...  69.1 us
    unnamed x21, local copies, waits for them, and re-layouts  11.4 us

profile of v7, /device:TPU:0, one launch (start us, length us, event | category | flops | bytes accessed | tf_op | source)
XLA Modules:
  0.0 517.0 jit_solution(8998732892371605113)
XLA Ops:
  0.7 0.8 reduce-window.9
  1.5 0.7 bitcast_subtract_fusion
  2.2 0.8 concatenate.31
  2.9 0.6 pad.21.small
  3.5 1.3 fusion.6.gains
  4.9 0.1 select_reduce_fusion
  5.0 0.8 reshape.188
  5.8 0.8 reshape.189
  6.7 0.7 fusion.2.gate_blocks
  7.3 1.6 compare_convert_fusion.masks
  8.9 116.8 %first_half.1 = (bf16[768,2048]{1,0:T(8,128)(2,1)}, f32[776,640]{1,0:T(8,128)}, f32[768,640]{1,0:T(8,128)}, bf16[768,640]{1,0:T(8,128)(2,1)}, f32[768,640]{1,0:T...) custom-call(bf16[768,512]{1,0:T(8,128)(2,1)} %tok.5, ...), custom_call_target="tpu_custom_call" | custom-call | tf_op jit(solution)/shard_map/first_half/pallas_call | solution.py:932
  125.7 1.3 slice.87
  127.0 221.9 %feed_both.1 = (f32[768,512]{1,0:T(8,128)}, f32[768,512]{1,0:T(8,128)}, f32[8,512]{1,0:T(8,128)}, f32[256,1536]{1,0:T(8,128)}, bf16[2,256,1536]{2,1,0:T(8,128)(2...) custom-call(bf16[768,640]{1,0:T(8,128)(2,1)} %get-tuple-element.65.m, ...), custom_call_target="tpu_custom_call" | custom-call | tf_op jit(solution)/shard_map/feed_both/pallas_call | solution.py:1451
  348.9 69.1 %recur_back.1 = (f32[640,1280]{1,0:T(8,128)}, f32[8,640]{1,0:T(8,128)}, f32[768,128]{1,0:T(8,128)}, f32[768,512]{1,0:T(8,128)}, f32[256,1536]{1,0:T(8,128)}, /*i...) custom-call(f32[776,8]{1,0:T(8,128)} %compare_convert_fusion.masks, ...), custom_call_target="tpu_custom_call" | custom-call | tf_op jit(solution)/shard_map/recur_back/pallas_call | solution.py:1752
  418.0 0.7 slice_reduce_fusion
  418.7 0.1 reshape_squeeze.3
  418.8 0.7 pad_maximum_fusion.3
  419.5 0.1 reshape.195
  419.6 0.1 reshape.196
  419.7 1.8 fusion.8
  421.6 0.1 stack.35
  421.7 0.1 stack.38
  421.8 0.1 stack.37
  421.9 0.1 stack.36
  422.1 0.1 stack.33
  422.2 0.1 stack.32
  422.3 0.1 stack.31
  422.4 0.1 stack.30
  422.6 0.1 concatenate.37
  422.7 0.1 pad_bitcast_fusion
  422.8 1.1 copy.53
  423.8 72.1 %last_reduce.1 = (f32[768,512]{1,0:T(8,128)}, f32[8,512]{1,0:T(8,128)}, f32[208,128]{1,0:T(8,128)}, f32[256,640]{1,0:T(8,128)}, f32[256,640]{1,0:T(8,128)}, /*in...) custom-call(bf16[2048,640]{1,0:T(8,128)(2,1)} %get-tuple-element.85., ...), custom_call_target="tpu_custom_call" | custom-call | tf_op jit(solution)/shard_map/last_reduce/pallas_call | solution.py:1926
  496.0 1.3 slice.105
  497.2 0.7 slice.89
  498.0 0.6 dynamic-slice_bitcast_fusion
  498.5 0.7 slice.100
  499.2 0.7 slice.91
  499.9 1.4 slice_multiply_fusion
  501.3 0.9 fusion.9
  502.2 0.6 reshape.202
  502.9 0.6 reshape.201
  503.5 0.0 copy-start
  503.5 2.8 pad_maximum_fusion
  506.3 0.0 copy-start.2
  506.3 2.3 copy.48
  508.6 0.0 copy-done
  508.6 1.6 copy.49
  510.2 0.0 copy-done.2
  510.2 0.0 copy-start.3
  510.2 1.1 copy.60
  511.3 0.8 copy-done.3
  512.2 0.0 copy-start.5
  512.2 0.0 copy-start.4
  512.2 1.1 copy.61
  513.3 0.4 copy-done.5
  513.7 0.0 copy-start.1
  513.7 0.8 copy.62
  514.5 0.0 copy-done.4
  514.5 0.8 copy.63
  515.4 0.0 copy-done.1
  515.4 1.1 copy.64
  (6 shorter events, 0.1 us)
Async XLA Ops:
  503.5 5.1 copy-start
  506.3 3.9 copy-start.2
  510.2 2.0 copy-start.3
  512.2 1.5 copy-start.5
  512.2 2.4 copy-start.4
  513.7 1.7 copy-start.1
